TPU v7x, 256 devices: a whole 4x4x8 slice. The times are simulated.
256 devices in a mesh: tower: 2 (over core), blk: 16 (over z_lo, x), seq: 8 (over y, z_hi).
Axes of the slice: x: 4, y: 4, z: 8 (z_hi: 2, z_lo: 4; z = z_hi * 4 + z_lo), core: 2. Of those that a mesh axis runs over, the one named last changes fastest.
Arguments:
- queries: bfloat16 [2, 16384, 1024], P('tower', ('blk', 'seq')), may hold values from -6 to 6
- key_rows: bfloat16 [2, 16384, 1024], P('tower', ('blk', 'seq')), may hold values from -6 to 6
- value_rows: bfloat16 [2, 16384, 1024], P('tower', ('blk', 'seq')), may hold values from -6 to 6
- cross_queries: bfloat16 [2, 16384, 1024], P('tower', ('blk', 'seq')), may hold values from -6 to 6
- cross_keys: bfloat16 [2, 16384, 1024], P('tower', ('blk', 'seq')), may hold values from -6 to 6
- cross_values: bfloat16 [2, 16384, 1024], P('tower', ('blk', 'seq')), may hold values from -6 to 6
- grad_out: bfloat16 [2, 16384, 1024], P('tower', ('blk', 'seq')), may hold values from -6 to 6
- offsets: int32 [2, 16], replicated, may hold values from -511 to 511, as said below
- key_valid: int32 [2, 16384], P(None, ('blk', 'seq')), may hold values from 0 to 1, as said below
Outputs:
- attended: bfloat16 [2, 16384, 1024], P('tower', ('blk', 'seq'))
- grad_queries: bfloat16 [2, 16384, 1024], P('tower', ('blk', 'seq'))
- grad_keys: bfloat16 [2, 16384, 1024], P('tower', ('blk', 'seq'))
- grad_values: bfloat16 [2, 16384, 1024], P('tower', ('blk', 'seq'))
- grad_cross_queries: bfloat16 [2, 16384, 1024], P('tower', ('blk', 'seq'))
- grad_cross_keys: bfloat16 [2, 16384, 1024], P('tower', ('blk', 'seq'))
- grad_cross_values: bfloat16 [2, 16384, 1024], P('tower', ('blk', 'seq'))
Inputs may be any that keep to these rules, and one draw needn't show every extreme that they name: Both ends of the range occur in every draw; for every block b, offsets[0, b] and offsets[1, b] have opposite signs, and every magnitude is at least 256. `key_valid`: positions k * 1024 + 1024 // 2 - 1 and k * 1024 + 1024 // 2 are always 1.
All inputs are finite; a program needn't handle non-finite values.
Results may differ from a plain program's by a relative error of at most 0.019.
Values may be sent and summed in bfloat16 or wider, within the bound.
No kernel may reach another device: no remote copies, remote signals or barrier semaphores. Data moves between devices by JAX's collectives and lax.ppermute only.
A program may use at most 128 MiB of HBM per device.

v0:
```python
import jax
import jax.numpy as jnp
from jax import lax
from jax.sharding import PartitionSpec as P

HEADS = 16
HEAD = 64
WINDOW = 2048
TILE = 512


def extended(block, sides, width):
    for axis, dim in sides:
        count = lax.axis_size(axis)
        forward = [(i, i + 1) for i in range(count - 1)]
        backward = [(target, source) for source, target in forward]
        low = lax.ppermute(
            lax.slice_in_dim(block, block.shape[dim] - width, None, axis=dim), axis, forward
        )
        high = lax.ppermute(lax.slice_in_dim(block, 0, width, axis=dim), axis, backward)
        block = jnp.concatenate([low, block, high], axis=dim)
    return block


def swapped(value, axis, bit):
    mask = 2**bit
    pairs = [(source, source ^ mask) for source in range(lax.axis_size(axis))]
    return lax.ppermute(value, axis, pairs)


def passed_along(block, axis, distance):
    devices = range(lax.axis_size(axis))
    route = [(i - distance, i) for i in devices if i - distance in devices]
    return lax.ppermute(block, axis, route)


def attend(query_tile, grad_tile, key_block, value_block, allowed, heads_here):
    score_scale = HEAD ** (-0.5)
    rows_count = query_tile.shape[0]
    keys_count = key_block.shape[0]
    q_heads = query_tile.reshape(rows_count, heads_here, HEAD)
    g_heads = grad_tile.reshape(rows_count, heads_here, HEAD)
    k_heads = key_block.reshape(keys_count, heads_here, HEAD)
    v_heads = value_block.reshape(keys_count, heads_here, HEAD)
    scores = (
        jnp.einsum("qhe,khe->hqk", q_heads, k_heads, preferred_element_type=jnp.float32)
        * score_scale
    )
    scores = jnp.where(allowed[None], scores, -1e30)
    row_max = jnp.max(scores, axis=2)
    unnormed = jnp.exp(scores - row_max[:, :, None])
    row_sum = jnp.sum(unnormed, axis=2)
    weights = unnormed / row_sum[:, :, None]
    prob_bf = weights.astype(jnp.bfloat16)
    result = jnp.einsum(
        "hqk,khe->qhe", prob_bf, v_heads, preferred_element_type=jnp.float32
    ).reshape(rows_count, -1)
    grad_probs = jnp.einsum("qhe,khe->hqk", g_heads, v_heads, preferred_element_type=jnp.float32)
    row_dot = jnp.sum(weights * grad_probs, axis=2)
    grad_scores = (weights * (grad_probs - row_dot[:, :, None]) * score_scale).astype(jnp.bfloat16)
    grad_query = jnp.einsum(
        "hqk,khe->qhe", grad_scores, k_heads, preferred_element_type=jnp.float32
    ).reshape(rows_count, -1)
    grad_key = jnp.einsum(
        "hqk,qhe->khe", grad_scores, q_heads, preferred_element_type=jnp.float32
    ).reshape(keys_count, -1)
    grad_value = jnp.einsum(
        "hqk,qhe->khe", prob_bf, g_heads, preferred_element_type=jnp.float32
    ).reshape(keys_count, -1)
    return (result, grad_query, grad_key, grad_value, jnp.stack((row_max, row_sum, row_dot)))


def shards(
    queries,
    key_rows,
    value_rows,
    cross_queries,
    cross_keys,
    cross_values,
    grad_out,
    offsets,
    key_valid,
):
    seq_count = lax.axis_size("seq")
    heads_here = HEADS // seq_count
    local_rows = (
        queries[0],
        key_rows[0],
        value_rows[0],
        cross_queries[0],
        cross_keys[0],
        cross_values[0],
        grad_out[0],
    )
    query_here, key_here, value_here, cross_query, cross_key, cross_value, cotangent = (
        lax.all_to_all(local_rows[0], "seq", split_axis=1, concat_axis=0, tiled=True),
        lax.all_to_all(local_rows[1], "seq", split_axis=1, concat_axis=0, tiled=True),
        lax.all_to_all(local_rows[2], "seq", split_axis=1, concat_axis=0, tiled=True),
        lax.all_to_all(local_rows[3], "seq", split_axis=1, concat_axis=0, tiled=True),
        lax.all_to_all(local_rows[4], "seq", split_axis=1, concat_axis=0, tiled=True),
        lax.all_to_all(local_rows[5], "seq", split_axis=1, concat_axis=0, tiled=True),
        lax.all_to_all(local_rows[6], "seq", split_axis=1, concat_axis=0, tiled=True),
    )
    block_len = query_here.shape[0]
    columns = query_here.shape[1]
    half_width = min(WINDOW // 2, block_len // 2)
    tile_rows = min(TILE, block_len)
    tile_count = block_len // tile_rows
    window_span = tile_rows + 2 * half_width
    tower_id = lax.axis_index("tower")
    block_id = lax.axis_index("blk")
    block_mask = lax.all_gather(key_valid, "seq", axis=1, tiled=True)
    mask_ext = extended(block_mask, (("blk", 1),), half_width)
    self_valid = lax.dynamic_index_in_dim(mask_ext, tower_id, 0, keepdims=False)
    other_valid = lax.dynamic_index_in_dim(mask_ext, 1 - tower_id, 0, keepdims=False)
    pair_ext = extended(jnp.stack((key_here, value_here)), (("blk", 1),), half_width)
    partner = swapped(jnp.stack((cross_key, cross_value)), "tower", 0)
    partner_ext = extended(partner, (("blk", 1),), half_width)
    align_shift = offsets[tower_id, block_id]
    band_start = half_width + align_shift
    band = lax.dynamic_slice_in_dim(partner_ext, band_start, block_len, 1)
    band_valid = lax.dynamic_slice_in_dim(other_valid, band_start, block_len) > 0
    rows_local = jnp.arange(tile_rows)
    keys_local = jnp.arange(window_span)
    near = jnp.abs(rows_local[:, None] + half_width - keys_local[None, :]) <= half_width

    def self_step(carry, tile_index):
        grad_key_acc, grad_value_acc = carry
        tile_start = tile_index * tile_rows
        query_tile = lax.dynamic_slice_in_dim(query_here, tile_start, tile_rows, 0)
        grad_tile = lax.dynamic_slice_in_dim(cotangent, tile_start, tile_rows, 0)
        key_window = lax.dynamic_slice_in_dim(pair_ext[0], tile_start, window_span, 0)
        value_window = lax.dynamic_slice_in_dim(pair_ext[1], tile_start, window_span, 0)
        allowed = (
            near & (lax.dynamic_slice_in_dim(self_valid, tile_start, window_span) > 0)[None, :]
        )
        result, grad_query, grad_key, grad_value, stats = attend(
            query_tile, grad_tile, key_window, value_window, allowed, heads_here
        )
        grad_key_acc = lax.dynamic_update_slice_in_dim(
            grad_key_acc,
            lax.dynamic_slice_in_dim(grad_key_acc, tile_start, window_span, 0) + grad_key,
            tile_start,
            0,
        )
        grad_value_acc = lax.dynamic_update_slice_in_dim(
            grad_value_acc,
            lax.dynamic_slice_in_dim(grad_value_acc, tile_start, window_span, 0) + grad_value,
            tile_start,
            0,
        )
        return ((grad_key_acc, grad_value_acc), (result, grad_query, stats))

    def cross_step(carry, tile_index):
        grad_key_acc, grad_value_acc = carry
        tile_start = tile_index * tile_rows
        query_tile = lax.dynamic_slice_in_dim(cross_query, tile_start, tile_rows, 0)
        grad_tile = lax.dynamic_slice_in_dim(cotangent, tile_start, tile_rows, 0)
        result, grad_query, grad_key, grad_value, stats = attend(
            query_tile, grad_tile, band[0], band[1], band_valid[None, :], heads_here
        )
        return ((grad_key_acc + grad_key, grad_value_acc + grad_value), (result, grad_query))

    zeros_ext = jnp.zeros((block_len + 2 * half_width, columns), jnp.float32)
    zeros_band = jnp.zeros((block_len, columns), jnp.float32)
    tile_ids = jnp.arange(tile_count)
    (self_gk, self_gv), (self_out, self_gq, self_stats) = lax.scan(
        self_step, (zeros_ext, zeros_ext), tile_ids
    )
    (cross_gk, cross_gv), (cross_out, cross_gq) = lax.scan(
        cross_step, (zeros_band, zeros_band), tile_ids
    )
    self_out = self_out.reshape(block_len, columns)
    cross_out = cross_out.reshape(block_len, columns)
    self_stats = jnp.transpose(self_stats, (1, 2, 0, 3)).reshape(3, heads_here, block_len)
    attended = (self_out + cross_out).astype(jnp.bfloat16)
    cross_ext = jnp.zeros((2, block_len + 2 * half_width, columns), jnp.float32)
    cross_ext = lax.dynamic_update_slice_in_dim(
        cross_ext, jnp.stack((cross_gk, cross_gv)), band_start, 1
    )
    self_ext = jnp.stack((self_gk, self_gv))
    self_core = self_ext[:, half_width : half_width + block_len]
    cross_core = cross_ext[:, half_width : half_width + block_len]
    upper_cut = block_len - half_width
    lower_send = jnp.concatenate((self_ext[:, :half_width], cross_ext[:, :half_width]), 0)
    upper_send = jnp.concatenate(
        (self_ext[:, block_len + half_width :], cross_ext[:, block_len + half_width :]), 0
    )
    from_above = passed_along(lower_send.astype(jnp.bfloat16), "blk", -1).astype(lower_send.dtype)
    from_below = passed_along(upper_send.astype(jnp.bfloat16), "blk", 1).astype(upper_send.dtype)
    self_core = (
        self_core.at[:, upper_cut:].add(from_above[:2]).at[:, :half_width].add(from_below[:2])
    )
    cross_core = (
        cross_core.at[:, upper_cut:].add(from_above[2:]).at[:, :half_width].add(from_below[2:])
    )
    returned = swapped(cross_core.astype(jnp.bfloat16), "tower", 0)
    head_outs = (
        attended,
        self_gq.reshape(block_len, columns).astype(jnp.bfloat16),
        self_core[0].astype(jnp.bfloat16),
        self_core[1].astype(jnp.bfloat16),
        cross_gq.reshape(block_len, columns).astype(jnp.bfloat16),
        returned[0],
        returned[1],
    )
    token_outs = (
        lax.all_to_all(head_outs[0], "seq", split_axis=0, concat_axis=1, tiled=True),
        lax.all_to_all(head_outs[1], "seq", split_axis=0, concat_axis=1, tiled=True),
        lax.all_to_all(head_outs[2], "seq", split_axis=0, concat_axis=1, tiled=True),
        lax.all_to_all(head_outs[3], "seq", split_axis=0, concat_axis=1, tiled=True),
        lax.all_to_all(head_outs[4], "seq", split_axis=0, concat_axis=1, tiled=True),
        lax.all_to_all(head_outs[5], "seq", split_axis=0, concat_axis=1, tiled=True),
        lax.all_to_all(head_outs[6], "seq", split_axis=0, concat_axis=1, tiled=True),
    )
    return tuple((piece[None] for piece in token_outs))


def solution(mesh):
    in_specs = (
        P("tower", ("blk", "seq"), None),
        P("tower", ("blk", "seq"), None),
        P("tower", ("blk", "seq"), None),
        P("tower", ("blk", "seq"), None),
        P("tower", ("blk", "seq"), None),
        P("tower", ("blk", "seq"), None),
        P("tower", ("blk", "seq"), None),
        P(),
        P(None, ("blk", "seq")),
    )
    out_specs = (
        P("tower", ("blk", "seq"), None),
        P("tower", ("blk", "seq"), None),
        P("tower", ("blk", "seq"), None),
        P("tower", ("blk", "seq"), None),
        P("tower", ("blk", "seq"), None),
        P("tower", ("blk", "seq"), None),
        P("tower", ("blk", "seq"), None),
    )
    return jax.shard_map(shards, mesh=mesh, in_specs=in_specs, out_specs=out_specs, check_vma=False)
```

profile of v0, /device:TPU:32, one launch (start us, length us, event | category | flops | bytes accessed | tf_op | source)
XLA Modules:
  0.0 503.9 jit_solution(13005847992831772088)
XLA Ops:
  2.5 10.2 %all-to-all-start = ((bf16[128,8,128]{0,2,1:T(8,128)(2,1)}), bf16[128,8,128]{0,2,1:T(8,128)(2,1)S(1)}, u32[]{:S(2)}, u32[]{:S(2)}) async-start(bf16[128,8,128]{0,2,1:T(8,128)(2,1)} %bitcast), calls=%async_computation | async-start | bytes 524288 | tf_op jit(solution)/shard_map/all_to_all | solution.py:96
  14.5 12.2 %all-to-all-done = bf16[128,8,128]{0,2,1:T(8,128)(2,1)S(1)} async-done(((bf16[128,8,128]{0,2,1:T(8,128)(2,1)}), bf16[128,8,128]{0,2,1:T(8,128)(2,1)S(1)}, u32[]{:S(2)}, u32[]{:S(2)}) %all-to-all-start) | async-done | bytes 262176 | tf_op jit(solution)/shard_map/all_to_all | solution.py:96
  26.7 3.4 all-to-all-start.1
  31.9 9.9 %all-to-all-done.1 = bf16[128,8,128]{0,2,1:T(8,128)(2,1)S(1)} async-done(((bf16[128,8,128]{0,2,1:T(8,128)(2,1)}), bf16[128,8,128]{0,2,1:T(8,128)(2,1)S(1)}, u32[]{:S(2)}, u32[]{:S(2)}) %all-to-all-start.1) | async-done | bytes 262176 | tf_op jit(solution)/shard_map/all_to_all | solution.py:97
  41.9 3.4 all-to-all-start.2
  47.1 9.8 %all-to-all-done.2 = bf16[128,8,128]{0,2,1:T(8,128)(2,1)S(1)} async-done(((bf16[128,8,128]{0,2,1:T(8,128)(2,1)}), bf16[128,8,128]{0,2,1:T(8,128)(2,1)S(1)}, u32[]{:S(2)}, u32[]{:S(2)}) %all-to-all-start.2) | async-done | bytes 262176 | tf_op jit(solution)/shard_map/all_to_all | solution.py:98
  56.9 3.4 all-to-all-start.5
  61.2 11.1 %all-to-all-done.5 = bf16[128,8,128]{0,2,1:T(8,128)(2,1)S(1)} async-done(((bf16[128,8,128]{0,2,1:T(8,128)(2,1)}), bf16[128,8,128]{0,2,1:T(8,128)(2,1)S(1)}, u32[]{:S(2)}, u32[]{:S(2)}) %all-to-all-start.5) | async-done | bytes 262176 | tf_op jit(solution)/shard_map/all_to_all | solution.py:100
  72.3 3.4 all-to-all-start.6
  75.7 30.9 %all_gather.3 = s32[2,1024]{1,0:T(2,128)S(1)} all-gather(s32[2,128]{1,0:T(2,128)S(1)} %copy-done.16), channel_id=1, replica_groups=mesh['tower'=2,'blk'=16,'seq'=8] {'seq'}, dimensions={1}, use_global_device_ids=true | all-gather | bytes 9216 | tf_op jit(solution)/shard_map/all_gather | solution.py:112
  106.6 2.6 collective-permute-start.1
  109.2 3.2 collective-permute-start
  113.3 3.4 all-to-all-start.3
  120.7 3.4 collective-permute-start.2
  124.1 4.6 collective-permute-start.3
  129.0 9.5 %all-to-all-start.4 = ((bf16[128,8,128]{0,2,1:T(8,128)(2,1)}), bf16[128,8,128]{0,2,1:T(8,128)(2,1)S(1)}, u32[]{:S(2)}, u32[]{:S(2)}) async-start(bf16[128,8,128]{0,2,1:T(8,128)(2,1)} %bitcast.13), calls=%async_computation.4 | async-start | bytes 524288 | tf_op jit(solution)/shard_map/all_to_all | solution.py:99
  141.3 8.4 %all-to-all-done.4 = bf16[128,8,128]{0,2,1:T(8,128)(2,1)S(1)} async-done(((bf16[128,8,128]{0,2,1:T(8,128)(2,1)}), bf16[128,8,128]{0,2,1:T(8,128)(2,1)S(1)}, u32[]{:S(2)}, u32[]{:S(2)}) %all-to-all-start.4) | async-done | bytes 262176 | tf_op jit(solution)/shard_map/all_to_all | solution.py:99
  153.1 2.6 collective-permute-start.6
  155.7 3.2 collective-permute-start.5
  160.0 119.6 %while.38 = (s32[]{:T(128)}, f32[2048,128]{0,1:T(8,128)S(1)}, f32[2048,128]{0,1:T(8,128)S(1)}, f32[2,512,128]{2,1,0:T(8,128)}, bf16[2,512,128]{2,1,0:T(8,128)(2,...) while((s32[]{:T(128)}, f32[2048,128]{0,1:T(8,128)S(1)}, ...), condition=%wide.region_4.5_spmd.clone, body=%wide.region_0.4_spmd.clone.sunk | while | flops 1658205184 | bytes 61505044 | solution.py:167
  166.7 3.7 fusion.168
  170.4 6.3 %fusion.166 = (f32[2,512]{1,0:T(2,128)S(1)}, f32[2,512,1536]{2,1,0:T(8,128)}) fusion(pred[512,1536]{1,0:T(8,128)(4,1)} %fusion.164, bf16[512,2,64]{0,2,1:T(8,128)(2,1)} %bitcast.214, bf16[1536,2,64]{0,2,1:T(8,128)(2,1)} %bitcast.206), kind=kOutput, calls=%fused_computation.110.clone.1 | convolution fusion | flops 207619584 | bytes 7606272 | tf_op jit(solution)/shard_map/while/body/eval_jaxpr/sub | solution.py:51
  176.7 4.7 fusion.170
  181.4 5.0 fusion.167
  186.4 14.2 %fusion.171 = bf16[2,64,512]{2,1,0:T(8,128)(2,1)} fusion(bf16[1536,2,64]{0,2,1:T(8,128)(2,1)S(1)} %bitcast.209, f32[2,512,1536]{2,1,0:T(8,128)} %fusion.168, f32[2,512,1536]{2,1,0:T(8,128)} %get-tuple-element.487, f32[2,512]{1,0:T(2,128)S(1)} %get-tuple-element.485), kind=kOutput, calls=%fused_computation.13.clone.1 | convolution fusion | flops 212339200 | bytes 13111296 | tf_op jit(solution)/shard_map/while/body/eval_jaxpr/hqk,khe->qhe/dot_general | solution.py:61
  200.6 14.9 %fusion.169 = f32[2,64,1536]{2,1,0:T(8,128)} fusion(bf16[512,2,64]{0,2,1:T(8,128)(2,1)} %bitcast.217, f32[2,512,1536]{2,1,0:T(8,128)} %fusion.168, f32[2,512,1536]{2,1,0:T(8,128)} %get-tuple-element.487, f32[2,512]{1,0:T(2,128)S(1)} %get-tuple-element.485), kind=kOutput, calls=%fused_computation.14.clone.1 | convolution fusion | flops 212339200 | bytes 13504512 | tf_op jit(solution)/shard_map/while/body/eval_jaxpr/hqk,qhe->khe/dot_general | solution.py:64
  226.3 3.7 fusion.168
  230.0 6.3 %fusion.166 = (f32[2,512]{1,0:T(2,128)S(1)}, f32[2,512,1536]{2,1,0:T(8,128)}) fusion(pred[512,1536]{1,0:T(8,128)(4,1)} %fusion.164, bf16[512,2,64]{0,2,1:T(8,128)(2,1)} %bitcast.214, bf16[1536,2,64]{0,2,1:T(8,128)(2,1)} %bitcast.206), kind=kOutput, calls=%fused_computation.110.clone.1 | convolution fusion | flops 207619584 | bytes 7606272 | tf_op jit(solution)/shard_map/while/body/eval_jaxpr/sub | solution.py:51
  236.3 4.7 fusion.170
  241.0 5.0 fusion.167
  246.0 14.2 %fusion.171 = bf16[2,64,512]{2,1,0:T(8,128)(2,1)} fusion(bf16[1536,2,64]{0,2,1:T(8,128)(2,1)S(1)} %bitcast.209, f32[2,512,1536]{2,1,0:T(8,128)} %fusion.168, f32[2,512,1536]{2,1,0:T(8,128)} %get-tuple-element.487, f32[2,512]{1,0:T(2,128)S(1)} %get-tuple-element.485), kind=kOutput, calls=%fused_computation.13.clone.1 | convolution fusion | flops 212339200 | bytes 13111296 | tf_op jit(solution)/shard_map/while/body/eval_jaxpr/hqk,khe->qhe/dot_general | solution.py:61
  260.2 14.9 %fusion.169 = f32[2,64,1536]{2,1,0:T(8,128)} fusion(bf16[512,2,64]{0,2,1:T(8,128)(2,1)} %bitcast.217, f32[2,512,1536]{2,1,0:T(8,128)} %fusion.168, f32[2,512,1536]{2,1,0:T(8,128)} %get-tuple-element.487, f32[2,512]{1,0:T(2,128)S(1)} %get-tuple-element.485), kind=kOutput, calls=%fused_computation.14.clone.1 | convolution fusion | flops 212339200 | bytes 13504512 | tf_op jit(solution)/shard_map/while/body/eval_jaxpr/hqk,qhe->khe/dot_general | solution.py:64
  279.7 4.2 all-to-all-start.8
  285.0 2.3 fusion.62
  289.4 94.5 %while.39 = (s32[]{:T(128)}, f32[1024,128]{0,1:T(8,128)}, f32[1024,128]{0,1:T(8,128)S(1)}, f32[2,512,128]{2,1,0:T(8,128)}, bf16[2,512,128]{2,1,0:T(8,128)(2,1)},...) while((s32[]{:T(128)}, f32[1024,128]{0,1:T(8,128)}, ...), condition=%wide.region_9.10_spmd.clone, body=%wide.region_5.9_spmd.clone.sunk | while | flops 828904448 | bytes 66213200 | solution.py:170
  294.0 2.8 fusion.187
  296.8 4.4 fusion.185
  301.2 11.9 %fusion.190 = bf16[2,512,64]{1,2,0:T(8,128)(2,1)} fusion(bf16[1024,2,64]{0,2,1:T(8,128)(2,1)} %bitcast.213, f32[2,512,1024]{2,1,0:T(8,128)} %fusion.187, f32[2,512,1024]{2,1,0:T(8,128)} %get-tuple-element.501, f32[2,512]{1,0:T(2,128)S(1)} %get-tuple-element.502), kind=kOutput, calls=%fused_computation.47.clone.1 | convolution fusion | flops 141559808 | bytes 8785920 | tf_op jit(solution)/shard_map/while/body/eval_jaxpr/hqk,khe->qhe/dot_general | solution.py:61
  313.2 12.4 %fusion.188 = f32[2,64,1024]{2,1,0:T(8,128)} fusion(bf16[512,2,64]{0,2,1:T(8,128)(2,1)} %bitcast.219, f32[2,512,1024]{2,1,0:T(8,128)} %fusion.187, f32[2,512,1024]{2,1,0:T(8,128)} %get-tuple-element.501, f32[2,512]{1,0:T(2,128)S(1)} %get-tuple-element.502), kind=kOutput, calls=%fused_computation.48.clone.1 | convolution fusion | flops 141559808 | bytes 9048064 | tf_op jit(solution)/shard_map/while/body/eval_jaxpr/hqk,qhe->khe/dot_general | solution.py:64
  327.2 3.9 fusion.189
  341.3 2.8 fusion.187
  344.1 4.4 fusion.185
  348.5 11.9 %fusion.190 = bf16[2,512,64]{1,2,0:T(8,128)(2,1)} fusion(bf16[1024,2,64]{0,2,1:T(8,128)(2,1)} %bitcast.213, f32[2,512,1024]{2,1,0:T(8,128)} %fusion.187, f32[2,512,1024]{2,1,0:T(8,128)} %get-tuple-element.501, f32[2,512]{1,0:T(2,128)S(1)} %get-tuple-element.502), kind=kOutput, calls=%fused_computation.47.clone.1 | convolution fusion | flops 141559808 | bytes 8785920 | tf_op jit(solution)/shard_map/while/body/eval_jaxpr/hqk,khe->qhe/dot_general | solution.py:61
  360.4 12.4 %fusion.188 = f32[2,64,1024]{2,1,0:T(8,128)} fusion(bf16[512,2,64]{0,2,1:T(8,128)(2,1)} %bitcast.219, f32[2,512,1024]{2,1,0:T(8,128)} %fusion.187, f32[2,512,1024]{2,1,0:T(8,128)} %get-tuple-element.501, f32[2,512]{1,0:T(2,128)S(1)} %get-tuple-element.502), kind=kOutput, calls=%fused_computation.48.clone.1 | convolution fusion | flops 141559808 | bytes 9048064 | tf_op jit(solution)/shard_map/while/body/eval_jaxpr/hqk,qhe->khe/dot_general | solution.py:64
  374.5 3.9 fusion.189
  384.0 2.1 pad_maximum_fusion.2
  387.7 6.2 %dynamic_update_slice.22 = f32[2,2048,128]{1,2,0:T(8,128)} dynamic-update-slice(f32[2,2048,128]{1,2,0:T(8,128)} %broadcast_in_dim.82, f32[2,1024,128]{1,2,0:T(8,128)} %pad_maximum_fusion.2, s32[]{:T(128)} %constant.183.clone.1, s32[]{:T(128)S(6)} %select_n.49, s32[]{:T(128)} %constant.183.clone.1) | dynamic-update-slice | bytes 2097156 | tf_op jit(solution)/shard_map/dynamic_update_slice | solution.py:178
  396.6 4.8 collective-permute-start.7
  405.4 9.5 %all-to-all-start.11 = ((bf16[8,128,128]{2,1,0:T(8,128)(2,1)}), bf16[8,128,128]{2,1,0:T(8,128)(2,1)S(1)}, u32[]{:S(2)}, u32[]{:S(2)}) async-start(bf16[8,128,128]{2,1,0:T(8,128)(2,1)} %bitcast.41), calls=%async_computation.11 | async-start | bytes 524288 | tf_op jit(solution)/shard_map/all_to_all | solution.py:212
  414.9 2.0 add_convert_fusion
  418.2 2.2 convert_element_type.59
  420.4 2.1 fusion.67
  422.4 3.7 all-to-all-done.11
  426.2 5.8 %all-to-all-start.7 = ((bf16[8,128,128]{2,1,0:T(8,128)(2,1)}), bf16[8,128,128]{2,1,0:T(8,128)(2,1)S(1)}, u32[]{:S(2)}, u32[]{:S(2)}) async-start(bf16[8,128,128]{2,1,0:T(8,128)(2,1)} %bitcast.25), calls=%async_computation.7 | async-start | bytes 524288 | tf_op jit(solution)/shard_map/all_to_all | solution.py:208
  432.0 2.4 fusion.66
  435.3 7.8 %all-to-all-done.7 = bf16[8,128,128]{2,1,0:T(8,128)(2,1)S(1)} async-done(((bf16[8,128,128]{2,1,0:T(8,128)(2,1)}), bf16[8,128,128]{2,1,0:T(8,128)(2,1)S(1)}, u32[]{:S(2)}, u32[]{:S(2)}) %all-to-all-start.7) | async-done | bytes 262176 | tf_op jit(solution)/shard_map/all_to_all | solution.py:208
  443.1 3.4 all-to-all-start.10
  448.8 8.9 %all-to-all-done.10 = bf16[8,128,128]{2,1,0:T(8,128)(2,1)S(1)} async-done(((bf16[8,128,128]{2,1,0:T(8,128)(2,1)}), bf16[8,128,128]{2,1,0:T(8,128)(2,1)S(1)}, u32[]{:S(2)}, u32[]{:S(2)}) %all-to-all-start.10) | async-done | bytes 262176 | tf_op jit(solution)/shard_map/all_to_all | solution.py:211
  457.7 3.4 all-to-all-start.9
  462.0 10.2 %all-to-all-done.9 = bf16[8,128,128]{2,1,0:T(8,128)(2,1)S(1)} async-done(((bf16[8,128,128]{2,1,0:T(8,128)(2,1)}), bf16[8,128,128]{2,1,0:T(8,128)(2,1)S(1)}, u32[]{:S(2)}, u32[]{:S(2)}) %all-to-all-start.9) | async-done | bytes 262176 | tf_op jit(solution)/shard_map/all_to_all | solution.py:210
  472.2 3.4 all-to-all-start.13
  476.5 10.3 %all-to-all-done.13 = bf16[8,128,128]{2,1,0:T(8,128)(2,1)S(1)} async-done(((bf16[8,128,128]{2,1,0:T(8,128)(2,1)}), bf16[8,128,128]{2,1,0:T(8,128)(2,1)S(1)}, u32[]{:S(2)}, u32[]{:S(2)}) %all-to-all-start.13) | async-done | bytes 262176 | tf_op jit(solution)/shard_map/all_to_all | solution.py:214
  486.8 3.4 all-to-all-start.12
  497.4 5.5 %all-to-all-done.12 = bf16[8,128,128]{2,1,0:T(8,128)(2,1)S(1)} async-done(((bf16[8,128,128]{2,1,0:T(8,128)(2,1)}), bf16[8,128,128]{2,1,0:T(8,128)(2,1)S(1)}, u32[]{:S(2)}, u32[]{:S(2)}) %all-to-all-start.12) | async-done | bytes 262176 | tf_op jit(solution)/shard_map/all_to_all | solution.py:213
  (202 shorter events, 87.3 us)
Async XLA Ops:
  0.6 59.7 %copy-start.13 = (bf16[1,128,1024]{2,1,0:T(8,128)(2,1)S(1)}, bf16[1,128,1024]{2,1,0:T(8,128)(2,1)}, u32[]{:S(2)}) copy-start(bf16[1,128,1024]{2,1,0:T(8,128)(2,1)} %param.26) | copy-start | bytes 786436
  0.6 75.1 %copy-start.16 = (s32[2,128]{1,0:T(2,128)S(1)}, s32[2,128]{1,0:T(2,128)}, u32[]{:S(2)}) copy-start(s32[2,128]{1,0:T(2,128)} %param.29) | copy-start | bytes 3076
  0.7 111.8 %copy-start.14 = (bf16[1,128,1024]{2,1,0:T(8,128)(2,1)S(1)}, bf16[1,128,1024]{2,1,0:T(8,128)(2,1)}, u32[]{:S(2)}) copy-start(bf16[1,128,1024]{2,1,0:T(8,128)(2,1)} %param.27) | copy-start | bytes 786436
  0.7 116.8 %copy-start.18 = (s32[2,16]{1,0:T(2,128)S(1)}, s32[2,16]{1,0:T(2,128)}, u32[]{:S(2)}) copy-start(s32[2,16]{1,0:T(2,128)} %param.28) | copy-start | bytes 388
  0.7 118.7 %copy-start.15 = (bf16[1,128,1024]{2,1,0:T(8,128)(2,1)S(1)}, bf16[1,128,1024]{2,1,0:T(8,128)(2,1)}, u32[]{:S(2)}) copy-start(bf16[1,128,1024]{2,1,0:T(8,128)(2,1)} %param.24) | copy-start | bytes 786436
  2.5 24.2 %all-to-all-start = ((bf16[128,8,128]{0,2,1:T(8,128)(2,1)}), bf16[128,8,128]{0,2,1:T(8,128)(2,1)S(1)}, u32[]{:S(2)}, u32[]{:S(2)}) async-start(bf16[128,8,128]{0,2,1:T(8,128)(2,1)} %bitcast), calls=%async_computation | async-start | bytes 524288 | tf_op jit(solution)/shard_map/all_to_all | solution.py:96
  26.7 15.1 %all-to-all-start.1 = ((bf16[128,8,128]{0,2,1:T(8,128)(2,1)}), bf16[128,8,128]{0,2,1:T(8,128)(2,1)S(1)}, u32[]{:S(2)}, u32[]{:S(2)}) async-start(bf16[128,8,128]{0,2,1:T(8,128)(2,1)} %bitcast.4), calls=%async_computation.1 | async-start | bytes 524288 | tf_op jit(solution)/shard_map/all_to_all | solution.py:97
  41.9 15.1 %all-to-all-start.2 = ((bf16[128,8,128]{0,2,1:T(8,128)(2,1)}), bf16[128,8,128]{0,2,1:T(8,128)(2,1)S(1)}, u32[]{:S(2)}, u32[]{:S(2)}) async-start(bf16[128,8,128]{0,2,1:T(8,128)(2,1)} %bitcast.7), calls=%async_computation.2 | async-start | bytes 524288 | tf_op jit(solution)/shard_map/all_to_all | solution.py:98
  56.9 15.4 %all-to-all-start.5 = ((bf16[128,8,128]{0,2,1:T(8,128)(2,1)}), bf16[128,8,128]{0,2,1:T(8,128)(2,1)S(1)}, u32[]{:S(2)}, u32[]{:S(2)}) async-start(bf16[128,8,128]{0,2,1:T(8,128)(2,1)} %bitcast.18), calls=%async_computation.5 | async-start | bytes 524288 | tf_op jit(solution)/shard_map/all_to_all | solution.py:100
  72.3 41.0 %all-to-all-start.6 = ((bf16[128,8,128]{0,2,1:T(8,128)(2,1)}), bf16[128,8,128]{0,2,1:T(8,128)(2,1)S(1)}, u32[]{:S(2)}, u32[]{:S(2)}) async-start(bf16[128,8,128]{0,2,1:T(8,128)(2,1)} %bitcast.21), calls=%async_computation.6 | async-start | bytes 524288 | tf_op jit(solution)/shard_map/all_to_all | solution.py:101
  106.6 32.8 %collective-permute-start.1 = (s32[2,512]{1,0:T(2,128)S(1)}, s32[2,512]{1,0:T(2,128)S(1)}, u32[]{:S(2)}, u32[]{:S(2)}) collective-permute-start(s32[2,512]{1,0:T(2,128)S(1)} %get-tuple-element.350), channel_id=1, source_target_pairs={{8,0},{16,8},{24,16},{32,24},{40,32},{48,40},{56,48},{64,56},{72,6... | collective-permute-start | bytes 12296 | tf_op jit(solution)/shard_map/ppermute | solution.py:20
  109.2 11.0 %collective-permute-start = (s32[2,512]{1,0:T(2,128)S(1)}, s32[2,512]{1,0:T(2,128)S(1)}, u32[]{:S(2)}, u32[]{:S(2)}) collective-permute-start(s32[2,512]{1,0:T(2,128)S(1)} %get-tuple-element.351), channel_id=1, source_target_pairs={{0,8},{8,16},{16,24},{24,32},{32,40},{40,48},{48,56},{56,64},{64,7... | collective-permute-start | bytes 12296 | tf_op jit(solution)/shard_map/ppermute | solution.py:17
  113.3 37.3 %copy-start.11 = (bf16[2,512,128]{2,1,0:T(8,128)(2,1)}, bf16[2,512,128]{2,1,0:T(8,128)(2,1)S(1)}, u32[]{:S(2)}) copy-start(bf16[2,512,128]{2,1,0:T(8,128)(2,1)S(1)} %fusion.79) | copy-start | bytes 786436
  113.3 15.7 %all-to-all-start.3 = ((bf16[128,8,128]{0,2,1:T(8,128)(2,1)}), bf16[128,8,128]{0,2,1:T(8,128)(2,1)S(1)}, u32[]{:S(2)}, u32[]{:S(2)}) async-start(bf16[128,8,128]{0,2,1:T(8,128)(2,1)} %bitcast.10), calls=%async_computation.3 | async-start | bytes 524288 | tf_op jit(solution)/shard_map/all_to_all | solution.py:102
  120.7 29.9 %collective-permute-start.2 = (bf16[2,512,128]{2,1,0:T(8,128)(2,1)S(1)}, bf16[2,512,128]{2,1,0:T(8,128)(2,1)S(1)}, u32[]{:S(2)}, u32[]{:S(2)}) collective-permute-start(bf16[2,512,128]{2,1,0:T(8,128)(2,1)S(1)} %get-tuple-element.348), channel_id=1, source_target_pairs={{0,8},{8,16},{16,24},{24,32},{32,40},{40,48},{48,56},{56,64},{64,7... | collective-permute-start | bytes 786440 | tf_op jit(solution)/shard_map/ppermute | solution.py:17
  124.1 26.5 %collective-permute-start.3 = (bf16[2,512,128]{2,1,0:T(8,128)(2,1)S(1)}, bf16[2,512,128]{2,1,0:T(8,128)(2,1)}, u32[]{:S(2)}, u32[]{:S(2)}) collective-permute-start(bf16[2,512,128]{2,1,0:T(8,128)(2,1)S(1)} %get-tuple-element.349), channel_id=1, source_target_pairs={{8,0},{16,8},{24,16},{32,24},{40,32},{48,40},{56,48},{64,56},{72,6... | collective-permute-start | bytes 786440 | tf_op jit(solution)/shard_map/ppermute | solution.py:20
  129.0 20.7 %all-to-all-start.4 = ((bf16[128,8,128]{0,2,1:T(8,128)(2,1)}), bf16[128,8,128]{0,2,1:T(8,128)(2,1)S(1)}, u32[]{:S(2)}, u32[]{:S(2)}) async-start(bf16[128,8,128]{0,2,1:T(8,128)(2,1)} %bitcast.13), calls=%async_computation.4 | async-start | bytes 524288 | tf_op jit(solution)/shard_map/all_to_all | solution.py:99
  139.4 12.8 %collective-permute-start.4 = (bf16[2,1024,128]{2,1,0:T(8,128)(2,1)}, bf16[2,1024,128]{2,1,0:T(8,128)(2,1)S(1)}, u32[]{:S(2)}, u32[]{:S(2)}) collective-permute-start(bf16[2,1024,128]{2,1,0:T(8,128)(2,1)} %pad_maximum_fusion.3), channel_id=1, source_target_pairs={{0,128},{128,0},{1,129},{129,1},{2,130},{130,2},{3,131},{131,3},{4... | collective-permute-start | bytes 1572872 | tf_op jit(solution)/shard_map/ppermute | solution.py:28
  152.2 7.6 %copy-start.12 = (bf16[2,1024,128]{2,1,0:T(8,128)(2,1)}, bf16[2,1024,128]{2,1,0:T(8,128)(2,1)S(1)}, u32[]{:S(2)}) copy-start(bf16[2,1024,128]{2,1,0:T(8,128)(2,1)S(1)} %collective-permute-done.4) | copy-start | bytes 1572868
  153.1 131.9 %collective-permute-start.6 = (bf16[2,512,128]{2,1,0:T(8,128)(2,1)}, bf16[2,512,128]{2,1,0:T(8,128)(2,1)}, u32[]{:S(2)}, u32[]{:S(2)}) collective-permute-start(bf16[2,512,128]{2,1,0:T(8,128)(2,1)} %get-tuple-element.344), channel_id=1, source_target_pairs={{8,0},{16,8},{24,16},{32,24},{40,32},{48,40},{56,48},{64,56},{72,6... | collective-permute-start | bytes 786440 | tf_op jit(solution)/shard_map/ppermute | solution.py:20
  155.7 129.3 %collective-permute-start.5 = (bf16[2,512,128]{2,1,0:T(8,128)(2,1)}, bf16[2,512,128]{2,1,0:T(8,128)(2,1)}, u32[]{:S(2)}, u32[]{:S(2)}) collective-permute-start(bf16[2,512,128]{2,1,0:T(8,128)(2,1)} %get-tuple-element.345), channel_id=1, source_target_pairs={{0,8},{8,16},{16,24},{24,32},{32,40},{40,48},{48,56},{56,64},{64,7... | collective-permute-start | bytes 786440 | tf_op jit(solution)/shard_map/ppermute | solution.py:17
  160.2 1.3 copy-start.19
  160.2 6.4 %copy-start.8 = (bf16[1024,128]{1,0:T(8,128)(2,1)}, bf16[1024,128]{1,0:T(8,128)(2,1)S(1)}, u32[]{:S(2)}) copy-start(bf16[1024,128]{1,0:T(8,128)(2,1)S(1)} %get-tuple-element.544) | copy-start | bytes 786436 | tf_op jit(solution)/shard_map/while
  163.9 2.8 copy-start.5
  181.4 5.0 copy-start.6
  200.5 15.0 %copy-start.7 = (bf16[2,64,512]{2,1,0:T(8,128)(2,1)S(1)}, bf16[2,64,512]{2,1,0:T(8,128)(2,1)}, u32[]{:S(2)}) copy-start(bf16[2,64,512]{2,1,0:T(8,128)(2,1)} %fusion.171) | copy-start | bytes 393220 | tf_op jit(solution)/shard_map/while
  215.5 4.3 copy-start.20
  218.1 1.7 copy-start.9
  219.8 1.3 copy-start.19
  219.8 6.4 %copy-start.8 = (bf16[1024,128]{1,0:T(8,128)(2,1)}, bf16[1024,128]{1,0:T(8,128)(2,1)S(1)}, u32[]{:S(2)}) copy-start(bf16[1024,128]{1,0:T(8,128)(2,1)S(1)} %get-tuple-element.544) | copy-start | bytes 786436 | tf_op jit(solution)/shard_map/while
  223.5 2.8 copy-start.5
  241.0 5.0 copy-start.6
  260.2 15.0 %copy-start.7 = (bf16[2,64,512]{2,1,0:T(8,128)(2,1)S(1)}, bf16[2,64,512]{2,1,0:T(8,128)(2,1)}, u32[]{:S(2)}) copy-start(bf16[2,64,512]{2,1,0:T(8,128)(2,1)} %fusion.171) | copy-start | bytes 393220 | tf_op jit(solution)/shard_map/while
  275.1 4.3 copy-start.20
  277.7 1.7 copy-start.9
  279.7 9.8 %copy-start = (f32[1024,128]{0,1:T(8,128)S(1)}, f32[1024,128]{0,1:T(8,128)}, u32[]{:S(2)}) copy-start(f32[1024,128]{0,1:T(8,128)} %custom-call.1) | copy-start | bytes 1572868
  279.7 9.8 %copy-start.17 = (pred[1024]{0:T(1024)(128)(4,1)S(1)}, pred[1024]{0:T(1024)(128)(4,1)}, u32[]{:S(2)}) copy-start(pred[1024]{0:T(1024)(128)(4,1)} %compare_reduce_fusion) | copy-start | bytes 3076
  279.7 125.8 %all-to-all-start.8 = ((bf16[8,128,128]{2,1,0:T(8,128)(2,1)}), bf16[8,128,128]{2,1,0:T(8,128)(2,1)}, u32[]{:S(2)}, u32[]{:S(2)}) async-start(bf16[8,128,128]{2,1,0:T(8,128)(2,1)} %bitcast.224), calls=%async_computation.8 | async-start | bytes 524288 | tf_op jit(solution)/shard_map/all_to_all | solution.py:209
  327.2 3.9 copy-start.21
  331.1 1.0 copy-start.1
  331.1 1.2 copy-start.4
  332.5 0.8 copy-start.2
  374.5 3.9 copy-start.21
  378.3 1.0 copy-start.1
  378.3 1.2 copy-start.4
  379.8 0.8 copy-start.2
  386.1 9.6 %copy-start.10 = (bf16[2,2048,128]{1,2,0:T(8,128)(2,1)S(1)}, bf16[2,2048,128]{1,2,0:T(8,128)(2,1)}, u32[]{:S(2)}) copy-start(bf16[2,2048,128]{1,2,0:T(8,128)(2,1)} %fusion.59) | copy-start | bytes 3145732
  395.7 8.7 %copy-start.3 = (f32[2,2048,128]{1,2,0:T(8,128)S(1)}, f32[2,2048,128]{1,2,0:T(8,128)}, u32[]{:S(2)}) copy-start(f32[2,2048,128]{1,2,0:T(8,128)} %dynamic_update_slice.22) | copy-start | bytes 6291460
  396.6 20.3 %collective-permute-start.7 = (bf16[4,512,128]{1,2,0:T(8,128)(2,1)}, bf16[4,512,128]{1,2,0:T(8,128)(2,1)}, u32[]{:S(2)}, u32[]{:S(2)}) collective-permute-start(bf16[4,512,128]{1,2,0:T(8,128)(2,1)} %pad_maximum_fusion.4), channel_id=1, source_target_pairs={{8,0},{16,8},{24,16},{32,24},{40,32},{48,40},{56,48},{64,56},{72,6... | collective-permute-start | bytes 1572872 | tf_op jit(solution)/shard_map/ppermute | solution.py:34
  402.4 15.8 %collective-permute-start.8 = (bf16[4,512,128]{1,2,0:T(8,128)(2,1)}, bf16[4,512,128]{1,2,0:T(8,128)(2,1)}, u32[]{:S(2)}, u32[]{:S(2)}) collective-permute-start(bf16[4,512,128]{1,2,0:T(8,128)(2,1)} %pad_maximum_fusion.5), channel_id=1, source_target_pairs={{0,8},{8,16},{16,24},{24,32},{32,40},{40,48},{48,56},{56,64},{64,7... | collective-permute-start | bytes 1572872 | tf_op jit(solution)/shard_map/ppermute | solution.py:34
  405.4 20.7 %all-to-all-start.11 = ((bf16[8,128,128]{2,1,0:T(8,128)(2,1)}), bf16[8,128,128]{2,1,0:T(8,128)(2,1)S(1)}, u32[]{:S(2)}, u32[]{:S(2)}) async-start(bf16[8,128,128]{2,1,0:T(8,128)(2,1)} %bitcast.41), calls=%async_computation.11 | async-start | bytes 524288 | tf_op jit(solution)/shard_map/all_to_all | solution.py:212
  426.2 17.0 %all-to-all-start.7 = ((bf16[8,128,128]{2,1,0:T(8,128)(2,1)}), bf16[8,128,128]{2,1,0:T(8,128)(2,1)S(1)}, u32[]{:S(2)}, u32[]{:S(2)}) async-start(bf16[8,128,128]{2,1,0:T(8,128)(2,1)} %bitcast.25), calls=%async_computation.7 | async-start | bytes 524288 | tf_op jit(solution)/shard_map/all_to_all | solution.py:208
  443.1 14.5 %all-to-all-start.10 = ((bf16[8,128,128]{2,1,0:T(8,128)(2,1)}), bf16[8,128,128]{2,1,0:T(8,128)(2,1)S(1)}, u32[]{:S(2)}, u32[]{:S(2)}) async-start(bf16[8,128,128]{2,1,0:T(8,128)(2,1)} %bitcast.38), calls=%async_computation.10 | async-start | bytes 524288 | tf_op jit(solution)/shard_map/all_to_all | solution.py:211
  447.9 13.2 %collective-permute-start.9 = (bf16[2,1024,128]{1,2,0:T(8,128)(2,1)S(1)}, bf16[2,1024,128]{1,2,0:T(8,128)(2,1)S(1)}, u32[]{:S(2)}, u32[]{:S(2)}) collective-permute-start(bf16[2,1024,128]{1,2,0:T(8,128)(2,1)S(1)} %convert_element_type.64), channel_id=1, source_target_pairs={{0,128},{128,0},{1,129},{129,1},{2,130},{130,2},{3,131},{131,3},{4... | collective-permute-start | bytes 1572872 | tf_op jit(solution)/shard_map/ppermute | solution.py:28
  457.7 14.5 %all-to-all-start.9 = ((bf16[8,128,128]{2,1,0:T(8,128)(2,1)}), bf16[8,128,128]{2,1,0:T(8,128)(2,1)S(1)}, u32[]{:S(2)}, u32[]{:S(2)}) async-start(bf16[8,128,128]{2,1,0:T(8,128)(2,1)} %bitcast.35), calls=%async_computation.9 | async-start | bytes 524288 | tf_op jit(solution)/shard_map/all_to_all | solution.py:210
  472.2 14.5 %all-to-all-start.13 = ((bf16[8,128,128]{2,1,0:T(8,128)(2,1)}), bf16[8,128,128]{2,1,0:T(8,128)(2,1)S(1)}, u32[]{:S(2)}, u32[]{:S(2)}) async-start(bf16[8,128,128]{2,1,0:T(8,128)(2,1)} %bitcast.47), calls=%async_computation.13 | async-start | bytes 524288 | tf_op jit(solution)/shard_map/all_to_all | solution.py:214
  486.8 16.1 %all-to-all-start.12 = ((bf16[8,128,128]{2,1,0:T(8,128)(2,1)}), bf16[8,128,128]{2,1,0:T(8,128)(2,1)S(1)}, u32[]{:S(2)}, u32[]{:S(2)}) async-start(bf16[8,128,128]{2,1,0:T(8,128)(2,1)} %bitcast.44), calls=%async_computation.12 | async-start | bytes 524288 | tf_op jit(solution)/shard_map/all_to_all | solution.py:213
where the time goes:
time: 513 us; the launch traced here: 504 us
  matrix products  169 us (33%)
  waiting for transfers between devices  98 us (19%)
  starting transfers between devices  96.4 us (19%)
  local copies, waits for them, and re-layouts  72.6 us (14%)
  blocking collectives  30.9 us (6%)
  other arithmetic  30.7 us (6%)
    dot_general x4, matrix products, attend(): jnp.einsum('hqk,qhe->khe', grad_scores, q_heads, preferred_element_type=j...  54.6 us
    dot_general x4, matrix products, attend(): jnp.einsum('hqk,khe->qhe', grad_scores, k_heads, preferred_element_type=j...  52.3 us
    all_gather x1, blocking collectives, shards(): block_mask = lax.all_gather(key_valid, 'seq', axis=1, tiled=True)  30.9 us
    sub x4, matrix products, attend(): unnormed = jnp.exp(scores - row_max[:, :, None])  21.4 us
    unnamed x42, local copies, waits for them, and re-layouts  19.1 us
    dot_general x4, matrix products, attend(): jnp.einsum('hqk,khe->qhe', prob_bf, v_heads, preferred_element_type=jnp.f...  17.1 us
    dynamic_update_slice x16, local copies, waits for them, and re-layouts, shards(): lax.scan(self_step, (zeros_ext, zeros_ext), tile_ids)  15.2 us
    dot_general x4, matrix products, attend(): jnp.einsum('qhe,khe->hqk', g_heads, v_heads, preferred_element_type=jnp.f...  12.9 us
  transfers between devices with their start and end apart: 24, of which 12 were waited for; matrix products, arithmetic and copies ran while one was open for 53% of the time, Pallas kernels for 0%

commit v1 on v0

v1 whole, which is shorter than its diff:
```python
import jax
import jax.numpy as jnp
from jax import lax
from jax.experimental import pallas as pl
from jax.experimental.pallas import tpu as pltpu
from jax.sharding import PartitionSpec as P

HEADS = 16
HEAD = 64
BLOCK = 1024
HALF = 512
CHUNK = 128
QROWS = 256
EXT = BLOCK + 2 * HALF
SELF_WIN = QROWS + 2 * HALF
CROSS_WIN = BLOCK + CHUNK
NEG = -16384.0
SCALE = HEAD**-0.5
VROWS = 16
F32 = jnp.float32
BF16 = jnp.bfloat16
NT = (((1,), (1,)), ((), ()))
NN = (((1,), (0,)), ((), ()))


def dot(a, b, dims=NN):
    return lax.dot_general(a, b, dims, preferred_element_type=F32)


def eye(n):
    rows = lax.broadcasted_iota(jnp.int32, (n, n), 0)
    return jnp.where(rows == lax.broadcasted_iota(jnp.int32, (n, n), 1), 1.0, 0.0).astype(BF16)


def flipped(x):
    return dot(eye(x.shape[1]), x, NT).astype(BF16)


def stage_keys(chunks, values, bias, kx, kt, v, vt):
    padded = jnp.concatenate([bias, jnp.zeros((CHUNK - 16, CHUNK), F32)], axis=0).astype(BF16)
    turned = dot(eye(CHUNK), padded, NT)
    lane = lax.broadcasted_iota(jnp.int32, (CHUNK, CHUNK), 1)
    for c in range(EXT // CHUNK):
        at = pl.ds(c * CHUNK, CHUNK)
        k = chunks(c)
        val = values(c)
        kx[at, 0:CHUNK] = k
        kx[at, CHUNK : 2 * CHUNK] = jnp.where(lane == c, turned, 0.0).astype(BF16)
        kt[:, at] = flipped(k)
        v[at, :] = val
        vt[:, at] = flipped(val)


def tile_step(q, gt, start, width, step, windowed, scratch):
    kx, kt, v, vt, s, e, ds, dk, dv = scratch
    count = width // step
    head_lane = lax.broadcasted_iota(jnp.int32, (QROWS, 2 * HEAD), 1) // HEAD
    scaled = q.astype(F32) * SCALE
    ones = jnp.ones((QROWS, CHUNK), BF16)
    win = pl.ds(start, width)
    outs, gqs, q_heads, g_heads = [], [], [], []
    for h in range(2):
        rows_h = slice(h * HEAD, (h + 1) * HEAD)
        cols_h = slice(h * QROWS, (h + 1) * QROWS)
        qh = jnp.where(head_lane == h, scaled, 0.0).astype(BF16)
        qx = jnp.concatenate([qh, ones], axis=1)
        top = None
        for b in range(count):
            at = pl.ds(start + b * step, step)
            scores = dot(kx[at, :], qx, NT)
            if windowed and b in (0, count - 1):
                r = lax.broadcasted_iota(jnp.int32, (step, QROWS), 0)
                c = lax.broadcasted_iota(jnp.int32, (step, QROWS), 1)
                scores = jnp.where(r >= c if b == 0 else r <= c, scores, -1e30)
            s[h, b * step : (b + 1) * step, :] = scores
            high = jnp.max(scores, axis=0, keepdims=True)
            top = high if top is None else jnp.maximum(top, high)
        total = jnp.zeros((1, QROWS), F32)
        for b in range(count):
            rows = slice(b * step, (b + 1) * step)
            p = jnp.exp(s[h, rows, :] - top)
            total = total + jnp.sum(p, axis=0, keepdims=True)
            s[h, rows, :] = p
            e[rows, cols_h] = p.astype(BF16)
        inverse = 1.0 / total
        out = dot(vt[rows_h, win], e[:, cols_h]) * inverse
        g = (gt[rows_h, :].astype(F32) * inverse).astype(BF16)
        row_dot = jnp.sum(out * g.astype(F32), axis=0, keepdims=True)
        zeros = jnp.zeros((HEAD, QROWS), BF16)
        gx = jnp.concatenate([g, zeros] if h == 0 else [zeros, g], axis=0)
        for b in range(count):
            rows = slice(b * step, (b + 1) * step)
            at = pl.ds(start + b * step, step)
            dp = dot(v[at, :], gx)
            ds[rows, cols_h] = (s[h, rows, :] * (dp - row_dot)).astype(BF16)
        gqs.append(dot(kt[rows_h, win], ds[:, cols_h]) * SCALE)
        outs.append(out)
        q_heads.append(qh)
        g_heads.append(gx)
    dv[win, :] += dot(e[...], jnp.concatenate(g_heads, axis=1), NT)
    dk[win, :] += dot(ds[...], jnp.concatenate(q_heads, axis=0))
    return jnp.concatenate(outs, axis=0), jnp.concatenate(gqs, axis=0)


def validity(r1, lo, hi, row):
    parts = [ref[c, 0:VROWS, :].astype(F32)[row : row + 1] for ref, n in ((lo, 4), (r1, 8), (hi, 4)) for c in range(n)]
    return jnp.concatenate(parts, axis=0)


def piece(lo, mid, hi, first):
    def get(c):
        if c < 4:
            return lo[c, first : first + CHUNK, :]
        if c < 12:
            return mid[c - 4, first : first + CHUNK, :]
        return hi[c - 12, first : first + CHUNK, :]

    return get


def emit_sums(dk, dv, pay, at, to_lo, to_hi):
    for n, acc in enumerate((dk, dv)):
        rows = slice(n * CHUNK, (n + 1) * CHUNK)
        spot = slice(at + n * CHUNK, at + (n + 1) * CHUNK)
        to_lo[:, rows, :] = acc[0:HALF, :].astype(BF16).reshape(4, CHUNK, CHUNK)
        pay[:, spot, :] = acc[HALF : HALF + BLOCK, :].astype(BF16).reshape(8, CHUNK, CHUNK)
        to_hi[:, rows, :] = acc[HALF + BLOCK : EXT, :].astype(BF16).reshape(4, CHUNK, CHUNK)


def self_kernel(r1, lo, hi, out_t, pay, to_lo, to_hi, kx, kt, v, vt, gt, s, e, ds, dk, dv):
    bias = jnp.where(validity(r1, lo, hi, 0) > 0.5, 0.0, NEG)
    stage_keys(piece(lo, r1, hi, VROWS), piece(lo, r1, hi, VROWS + CHUNK), bias, kx, kt, v, vt)
    q0, g0 = VROWS + 2 * CHUNK, VROWS + 3 * CHUNK
    for c in range(8):
        gt[:, c * CHUNK : (c + 1) * CHUNK] = flipped(r1[c, g0 : g0 + CHUNK, :])
    dk[...] = jnp.zeros_like(dk)
    dv[...] = jnp.zeros_like(dv)

    def step(i, carry):
        start = pl.multiple_of(i * QROWS, QROWS)
        here = pl.ds(start, QROWS)
        q = r1[pl.ds(2 * i, 2), q0 : q0 + CHUNK, :].reshape(QROWS, CHUNK)
        out, gq = tile_step(q, gt[:, here], start, SELF_WIN, QROWS, True, (kx, kt, v, vt, s, e, ds, dk, dv))
        out_t[:, here] = out
        pay[pl.ds(2 * i, 2), 0:CHUNK, :] = flipped(gq.astype(BF16)).reshape(2, CHUNK, CHUNK)
        return carry

    lax.fori_loop(0, BLOCK // QROWS, step, 0)
    emit_sums(dk, dv, pay, CHUNK, to_lo, to_hi)


def cross_kernel(band, r1, lo, hi, r2, mid, clo, chi, out_t, pay, back, to_lo, to_hi, kx, kt, v, vt, gt, s, e, ds, dk, dv):
    first = band[0]
    place = lax.broadcasted_iota(jnp.int32, (16, CHUNK), 0) * CHUNK + lax.broadcasted_iota(jnp.int32, (16, CHUNK), 1)
    inside = (place >= first) & (place < first + BLOCK)
    bias = jnp.where(inside & (validity(r1, lo, hi, 1) > 0.5), 0.0, NEG)
    stage_keys(piece(clo, mid, chi, 0), piece(clo, mid, chi, CHUNK), bias, kx, kt, v, vt)
    q0, g0 = 2 * CHUNK, VROWS + 3 * CHUNK
    for c in range(8):
        gt[:, c * CHUNK : (c + 1) * CHUNK] = flipped(r1[c, g0 : g0 + CHUNK, :])
    dk[...] = jnp.zeros_like(dk)
    dv[...] = jnp.zeros_like(dv)
    start = pl.multiple_of(lax.shift_right_logical(first, 7) * CHUNK, CHUNK)

    def step(i, carry):
        here = pl.ds(pl.multiple_of(i * QROWS, QROWS), QROWS)
        q = r2[pl.ds(2 * i, 2), q0 : q0 + CHUNK, :].reshape(QROWS, CHUNK)
        out, gq = tile_step(q, gt[:, here], start, CROSS_WIN, 384, False, (kx, kt, v, vt, s, e, ds, dk, dv))
        both = (out + out_t[:, here]).astype(BF16)
        pay[pl.ds(2 * i, 2), 0:CHUNK, :] = flipped(both).reshape(2, CHUNK, CHUNK)
        pay[pl.ds(2 * i, 2), CHUNK : 2 * CHUNK, :] = flipped(gq.astype(BF16)).reshape(2, CHUNK, CHUNK)
        return carry

    lax.fori_loop(0, BLOCK // QROWS, step, 0)
    emit_sums(dk, dv, back, 0, to_lo, to_hi)


def scratch(width):
    return [
        pltpu.VMEM((EXT, 2 * CHUNK), BF16),
        pltpu.VMEM((CHUNK, EXT), BF16),
        pltpu.VMEM((EXT, CHUNK), BF16),
        pltpu.VMEM((CHUNK, EXT), BF16),
        pltpu.VMEM((CHUNK, BLOCK), BF16),
        pltpu.VMEM((2, width, QROWS), F32),
        pltpu.VMEM((width, 2 * QROWS), BF16),
        pltpu.VMEM((width, 2 * QROWS), BF16),
        pltpu.VMEM((EXT, CHUNK), F32),
        pltpu.VMEM((EXT, CHUNK), F32),
    ]


def shaped(shape, dtype=BF16):
    return jax.ShapeDtypeStruct(shape, dtype)


def run_self(r1, lo, hi):
    vmem = pl.BlockSpec(memory_space=pltpu.VMEM)
    return pl.pallas_call(
        self_kernel,
        out_shape=(
            shaped((CHUNK, BLOCK), F32),
            shaped((8, 3 * CHUNK, CHUNK)),
            shaped((4, 2 * CHUNK, CHUNK)),
            shaped((4, 2 * CHUNK, CHUNK)),
        ),
        in_specs=[vmem] * 3,
        out_specs=[vmem] * 4,
        scratch_shapes=scratch(SELF_WIN),
        compiler_params=pltpu.CompilerParams(vmem_limit_bytes=36 * 2**20),
        cost_estimate=pl.CostEstimate(flops=8 * 10**9, bytes_accessed=3 * 2**20, transcendentals=2621440),
        name="self_attention",
    )(r1, lo, hi)


def run_cross(band, r1, lo, hi, r2, mid, clo, chi, out_t):
    vmem = pl.BlockSpec(memory_space=pltpu.VMEM)
    return pl.pallas_call(
        cross_kernel,
        out_shape=(
            shaped((8, 2 * CHUNK, CHUNK)),
            shaped((8, 2 * CHUNK, CHUNK)),
            shaped((4, 2 * CHUNK, CHUNK)),
            shaped((4, 2 * CHUNK, CHUNK)),
        ),
        in_specs=[pl.BlockSpec(memory_space=pltpu.SMEM)] + [vmem] * 8,
        out_specs=[vmem] * 4,
        scratch_shapes=scratch(CROSS_WIN),
        compiler_params=pltpu.CompilerParams(vmem_limit_bytes=36 * 2**20),
        cost_estimate=pl.CostEstimate(flops=8 * 10**9, bytes_accessed=3 * 2**20, transcendentals=2359296),
        name="cross_attention",
    )(band, r1, lo, hi, r2, mid, clo, chi, out_t)


def pieces(rows):
    return rows.reshape(CHUNK, 8, CHUNK).transpose(1, 0, 2)


def exchange(packed):
    return lax.all_to_all(packed, "seq", split_axis=0, concat_axis=0, tiled=True)


def whole(received, n):
    part = received[:, n * CHUNK : (n + 1) * CHUNK, :]
    return part.transpose(1, 0, 2).reshape(1, CHUNK, HEADS * HEAD)


def shards(queries, key_rows, value_rows, cross_queries, cross_keys, cross_values, grad_out, offsets, key_valid):
    tower_id = lax.axis_index("tower")
    block_id = lax.axis_index("blk")
    blocks = lax.axis_size("blk")
    up = [(b, b + 1) for b in range(blocks - 1)]
    down = [(b + 1, b) for b in range(blocks - 1)]
    over_up = [(t * blocks + b, (1 - t) * blocks + b + 1) for t in range(2) for b in range(blocks - 1)]
    over_down = [(t * blocks + b + 1, (1 - t) * blocks + b) for t in range(2) for b in range(blocks - 1)]
    swap = [(0, 1), (1, 0)]
    both = ("tower", "blk")

    own = lax.dynamic_index_in_dim(key_valid, tower_id, 0, keepdims=True)
    other = lax.dynamic_index_in_dim(key_valid, 1 - tower_id, 0, keepdims=True)
    marks = jnp.concatenate([own, other, jnp.zeros((VROWS - 2, CHUNK), jnp.int32)], 0).astype(BF16)
    marks = jnp.broadcast_to(marks[None], (8, VROWS, CHUNK))
    pack1 = jnp.concatenate(
        [marks, pieces(key_rows[0]), pieces(value_rows[0]), pieces(queries[0]), pieces(grad_out[0])], axis=1
    )
    r1 = exchange(pack1)
    pack2 = jnp.concatenate([pieces(cross_keys[0]), pieces(cross_values[0]), pieces(cross_queries[0])], axis=1)
    r2 = exchange(pack2)
    near = VROWS + 2 * CHUNK
    lo = lax.ppermute(r1[4:8, :near], "blk", up)
    hi = lax.ppermute(r1[0:4, :near], "blk", down)
    mid = lax.ppermute(r2[:, : 2 * CHUNK], "tower", swap)
    clo = lax.ppermute(r2[4:8, : 2 * CHUNK], both, over_up)
    chi = lax.ppermute(r2[0:4, : 2 * CHUNK], both, over_down)

    out_t, pay_s, s_lo, s_hi = run_self(r1, lo, hi)
    band = (HALF + offsets[tower_id, block_id]).reshape(1)
    pay_c, back, c_lo, c_hi = run_cross(band, r1, lo, hi, r2, mid, clo, chi, out_t)

    def merged(center, below, above):
        center = center.astype(F32)
        return jnp.concatenate([center[0:4] + below.astype(F32), center[4:8] + above.astype(F32)], 0).astype(BF16)

    above = lax.ppermute(s_lo, "blk", down)
    below = lax.ppermute(s_hi, "blk", up)
    sent_s = jnp.concatenate([pay_s[:, :CHUNK], merged(pay_s[:, CHUNK:], below, above)], axis=1)
    got_s = exchange(sent_s)
    c_above = lax.ppermute(c_lo, both, over_down)
    c_below = lax.ppermute(c_hi, both, over_up)
    c_mid = lax.ppermute(back, "tower", swap)
    sent_c = jnp.concatenate([pay_c, merged(c_mid, c_below, c_above)], axis=1)
    got_c = exchange(sent_c)
    return (
        whole(got_c, 0),
        whole(got_s, 0),
        whole(got_s, 1),
        whole(got_s, 2),
        whole(got_c, 1),
        whole(got_c, 2),
        whole(got_c, 3),
    )


def solution(mesh):
    rows = P("tower", ("blk", "seq"), None)
    in_specs = (rows,) * 7 + (P(), P(None, ("blk", "seq")))
    return jax.shard_map(shards, mesh=mesh, in_specs=in_specs, out_specs=(rows,) * 7, check_vma=False)
```

time: 513 us -> 190 us (0.37); the launches traced: 504 us -> 189 us
  matrix products: 169 us -> 0 us
  local copies, waits for them, and re-layouts: 72.6 us -> 20.2 us
  starting transfers between devices: 96.4 us -> 59.9 us
  blocking collectives: 30.9 us -> 0 us
  Pallas kernels: 0 us -> 26.6 us
  other arithmetic: 30.7 us -> 4.15 us
  waiting for transfers between devices: 98 us -> 76.7 us
    dot_general x20 -> x0, matrix products: 148 us -> none  [the longest x4 54.6 us: attend(): jnp.einsum('hqk,qhe->khe', grad_scores, q_heads, preferred_element_type=j...]
    all_to_all x14 -> x4, starting transfers between devices: 69.9 us -> 27.5 us  [exchange(): lax.all_to_all(packed, 'seq', split_axis=0, concat_axis=0, tiled=True)]
    all_to_all x14 -> x4, waiting for transfers between devices: 97.9 us -> 65 us  [exchange(): lax.all_to_all(packed, 'seq', split_axis=0, concat_axis=0, tiled=True)]
    all_gather x1 -> x0, blocking collectives: 30.9 us -> none  [shards(): block_mask = lax.all_gather(key_valid, 'seq', axis=1, tiled=True)]
    pallas_call x0 -> x2, Pallas kernels: none -> 26.6 us  [the longest x1 13.6 us: run_self(): pl.pallas_call(self_kernel, out_shape=(shaped((CHUNK, BLOCK), F32), shape...]
    dynamic_update_slice x17 -> x0, local copies, waits for them, and re-layouts: 21.4 us -> none  [the longest x16 15.2 us: shards(): lax.scan(self_step, (zeros_ext, zeros_ext), tile_ids)]
    sub x4 -> x0, matrix products: 21.4 us -> none  [attend(): unnormed = jnp.exp(scores - row_max[:, :, None])]
    dynamic_slice x22 -> x1, local copies, waits for them, and re-layouts: 14.5 us -> 0.59 us  [shards(): band = (HALF + offsets[tower_id, block_id]).reshape(1)]
  transfers between devices with their start and end apart: 24 -> 14, of which waited for: 12 -> 7; matrix products, arithmetic and copies ran while one was open for 53% -> 6% of each run, Pallas kernels for 0% -> 14%
where the time goes in v1:
time: 190 us; the launch traced here: 189 us
  waiting for transfers between devices  76.7 us (40%)
  starting transfers between devices  59.9 us (32%)
  Pallas kernels  26.6 us (14%)
  local copies, waits for them, and re-layouts  20.2 us (11%)
  other arithmetic  4.15 us (2%)
    all_to_all x4, waiting for transfers between devices, exchange(): lax.all_to_all(packed, 'seq', split_axis=0, concat_axis=0, tiled=True)  65 us
    all_to_all x4, starting transfers between devices, exchange(): lax.all_to_all(packed, 'seq', split_axis=0, concat_axis=0, tiled=True)  27.5 us
    pallas_call x1, Pallas kernels, run_self(): pl.pallas_call(self_kernel, out_shape=(shaped((CHUNK, BLOCK), F32), shape...  13.6 us
    pallas_call x1, Pallas kernels, run_cross(): pl.pallas_call(cross_kernel, out_shape=(shaped((8, 2 * CHUNK, CHUNK)), sh...  13 us
    unnamed x36, local copies, waits for them, and re-layouts  12.5 us
    ppermute x1, starting transfers between devices, shards(): c_above = lax.ppermute(c_lo, both, over_down)  6.59 us
    ppermute x1, starting transfers between devices, shards(): above = lax.ppermute(s_lo, 'blk', down)  6.03 us
    ppermute x1, waiting for transfers between devices, shards(): c_below = lax.ppermute(c_hi, both, over_up)  5.2 us
  transfers between devices with their start and end apart: 14, of which 7 were waited for; matrix products, arithmetic and copies ran while one was open for 6% of the time, Pallas kernels for 14%

profile of v1, /device:TPU:32, one launch (start us, length us, event | category | flops | bytes accessed | tf_op | source)
XLA Modules:
  0.0 189.3 jit_solution(17072241568054757090)
XLA Ops:
  0.7 0.8 dynamic-slice_convert_fusion.1
  1.6 0.6 broadcast_dynamic-update-slice_fusion
  2.2 1.1 copy.16
  3.3 0.2 copy.17
  3.5 0.2 copy.18
  3.7 0.2 copy.19
  3.9 0.2 copy.20
  4.1 0.2 copy.21
  4.3 0.2 copy-done.4
  4.7 0.2 copy.23
  4.8 0.8 bitcast_dynamic-update-slice_fusion.3
  5.6 0.8 bitcast_dynamic-update-slice_fusion.2
  6.4 0.8 bitcast_dynamic-update-slice_fusion.1
  7.1 0.8 bitcast_dynamic-update-slice_fusion
  7.9 10.3 %all-to-all-start = ((bf16[8,528,128]{2,1,0:T(8,128)(2,1)}), bf16[8,528,128]{2,1,0:T(8,128)(2,1)S(1)}, u32[]{:S(2)}, u32[]{:S(2)}) async-start(bf16[8,528,128]{2,1,0:T(8,128)(2,1)} %bitcast_dynamic-update-slice_fusion), calls=%async_computation | async-start | bytes 2162688 | tf_op jit(solution)/shard_map/all_to_all | solution.py:240
  18.2 0.2 copy.24
  18.4 0.2 copy.25
  18.8 0.2 copy.27
  19.0 0.2 copy-done.7
  19.3 0.2 copy.29
  19.5 1.0 pad_maximum_fusion
  20.5 29.4 %all-to-all-done.r1 = bf16[8,528,128]{2,1,0:T(8,128)(2,1)S(1)} async-done(((bf16[8,528,128]{2,1,0:T(8,128)(2,1)}), bf16[8,528,128]{2,1,0:T(8,128)(2,1)S(1)}, u32[]{:S(2)}, u32[]{:S(2)}) %all-to-all-start) | async-done | bytes 1081376 | tf_op jit(solution)/shard_map/all_to_all | solution.py:240
  49.8 3.5 %all-to-all-start.1 = ((bf16[8,384,128]{2,1,0:T(8,128)(2,1)}), bf16[8,384,128]{2,1,0:T(8,128)(2,1)S(1)}, u32[]{:S(2)}, u32[]{:S(2)}) async-start(bf16[8,384,128]{2,1,0:T(8,128)(2,1)} %pad_maximum_fusion), calls=%async_computation.1 | async-start | bytes 1572864 | tf_op jit(solution)/shard_map/all_to_all | solution.py:240
  53.4 0.9 fusion.4
  54.2 3.4 %collective-permute-start = (bf16[4,272,128]{2,1,0:T(8,128)(2,1)}, bf16[4,272,128]{2,1,0:T(8,128)(2,1)S(1)}, u32[]{:S(2)}, u32[]{:S(2)}) collective-permute-start(bf16[4,272,128]{2,1,0:T(8,128)(2,1)} %get-tuple-element.31), channel_id=1, source_target_pairs={{0,8},{8,16},{16,24},{24,32},{32,40},{40,48},{48,56},{56,64},{64,7... | collective-permute-start | bytes 835592 | tf_op jit(solution)/shard_map/ppermute | solution.py:270
  57.6 4.6 %collective-permute-start.1 = (bf16[4,272,128]{2,1,0:T(8,128)(2,1)}, bf16[4,272,128]{2,1,0:T(8,128)(2,1)S(1)}, u32[]{:S(2)}, u32[]{:S(2)}) collective-permute-start(bf16[4,272,128]{2,1,0:T(8,128)(2,1)} %get-tuple-element.30), channel_id=1, source_target_pairs={{8,0},{16,8},{24,16},{32,24},{40,32},{48,40},{56,48},{64,56},{72,6... | collective-permute-start | bytes 835592 | tf_op jit(solution)/shard_map/ppermute | solution.py:271
  62.2 0.6 dynamic_slice.10
  63.5 9.5 %all-to-all-done.1.r2 = bf16[8,384,128]{2,1,0:T(8,128)(2,1)S(1)} async-done(((bf16[8,384,128]{2,1,0:T(8,128)(2,1)}), bf16[8,384,128]{2,1,0:T(8,128)(2,1)S(1)}, u32[]{:S(2)}, u32[]{:S(2)}) %all-to-all-start.1) | async-done | bytes 786464 | tf_op jit(solution)/shard_map/all_to_all | solution.py:240
  73.0 0.8 fusion.5
  73.8 2.9 %collective-permute-start.3 = (bf16[4,256,128]{2,1,0:T(8,128)(2,1)}, bf16[4,256,128]{2,1,0:T(8,128)(2,1)S(1)}, u32[]{:S(2)}, u32[]{:S(2)}) collective-permute-start(bf16[4,256,128]{2,1,0:T(8,128)(2,1)} %get-tuple-element.44), channel_id=1, source_target_pairs={{0,136},{8,144},{16,152},{24,160},{32,168},{40,176},{48,184},{56,1... | collective-permute-start | bytes 786440 | tf_op jit(solution)/shard_map/ppermute | solution.py:273
  76.7 4.8 %collective-permute-start.4 = (bf16[4,256,128]{2,1,0:T(8,128)(2,1)}, bf16[4,256,128]{2,1,0:T(8,128)(2,1)S(1)}, u32[]{:S(2)}, u32[]{:S(2)}) collective-permute-start(bf16[4,256,128]{2,1,0:T(8,128)(2,1)} %get-tuple-element.43), channel_id=1, source_target_pairs={{8,128},{16,136},{24,144},{32,152},{40,160},{48,168},{56,176},{64,... | collective-permute-start | bytes 786440 | tf_op jit(solution)/shard_map/ppermute | solution.py:274
  81.5 0.8 slice.74
  82.3 13.6 %self_attention.1 = (f32[128,1024]{1,0:T(8,128)S(1)}, bf16[8,384,128]{2,1,0:T(8,128)(2,1)S(1)}, bf16[4,256,128]{2,1,0:T(8,128)(2,1)S(1)}, bf16[4,256,128]{2,1,0:T(8,128)(2,1)S(1)}) custom-call(bf16[8,528,128]{2,1,0:T(8,128)(2,1)S(1)} %all-to-all-done.r1, bf16[4,272,128]{2,1,0:T(8,128)(2,1)S(1)} %collective-permute-done.lo, ...), custom_call_target="tpu_custom_call" | custom-call | flops 8000000000 | bytes 3145728 | tf_op jit(solution)/shard_map/self_attention/pallas_call | solution.py:199
  95.9 1.9 %collective-permute-start.8 = (bf16[4,256,128]{2,1,0:T(8,128)(2,1)S(1)}, bf16[4,256,128]{2,1,0:T(8,128)(2,1)S(1)}, u32[]{:S(2)}, u32[]{:S(2)}) collective-permute-start(bf16[4,256,128]{2,1,0:T(8,128)(2,1)S(1)} %get-tuple-element.21), channel_id=1, source_target_pairs={{0,8},{8,16},{16,24},{24,32},{32,40},{40,48},{48,56},{56,64},{64,7... | collective-permute-start | bytes 786440 | tf_op jit(solution)/shard_map/ppermute | solution.py:285
  97.8 6.0 %collective-permute-start.9 = (bf16[4,256,128]{2,1,0:T(8,128)(2,1)S(1)}, bf16[4,256,128]{2,1,0:T(8,128)(2,1)S(1)}, u32[]{:S(2)}, u32[]{:S(2)}) collective-permute-start(bf16[4,256,128]{2,1,0:T(8,128)(2,1)S(1)} %get-tuple-element.22), channel_id=1, source_target_pairs={{8,0},{16,8},{24,16},{32,24},{40,32},{48,40},{56,48},{64,56},{72,6... | collective-permute-start | bytes 786440 | tf_op jit(solution)/shard_map/ppermute | solution.py:284
  104.0 4.7 %collective-permute-done.8 = bf16[4,256,128]{2,1,0:T(8,128)(2,1)S(1)} collective-permute-done((bf16[4,256,128]{2,1,0:T(8,128)(2,1)S(1)}, bf16[4,256,128]{2,1,0:T(8,128)(2,1)S(1)}, u32[]{:S(2)}, u32[]{:S(2)}) %collective-permute-start.8) | collective-permute-done | bytes 262176 | tf_op jit(solution)/shard_map/ppermute | solution.py:285
  108.6 1.2 collective-permute-done.9
  109.9 0.9 maximum_maximum_fusion.1
  110.9 4.2 %all-to-all-start.3 = ((bf16[8,384,128]{2,1,0:T(8,128)(2,1)}), bf16[8,384,128]{2,1,0:T(8,128)(2,1)}, u32[]{:S(2)}, u32[]{:S(2)}) async-start(bf16[8,384,128]{2,1,0:T(8,128)(2,1)} %maximum_maximum_fusion.1), calls=%async_computation.3 | async-start | bytes 1572864 | tf_op jit(solution)/shard_map/all_to_all | solution.py:240
  115.1 1.0 copy-done.1
  116.2 13.0 %cross_attention.1 = (bf16[8,256,128]{2,1,0:T(8,128)(2,1)S(1)}, bf16[8,256,128]{2,1,0:T(8,128)(2,1)S(1)}, bf16[4,256,128]{2,1,0:T(8,128)(2,1)S(1)}, bf16[4,256,128]{2,1,0:T(8,128)(2,1)S(1)}) custom-call(s32[1]{0:T(128)} %bitcast.band, bf16[8,528,128]{2,1,0:T(8,128)(2,1)S(1)} %all-to-all-done.r1, bf16[4,272,128]{2,1,0:T(8,128)(2,1)S(1)} %collective-permute-done.lo, ...), custom_call_target="tpu_custom_call" | custom-call | flops 8000000000 | bytes 3145728 | tf_op jit(solution)/shard_map/cross_attention/pallas_call | solution.py:218
  129.2 0.3 collective-permute-start.5
  129.5 1.9 %collective-permute-start.6 = (bf16[4,256,128]{2,1,0:T(8,128)(2,1)S(1)}, bf16[4,256,128]{2,1,0:T(8,128)(2,1)S(1)}, u32[]{:S(2)}, u32[]{:S(2)}) collective-permute-start(bf16[4,256,128]{2,1,0:T(8,128)(2,1)S(1)} %get-tuple-element.18), channel_id=1, source_target_pairs={{0,136},{8,144},{16,152},{24,160},{32,168},{40,176},{48,184},{56,1... | collective-permute-start | bytes 786440 | tf_op jit(solution)/shard_map/ppermute | solution.py:289
  131.4 6.6 %collective-permute-start.7 = (bf16[4,256,128]{2,1,0:T(8,128)(2,1)S(1)}, bf16[4,256,128]{2,1,0:T(8,128)(2,1)S(1)}, u32[]{:S(2)}, u32[]{:S(2)}) collective-permute-start(bf16[4,256,128]{2,1,0:T(8,128)(2,1)S(1)} %get-tuple-element.19), channel_id=1, source_target_pairs={{8,128},{16,136},{24,144},{32,152},{40,160},{48,168},{56,176},{64,... | collective-permute-start | bytes 786440 | tf_op jit(solution)/shard_map/ppermute | solution.py:288
  138.1 5.2 %collective-permute-done.6 = bf16[4,256,128]{2,1,0:T(8,128)(2,1)S(1)} collective-permute-done((bf16[4,256,128]{2,1,0:T(8,128)(2,1)S(1)}, bf16[4,256,128]{2,1,0:T(8,128)(2,1)S(1)}, u32[]{:S(2)}, u32[]{:S(2)}) %collective-permute-start.6) | collective-permute-done | bytes 262176 | tf_op jit(solution)/shard_map/ppermute | solution.py:289
  143.3 0.7 collective-permute-done.7
  144.1 1.1 maximum_maximum_fusion
  145.2 9.5 %all-to-all-start.2 = ((bf16[8,512,128]{2,1,0:T(8,128)(2,1)}), bf16[8,512,128]{2,1,0:T(8,128)(2,1)S(1)}, u32[]{:S(2)}, u32[]{:S(2)}) async-start(bf16[8,512,128]{2,1,0:T(8,128)(2,1)} %maximum_maximum_fusion), calls=%async_computation.2 | async-start | bytes 2097152 | tf_op jit(solution)/shard_map/all_to_all | solution.py:240
  154.7 1.2 slice_bitcast_fusion.3
  155.8 0.2 copy.31
  156.0 0.9 copy.38
  156.9 0.2 copy.32
  157.0 0.9 copy.39
  157.9 0.2 copy.33
  158.1 0.9 copy.40
  158.9 26.1 %all-to-all-done.2 = bf16[8,512,128]{2,1,0:T(8,128)(2,1)S(1)} async-done(((bf16[8,512,128]{2,1,0:T(8,128)(2,1)}), bf16[8,512,128]{2,1,0:T(8,128)(2,1)S(1)}, u32[]{:S(2)}, u32[]{:S(2)}) %all-to-all-start.2) | async-done | bytes 1048608 | tf_op jit(solution)/shard_map/all_to_all | solution.py:240
  185.1 0.2 copy.30
  185.3 0.9 copy.37
  186.2 0.2 copy.34
  186.4 0.9 copy.41
  187.2 0.2 copy.35
  187.4 0.9 copy.42
  188.3 0.2 copy.36
  188.4 0.9 copy.43
  (35 shorter events, 1.2 us)
Async XLA Ops:
  0.6 2.9 %copy-start.2 = (bf16[1,128,1024]{2,1,0:T(8,128)(2,1)S(1)}, bf16[1,128,1024]{2,1,0:T(8,128)(2,1)}, u32[]{:S(2)}) copy-start(bf16[1,128,1024]{2,1,0:T(8,128)(2,1)} %param.11) | copy-start | bytes 786436
  0.6 3.3 %copy-start.3 = (bf16[1,128,1024]{2,1,0:T(8,128)(2,1)S(1)}, bf16[1,128,1024]{2,1,0:T(8,128)(2,1)}, u32[]{:S(2)}) copy-start(bf16[1,128,1024]{2,1,0:T(8,128)(2,1)} %param.9) | copy-start | bytes 786436
  3.5 1.0 copy-start.4
  7.9 10.3 %copy-start.5 = (bf16[1,128,1024]{2,1,0:T(8,128)(2,1)S(1)}, bf16[1,128,1024]{2,1,0:T(8,128)(2,1)}, u32[]{:S(2)}) copy-start(bf16[1,128,1024]{2,1,0:T(8,128)(2,1)} %param.13) | copy-start | bytes 786436
  7.9 10.7 %copy-start.6 = (bf16[1,128,1024]{2,1,0:T(8,128)(2,1)S(1)}, bf16[1,128,1024]{2,1,0:T(8,128)(2,1)}, u32[]{:S(2)}) copy-start(bf16[1,128,1024]{2,1,0:T(8,128)(2,1)} %param.14) | copy-start | bytes 786436
  7.9 42.0 %all-to-all-start = ((bf16[8,528,128]{2,1,0:T(8,128)(2,1)}), bf16[8,528,128]{2,1,0:T(8,128)(2,1)S(1)}, u32[]{:S(2)}, u32[]{:S(2)}) async-start(bf16[8,528,128]{2,1,0:T(8,128)(2,1)} %bitcast_dynamic-update-slice_fusion), calls=%async_computation | async-start | bytes 2162688 | tf_op jit(solution)/shard_map/all_to_all | solution.py:240
  18.2 1.0 copy-start.7
  20.5 41.7 %copy-start.8 = (s32[2,16]{1,0:T(2,128)S(1)}, s32[2,16]{1,0:T(2,128)}, u32[]{:S(2)}) copy-start(s32[2,16]{1,0:T(2,128)} %param.16) | copy-start | bytes 388
  49.8 23.1 %all-to-all-start.1 = ((bf16[8,384,128]{2,1,0:T(8,128)(2,1)}), bf16[8,384,128]{2,1,0:T(8,128)(2,1)S(1)}, u32[]{:S(2)}, u32[]{:S(2)}) async-start(bf16[8,384,128]{2,1,0:T(8,128)(2,1)} %pad_maximum_fusion), calls=%async_computation.1 | async-start | bytes 1572864 | tf_op jit(solution)/shard_map/all_to_all | solution.py:240
  54.2 28.0 %collective-permute-start = (bf16[4,272,128]{2,1,0:T(8,128)(2,1)}, bf16[4,272,128]{2,1,0:T(8,128)(2,1)S(1)}, u32[]{:S(2)}, u32[]{:S(2)}) collective-permute-start(bf16[4,272,128]{2,1,0:T(8,128)(2,1)} %get-tuple-element.31), channel_id=1, source_target_pairs={{0,8},{8,16},{16,24},{24,32},{32,40},{40,48},{48,56},{56,64},{64,7... | collective-permute-start | bytes 835592 | tf_op jit(solution)/shard_map/ppermute | solution.py:270
  57.6 24.7 %collective-permute-start.1 = (bf16[4,272,128]{2,1,0:T(8,128)(2,1)}, bf16[4,272,128]{2,1,0:T(8,128)(2,1)S(1)}, u32[]{:S(2)}, u32[]{:S(2)}) collective-permute-start(bf16[4,272,128]{2,1,0:T(8,128)(2,1)} %get-tuple-element.30), channel_id=1, source_target_pairs={{8,0},{16,8},{24,16},{32,24},{40,32},{48,40},{56,48},{64,56},{72,6... | collective-permute-start | bytes 835592 | tf_op jit(solution)/shard_map/ppermute | solution.py:271
  73.8 41.3 %collective-permute-start.3 = (bf16[4,256,128]{2,1,0:T(8,128)(2,1)}, bf16[4,256,128]{2,1,0:T(8,128)(2,1)S(1)}, u32[]{:S(2)}, u32[]{:S(2)}) collective-permute-start(bf16[4,256,128]{2,1,0:T(8,128)(2,1)} %get-tuple-element.44), channel_id=1, source_target_pairs={{0,136},{8,144},{16,152},{24,160},{32,168},{40,176},{48,184},{56,1... | collective-permute-start | bytes 786440 | tf_op jit(solution)/shard_map/ppermute | solution.py:273
  76.7 38.4 %collective-permute-start.4 = (bf16[4,256,128]{2,1,0:T(8,128)(2,1)}, bf16[4,256,128]{2,1,0:T(8,128)(2,1)S(1)}, u32[]{:S(2)}, u32[]{:S(2)}) collective-permute-start(bf16[4,256,128]{2,1,0:T(8,128)(2,1)} %get-tuple-element.43), channel_id=1, source_target_pairs={{8,128},{16,136},{24,144},{32,152},{40,160},{48,168},{56,176},{64,... | collective-permute-start | bytes 786440 | tf_op jit(solution)/shard_map/ppermute | solution.py:274
  82.3 32.8 %collective-permute-start.2 = (bf16[8,256,128]{2,1,0:T(8,128)(2,1)}, bf16[8,256,128]{2,1,0:T(8,128)(2,1)S(1)}, u32[]{:S(2)}, u32[]{:S(2)}) collective-permute-start(bf16[8,256,128]{2,1,0:T(8,128)(2,1)} %slice.74), channel_id=1, source_target_pairs={{0,128},{128,0},{1,129},{129,1},{2,130},{130,2},{3,131},{131,3},{4... | collective-permute-start | bytes 1572872 | tf_op jit(solution)/shard_map/ppermute | solution.py:272
  95.9 14.0 %copy-start = (f32[128,1024]{1,0:T(8,128)}, f32[128,1024]{1,0:T(8,128)S(1)}, u32[]{:S(2)}) copy-start(f32[128,1024]{1,0:T(8,128)S(1)} %get-tuple-element.15.out_t) | copy-start | bytes 1572868
  95.9 12.7 %collective-permute-start.8 = (bf16[4,256,128]{2,1,0:T(8,128)(2,1)S(1)}, bf16[4,256,128]{2,1,0:T(8,128)(2,1)S(1)}, u32[]{:S(2)}, u32[]{:S(2)}) collective-permute-start(bf16[4,256,128]{2,1,0:T(8,128)(2,1)S(1)} %get-tuple-element.21), channel_id=1, source_target_pairs={{0,8},{8,16},{16,24},{24,32},{32,40},{40,48},{48,56},{56,64},{64,7... | collective-permute-start | bytes 786440 | tf_op jit(solution)/shard_map/ppermute | solution.py:285
  97.8 12.0 %collective-permute-start.9 = (bf16[4,256,128]{2,1,0:T(8,128)(2,1)S(1)}, bf16[4,256,128]{2,1,0:T(8,128)(2,1)S(1)}, u32[]{:S(2)}, u32[]{:S(2)}) collective-permute-start(bf16[4,256,128]{2,1,0:T(8,128)(2,1)S(1)} %get-tuple-element.22), channel_id=1, source_target_pairs={{8,0},{16,8},{24,16},{32,24},{40,32},{48,40},{56,48},{64,56},{72,6... | collective-permute-start | bytes 786440 | tf_op jit(solution)/shard_map/ppermute | solution.py:284
  110.9 34.3 %all-to-all-start.3 = ((bf16[8,384,128]{2,1,0:T(8,128)(2,1)}), bf16[8,384,128]{2,1,0:T(8,128)(2,1)}, u32[]{:S(2)}, u32[]{:S(2)}) async-start(bf16[8,384,128]{2,1,0:T(8,128)(2,1)} %maximum_maximum_fusion.1), calls=%async_computation.3 | async-start | bytes 1572864 | tf_op jit(solution)/shard_map/all_to_all | solution.py:240
  115.1 1.0 copy-start.1
  129.2 8.8 %collective-permute-start.5 = (bf16[8,256,128]{2,1,0:T(8,128)(2,1)S(1)}, bf16[8,256,128]{2,1,0:T(8,128)(2,1)S(1)}, u32[]{:S(2)}, u32[]{:S(2)}) collective-permute-start(bf16[8,256,128]{2,1,0:T(8,128)(2,1)S(1)} %get-tuple-element.17), channel_id=1, source_target_pairs={{0,128},{128,0},{1,129},{129,1},{2,130},{130,2},{3,131},{131,3},{4... | collective-permute-start | bytes 1572872 | tf_op jit(solution)/shard_map/ppermute | solution.py:290
  129.5 13.8 %collective-permute-start.6 = (bf16[4,256,128]{2,1,0:T(8,128)(2,1)S(1)}, bf16[4,256,128]{2,1,0:T(8,128)(2,1)S(1)}, u32[]{:S(2)}, u32[]{:S(2)}) collective-permute-start(bf16[4,256,128]{2,1,0:T(8,128)(2,1)S(1)} %get-tuple-element.18), channel_id=1, source_target_pairs={{0,136},{8,144},{16,152},{24,160},{32,168},{40,176},{48,184},{56,1... | collective-permute-start | bytes 786440 | tf_op jit(solution)/shard_map/ppermute | solution.py:289
  131.4 12.6 %collective-permute-start.7 = (bf16[4,256,128]{2,1,0:T(8,128)(2,1)S(1)}, bf16[4,256,128]{2,1,0:T(8,128)(2,1)S(1)}, u32[]{:S(2)}, u32[]{:S(2)}) collective-permute-start(bf16[4,256,128]{2,1,0:T(8,128)(2,1)S(1)} %get-tuple-element.19), channel_id=1, source_target_pairs={{8,128},{16,136},{24,144},{32,152},{40,160},{48,168},{56,176},{64,... | collective-permute-start | bytes 786440 | tf_op jit(solution)/shard_map/ppermute | solution.py:288
  145.2 39.8 %all-to-all-start.2 = ((bf16[8,512,128]{2,1,0:T(8,128)(2,1)}), bf16[8,512,128]{2,1,0:T(8,128)(2,1)S(1)}, u32[]{:S(2)}, u32[]{:S(2)}) async-start(bf16[8,512,128]{2,1,0:T(8,128)(2,1)} %maximum_maximum_fusion), calls=%async_computation.2 | async-start | bytes 2097152 | tf_op jit(solution)/shard_map/all_to_all | solution.py:240

commit v2 on v1

v2 whole, which is shorter than its diff:
```python
import functools

import jax
import jax.numpy as jnp
from jax import lax
from jax.experimental import pallas as pl
from jax.experimental.pallas import tpu as pltpu
from jax.sharding import PartitionSpec as P

HEADS = 16
HEAD = 64
BLOCK = 1024
HALF = 512
CHUNK = 128
QROWS = 256
EXT = BLOCK + 2 * HALF
SELF_WIN = QROWS + 2 * HALF
CROSS_WIN = BLOCK + CHUNK
NEG = -16384.0
SCALE = HEAD**-0.5
VROWS = 16
F32 = jnp.float32
BF16 = jnp.bfloat16
NT = (((1,), (1,)), ((), ()))
NN = (((1,), (0,)), ((), ()))


def dot(a, b, dims=NN):
    return lax.dot_general(a, b, dims, preferred_element_type=F32)


def eye(n):
    rows = lax.broadcasted_iota(jnp.int32, (n, n), 0)
    return jnp.where(rows == lax.broadcasted_iota(jnp.int32, (n, n), 1), 1.0, 0.0).astype(BF16)


def flipped(x):
    return dot(eye(x.shape[1]), x, NT).astype(BF16)


def stage_keys(chunks, values, bias, kx, kt, v, vt):
    padded = jnp.concatenate([bias, jnp.zeros((CHUNK - 16, CHUNK), F32)], axis=0).astype(BF16)
    turned = dot(eye(CHUNK), padded, NT)
    lane = lax.broadcasted_iota(jnp.int32, (CHUNK, CHUNK), 1)
    for c in range(EXT // CHUNK):
        at = pl.ds(c * CHUNK, CHUNK)
        k = chunks(c)
        val = values(c)
        kx[at, 0:CHUNK] = k
        kx[at, CHUNK : 2 * CHUNK] = jnp.where(lane == c, turned, 0.0).astype(BF16)
        kt[:, at] = flipped(k)
        v[at, :] = val
        vt[:, at] = flipped(val)


def tile_step(q, gt, start, width, step, windowed, scratch):
    kx, kt, v, vt, s, e, ds, dk, dv = scratch
    count = width // step
    head_lane = lax.broadcasted_iota(jnp.int32, (QROWS, 2 * HEAD), 1) // HEAD
    scaled = q.astype(F32) * SCALE
    ones = jnp.ones((QROWS, CHUNK), BF16)
    win = pl.ds(start, width)
    outs, gqs, q_heads, g_heads, tops, dots = [], [], [], [], [], []
    for h in range(2):
        qh = jnp.where(head_lane == h, scaled, 0.0).astype(BF16)
        qx = jnp.concatenate([qh, ones], axis=1)
        q_heads.append(qh)
        top = None
        for b in range(count):
            at = pl.ds(start + b * step, step)
            scores = dot(kx[at, :], qx, NT)
            if windowed and b in (0, count - 1):
                r = lax.broadcasted_iota(jnp.int32, (step, QROWS), 0)
                c = lax.broadcasted_iota(jnp.int32, (step, QROWS), 1)
                scores = jnp.where(r >= c if b == 0 else r <= c, scores, -1e30)
            s[h, b * step : (b + 1) * step, :] = scores
            high = jnp.max(scores, axis=0, keepdims=True)
            top = high if top is None else jnp.maximum(top, high)
        tops.append(top)
    for h in range(2):
        rows_h = slice(h * HEAD, (h + 1) * HEAD)
        cols_h = slice(h * QROWS, (h + 1) * QROWS)
        total = jnp.zeros((1, QROWS), F32)
        for b in range(count):
            rows = slice(b * step, (b + 1) * step)
            p = jnp.exp(s[h, rows, :] - tops[h])
            total = total + jnp.sum(p, axis=0, keepdims=True)
            e[rows, cols_h] = p.astype(BF16)
        inverse = 1.0 / total
        out = dot(vt[rows_h, win], e[:, cols_h]) * inverse
        g = (gt[rows_h, :].astype(F32) * inverse).astype(BF16)
        dots.append(jnp.sum(out * g.astype(F32), axis=0, keepdims=True))
        zeros = jnp.zeros((HEAD, QROWS), BF16)
        g_heads.append(jnp.concatenate([g, zeros] if h == 0 else [zeros, g], axis=0))
        outs.append(out)
    for h in range(2):
        rows_h = slice(h * HEAD, (h + 1) * HEAD)
        cols_h = slice(h * QROWS, (h + 1) * QROWS)
        for b in range(count):
            rows = slice(b * step, (b + 1) * step)
            at = pl.ds(start + b * step, step)
            dp = dot(v[at, :], g_heads[h])
            ds[rows, cols_h] = (e[rows, cols_h].astype(F32) * (dp - dots[h])).astype(BF16)
        gqs.append(dot(kt[rows_h, win], ds[:, cols_h]) * SCALE)
    dv[win, :] += dot(e[...], jnp.concatenate(g_heads, axis=1), NT)
    dk[win, :] += dot(ds[...], jnp.concatenate(q_heads, axis=0))
    return jnp.concatenate(outs, axis=0), jnp.concatenate(gqs, axis=0)


def validity(refs, row):
    parts = [ref[c, 0:VROWS, :].astype(F32)[row : row + 1] for ref in refs for c in range(4)]
    return jnp.concatenate(parts, axis=0)


def piece(refs, first):
    return lambda c: refs[c // 4][c % 4, first : first + CHUNK, :]


def emit_sums(dk, dv, back, to_lo, to_hi):
    for n, acc in enumerate((dk, dv)):
        rows = slice(n * CHUNK, (n + 1) * CHUNK)
        to_lo[:, rows, :] = acc[0:HALF, :].astype(BF16).reshape(4, CHUNK, CHUNK)
        back[:, rows, :] = acc[HALF : HALF + BLOCK, :].astype(BF16).reshape(8, CHUNK, CHUNK)
        to_hi[:, rows, :] = acc[HALF + BLOCK : EXT, :].astype(BF16).reshape(4, CHUNK, CHUNK)


def self_kernel(before, low, high, after, asks, out_t, pay, back, to_lo, to_hi, kx, kt, v, vt, gt, s, e, ds, dk, dv):
    refs = (before, low, high, after)
    bias = jnp.where(validity(refs, 0) > 0.5, 0.0, NEG)
    stage_keys(piece(refs, VROWS), piece(refs, VROWS + CHUNK), bias, kx, kt, v, vt)
    for c in range(8):
        gt[:, c * CHUNK : (c + 1) * CHUNK] = flipped(asks[c, CHUNK : 2 * CHUNK, :])
    dk[...] = jnp.zeros_like(dk)
    dv[...] = jnp.zeros_like(dv)

    def step(i, carry):
        start = pl.multiple_of(i * QROWS, QROWS)
        here = pl.ds(start, QROWS)
        q = asks[pl.ds(2 * i, 2), 0:CHUNK, :].reshape(QROWS, CHUNK)
        out, gq = tile_step(q, gt[:, here], start, SELF_WIN, QROWS, True, (kx, kt, v, vt, s, e, ds, dk, dv))
        out_t[:, here] = out
        pay[pl.ds(2 * i, 2), 0:CHUNK, :] = flipped(gq.astype(BF16)).reshape(2, CHUNK, CHUNK)
        return carry

    lax.fori_loop(0, BLOCK // QROWS, step, 0)
    emit_sums(dk, dv, back, to_lo, to_hi)


def cross_kernel(pos, before, low, high, after, asks, out_t, pay, back, to_lo, to_hi, kx, kt, v, vt, gt, s, e, ds, dk, dv):
    first = pos[2]
    place = lax.broadcasted_iota(jnp.int32, (16, CHUNK), 0) * CHUNK + lax.broadcasted_iota(jnp.int32, (16, CHUNK), 1)
    inside = (place >= first) & (place < first + BLOCK)
    refs = (before, low, high, after)
    bias = jnp.where(inside & (validity(refs, 1) > 0.5), 0.0, NEG)
    stage_keys(piece(refs, VROWS + 2 * CHUNK), piece(refs, VROWS + 3 * CHUNK), bias, kx, kt, v, vt)
    for c in range(8):
        gt[:, c * CHUNK : (c + 1) * CHUNK] = flipped(asks[c, CHUNK : 2 * CHUNK, :])
    dk[...] = jnp.zeros_like(dk)
    dv[...] = jnp.zeros_like(dv)
    start = pl.multiple_of(lax.shift_right_logical(first, 7) * CHUNK, CHUNK)

    def step(i, carry):
        here = pl.ds(pl.multiple_of(i * QROWS, QROWS), QROWS)
        q = asks[pl.ds(2 * i, 2), 2 * CHUNK : 3 * CHUNK, :].reshape(QROWS, CHUNK)
        out, gq = tile_step(q, gt[:, here], start, CROSS_WIN, 384, False, (kx, kt, v, vt, s, e, ds, dk, dv))
        both = (out + out_t[:, here]).astype(BF16)
        pay[pl.ds(2 * i, 2), 0:CHUNK, :] = flipped(both).reshape(2, CHUNK, CHUNK)
        pay[pl.ds(2 * i, 2), CHUNK : 2 * CHUNK, :] = flipped(gq.astype(BF16)).reshape(2, CHUNK, CHUNK)
        return carry

    lax.fori_loop(0, BLOCK // QROWS, step, 0)
    emit_sums(dk, dv, back, to_lo, to_hi)


def scratch(width):
    return [
        pltpu.VMEM((EXT, 2 * CHUNK), BF16),
        pltpu.VMEM((CHUNK, EXT), BF16),
        pltpu.VMEM((EXT, CHUNK), BF16),
        pltpu.VMEM((CHUNK, EXT), BF16),
        pltpu.VMEM((CHUNK, BLOCK), BF16),
        pltpu.VMEM((2, width, QROWS), F32),
        pltpu.VMEM((width, 2 * QROWS), BF16),
        pltpu.VMEM((width, 2 * QROWS), BF16),
        pltpu.VMEM((EXT, CHUNK), F32),
        pltpu.VMEM((EXT, CHUNK), F32),
    ]


def shaped(shape, dtype=BF16):
    return jax.ShapeDtypeStruct(shape, dtype)


def run_attention(kernel, name, width, operands, outs):
    vmem = pl.BlockSpec(memory_space=pltpu.VMEM)
    outs = outs + (shaped((8, 2 * CHUNK, CHUNK)), shaped((4, 2 * CHUNK, CHUNK)), shaped((4, 2 * CHUNK, CHUNK)))
    return pl.pallas_call(
        kernel,
        out_shape=outs,
        in_specs=[pl.BlockSpec(memory_space=pltpu.SMEM) if x.ndim == 1 else vmem for x in operands],
        out_specs=[vmem] * len(outs),
        scratch_shapes=scratch(width),
        compiler_params=pltpu.CompilerParams(vmem_limit_bytes=14 * 2**20),
        cost_estimate=pl.CostEstimate(flops=8 * 10**9, bytes_accessed=3 * 2**20, transcendentals=2621440),
        name=name,
    )(*operands)


def run_self(*operands):
    outs = (shaped((CHUNK, BLOCK), F32), shaped((8, CHUNK, CHUNK)))
    return run_attention(self_kernel, "self_attention", SELF_WIN, operands, outs)


def run_cross(*operands):
    outs = (shaped((8, 2 * CHUNK, CHUNK)),)
    return run_attention(cross_kernel, "cross_attention", CROSS_WIN, operands, outs)


def small_call(kernel, name, pos, operands, outs):
    vmem = pl.BlockSpec(memory_space=pltpu.VMEM)
    return pl.pallas_call(
        kernel,
        out_shape=outs,
        in_specs=[pl.BlockSpec(memory_space=pltpu.SMEM)] + [vmem] * len(operands),
        out_specs=[vmem] * len(outs),
        compiler_params=pltpu.CompilerParams(vmem_limit_bytes=8 * 2**20),
        cost_estimate=pl.CostEstimate(flops=0, bytes_accessed=2**21, transcendentals=0),
        name=name,
    )(pos, *operands)


def pack_kernel(marked, count, pos, *refs):
    rows, outs = refs[:count], refs[count:]
    at = 0
    if marked:
        valid = rows[0][...].astype(F32)
        own = jnp.where(pos[3] == 0, valid[0:1], valid[1:2])
        other = jnp.where(pos[3] == 0, valid[1:2], valid[0:1])
        marks = jnp.concatenate([own, other, jnp.zeros((VROWS - 2, CHUNK), F32)], axis=0).astype(BF16)
        for out in outs:
            for d in range(4):
                out[d, 0:VROWS, :] = marks
        at, rows = VROWS, rows[1:]
    for n, ref in enumerate(rows):
        spot = slice(at + n * CHUNK, at + (n + 1) * CHUNK)
        for out, z in zip(outs, (pos[1], 1 - pos[1])):
            for d in range(4):
                first = pl.multiple_of((2 * lax.rem(pos[0] + d, 4) + z) * CHUNK, CHUNK)
                out[d, spot, :] = ref[0, :, pl.ds(first, CHUNK)]


def pack(pos, *rows, marked=False):
    height = (len(rows) - 1) * CHUNK + VROWS if marked else len(rows) * CHUNK
    kernel = functools.partial(pack_kernel, marked, len(rows))
    return small_call(kernel, "pack", pos, rows, (shaped((4, height, CHUNK)),) * 2)


def join_kernel(pos, *refs):
    outs = refs[-4:]
    at = 0
    for keep, got in zip(refs[0:-4:2], refs[1:-4:2]):
        rows = slice(at, at + keep.shape[1])
        at += keep.shape[1]
        for d in range(4):
            outs[d][pl.ds(pos[1], 1), rows, :] = keep[d][None]
            outs[d][pl.ds(1 - pos[1], 1), rows, :] = got[d][None]


def join(pos, *pairs):
    height = sum(x.shape[1] for x in pairs[::2])
    return small_call(join_kernel, "join", pos, pairs, (shaped((2, height, CHUNK)),) * 4)


def halves_kernel(pos, *refs):
    parts, (low, high) = refs[:-2], refs[-2:]
    for d in range(4):
        y = lax.rem(pos[0] - d + 4, 4)

        @pl.when(y < 2)
        def _():
            low[pl.ds(2 * y, 2)] = parts[d][...]

        @pl.when(y >= 2)
        def _():
            high[pl.ds(2 * y - 4, 2)] = parts[d][...]


def halves(pos, parts):
    return small_call(halves_kernel, "halves", pos, parts, (shaped((4,) + parts[0].shape[1:]),) * 2)


def whole_kernel(pos, *refs):
    for d in range(4):
        refs[-1][pl.ds(2 * lax.rem(pos[0] - d + 4, 4), 2)] = refs[d][...]


def whole(pos, parts):
    return small_call(whole_kernel, "whole", pos, parts, (shaped((8,) + parts[0].shape[1:]),))[0]


def unpack_kernel(pos, got, *outs):
    for n, out in enumerate(outs):
        for s in range(8):
            out[0, :, s * CHUNK : (s + 1) * CHUNK] = got[s, n * CHUNK : (n + 1) * CHUNK, :]


def unpack(pos, got):
    outs = (shaped((1, CHUNK, HEADS * HEAD)),) * (got.shape[1] // CHUNK)
    return small_call(unpack_kernel, "unpack", pos, (got,), outs)


def merge_kernel(pos, *refs):
    out = refs[-1]
    for n in range(2):
        rows = slice(2 * n * CHUNK, 2 * (n + 1) * CHUNK)
        center, below, above = refs[3 * n : 3 * n + 3]
        for first, halo in ((0, below), (4, above)):
            total = center[first : first + 4].astype(F32) + halo[...].astype(F32)
            out[first : first + 4, rows, :] = total.astype(BF16)


def merge(pos, *parts):
    return small_call(merge_kernel, "merge", pos, parts, (shaped((8, 4 * CHUNK, CHUNK)),))[0]


def order_kernel(pos, *refs):
    outs = refs[-2:]
    at = 0
    for ref in refs[:-2]:
        rows = slice(at, at + ref.shape[1])
        at += ref.shape[1]
        for out, z in zip(outs, (pos[1], 1 - pos[1])):
            for d in range(4):
                out[d, rows, :] = ref[pl.ds(2 * lax.rem(pos[0] + d, 4) + z, 1)][0]


def order(pos, *parts):
    height = sum(x.shape[1] for x in parts)
    return small_call(order_kernel, "order", pos, parts, (shaped((4, height, CHUNK)),) * 2)


def unpack_parts_kernel(pos, *refs):
    parts, outs = refs[:4], refs[4:]
    for d in range(4):
        y = lax.rem(pos[0] - d + 4, 4)
        for n, out in enumerate(outs):
            for z in range(2):
                at = pl.multiple_of((2 * y + z) * CHUNK, CHUNK)
                out[0, :, pl.ds(at, CHUNK)] = parts[d][z, n * CHUNK : (n + 1) * CHUNK, :]


def unpack_parts(pos, parts):
    outs = (shaped((1, CHUNK, HEADS * HEAD)),) * (parts[0].shape[1] // CHUNK)
    return small_call(unpack_parts_kernel, "unpack_parts", pos, parts, outs)


def across_z(send):
    size = lax.axis_size("seq")
    return lax.ppermute(send, "seq", [(i, i ^ 1) for i in range(size)])


def along_y(parts):
    size = lax.axis_size("seq")
    return (parts[0],) + tuple(
        lax.ppermute(parts[d], "seq", [(i, (i + 2 * d) % size) for i in range(size)]) for d in range(1, 4)
    )


def exchange(packed):
    return lax.all_to_all(packed, "seq", split_axis=0, concat_axis=0, tiled=True)


def shards(queries, key_rows, value_rows, cross_queries, cross_keys, cross_values, grad_out, offsets, key_valid):
    tower_id = lax.axis_index("tower")
    block_id = lax.axis_index("blk")
    blocks = lax.axis_size("blk")
    up = [(b, b + 1) for b in range(blocks - 1)]
    down = [(b + 1, b) for b in range(blocks - 1)]
    over_up = [(t * blocks + b, (1 - t) * blocks + b + 1) for t in range(2) for b in range(blocks - 1)]
    over_down = [(t * blocks + b + 1, (1 - t) * blocks + b) for t in range(2) for b in range(blocks - 1)]
    swap = [(0, 1), (1, 0)]
    both = ("tower", "blk")

    seq_id = lax.axis_index("seq")
    band = HALF + offsets[tower_id, block_id]
    pos = jnp.stack([seq_id // 2, seq_id % 2, band, tower_id]).astype(jnp.int32)

    hold = lax.optimization_barrier
    swapped_k = lax.ppermute(cross_keys, "tower", swap)
    swapped_v = lax.ppermute(cross_values, "tower", swap)
    keep_a, send_a = pack(pos, key_valid, key_rows, value_rows, marked=True)
    got_a = across_z(send_a)
    keep_c, send_c = pack(pos, swapped_k, swapped_v)
    queries, send_c = hold((queries, send_c))
    got_c = across_z(send_c)
    keep_b, send_b = pack(pos, queries, grad_out, cross_queries)
    got_b = across_z(send_b)
    low, high = halves(pos, along_y(join(pos, keep_a, got_a, keep_c, got_c)))
    before = lax.ppermute(high, "blk", up)
    after = lax.ppermute(low, "blk", down)
    asks = whole(pos, along_y(join(pos, keep_b, got_b)))

    out_t, pay_q, center, to_lo, to_hi = run_self(before, low, high, after, asks)
    above = lax.ppermute(to_lo, "blk", down)
    below = lax.ppermute(to_hi, "blk", up)
    pay_x, back, c_lo, c_hi = run_cross(pos, before, low, high, after, asks, out_t)
    keep_p, send_p = order(pos, pay_q, pay_x)
    got_p = across_z(send_p)
    c_above = lax.ppermute(c_lo, both, over_down)
    c_below = lax.ppermute(c_hi, both, over_up)
    c_mid = lax.ppermute(back, "tower", swap)
    got_p, center = hold((got_p, center))
    got_s = exchange(merge(pos, center, below, above, c_mid, c_below, c_above))
    g_q, attended, g_cq = unpack_parts(pos, along_y(join(pos, keep_p, got_p)))
    g_k, g_v, g_ck, g_cv = unpack(pos, got_s)
    return attended, g_q, g_k, g_v, g_cq, g_ck, g_cv


def solution(mesh):
    rows = P("tower", ("blk", "seq"), None)
    in_specs = (rows,) * 7 + (P(), P(None, ("blk", "seq")))
    return jax.shard_map(shards, mesh=mesh, in_specs=in_specs, out_specs=(rows,) * 7, check_vma=False)
```

time: 190 us -> 173 us (0.911)
  local copies, waits for them, and re-layouts: 20.2 us -> 3.76 us
  waiting for transfers between devices: 76.7 us -> 67.6 us
  Pallas kernels: 26.6 us -> 33.9 us
  starting transfers between devices: 59.9 us -> 65.4 us
  other arithmetic: 4.15 us -> 0.08 us
    all_to_all x4 -> x1, waiting for transfers between devices: 65 us -> 10.6 us  [exchange(): lax.all_to_all(packed, 'seq', split_axis=0, concat_axis=0, tiled=True)]
    ppermute x7 -> x19, waiting for transfers between devices: 5.84 us -> 56.9 us  [the longest x4 30.4 us: across_z(): return lax.ppermute(send, 'seq', [(i, i ^ 1) for i in range(size)])]
    ppermute x7 -> x19, starting transfers between devices: 23.6 us -> 50.5 us  [the longest x4 17.6 us: across_z(): return lax.ppermute(send, 'seq', [(i, i ^ 1) for i in range(size)])]
    all_to_all x4 -> x1, starting transfers between devices: 27.5 us -> 7.31 us  [exchange(): lax.all_to_all(packed, 'seq', split_axis=0, concat_axis=0, tiled=True)]
    unnamed x36 -> x14, local copies, waits for them, and re-layouts: 12.5 us -> 3.18 us
    pallas_call x2 -> x14, Pallas kernels: 26.6 us -> 33.9 us  [the longest x2 23 us: run_attention(): pl.pallas_call(kernel, out_shape=outs, in_specs=[pl.BlockSpec(memory_spac...]
    ppermute x1, waiting for transfers between devices: 5.2 us -> 0.01 us  [shards(): c_below = lax.ppermute(c_hi, both, over_up)]
    concatenate x4 -> x0, other arithmetic: 3.03 us -> none  [the longest x1 1.05 us: shards(): sent_c = jnp.concatenate([pay_c, merged(c_mid, c_below, c_above)], axis=1)]
  transfers between devices with their start and end apart: 14 -> 23, of which waited for: 7 -> 12; matrix products, arithmetic and copies ran while one was open for 6% -> 0% of each run, Pallas kernels for 14% -> 4%
where the time goes in v2:
time: 173 us; the launch traced here: 172 us
  waiting for transfers between devices  67.6 us (39%)
  starting transfers between devices  65.4 us (38%)
  Pallas kernels  33.9 us (20%)
  local copies, waits for them, and re-layouts  3.76 us (2%)
    ppermute x4, waiting for transfers between devices, across_z(): return lax.ppermute(send, 'seq', [(i, i ^ 1) for i in range(size)])  30.4 us
    pallas_call x2, Pallas kernels, run_attention(): pl.pallas_call(kernel, out_shape=outs, in_specs=[pl.BlockSpec(memory_spac...  23 us
    ppermute x9, waiting for transfers between devices, along_y(): lax.ppermute(parts[d], 'seq', [(i, (i + 2 * d) % size) for i in range(siz...  22.7 us
    ppermute x4, starting transfers between devices, across_z(): return lax.ppermute(send, 'seq', [(i, i ^ 1) for i in range(size)])  17.6 us
    ppermute x9, starting transfers between devices, along_y(): lax.ppermute(parts[d], 'seq', [(i, (i + 2 * d) % size) for i in range(siz...  16.4 us
    pallas_call x12, Pallas kernels, small_call(): pl.pallas_call(kernel, out_shape=outs, in_specs=[pl.BlockSpec(memory_spac...  10.9 us
    all_to_all x1, waiting for transfers between devices, exchange(): lax.all_to_all(packed, 'seq', split_axis=0, concat_axis=0, tiled=True)  10.6 us
    all_to_all x1, starting transfers between devices, exchange(): lax.all_to_all(packed, 'seq', split_axis=0, concat_axis=0, tiled=True)  7.31 us
  transfers between devices with their start and end apart: 23, of which 12 were waited for; matrix products, arithmetic and copies ran while one was open for 0% of the time, Pallas kernels for 4%

profile of v2, /device:TPU:32, one launch (start us, length us, event | category | flops | bytes accessed | tf_op | source)
XLA Modules:
  0.0 172.3 jit_solution(12381527734699384983)
XLA Ops:
  0.6 0.1 collective-permute-start.1
  0.7 0.5 collective-permute-start.2
  1.2 0.7 copy-done.6
  1.9 0.6 dynamic_slice.3
  3.1 0.0 copy-start.5
  3.2 0.1 pad_add_fusion.pos
  3.2 0.6 copy-done.5
  3.8 0.9 copy-done
  4.8 0.9 copy-done.1
  5.7 0.7 pack.3
  6.4 6.4 %collective-permute-start = (bf16[4,272,128]{2,1,0:T(8,128)(2,1)S(1)}, bf16[4,272,128]{2,1,0:T(8,128)(2,1)S(1)}, u32[]{:S(2)}, u32[]{:S(2)}) collective-permute-start(bf16[4,272,128]{2,1,0:T(8,128)(2,1)S(1)} %get-tuple-element.50), channel_id=1, source_target_pairs={{0,1},{1,0},{2,3},{3,2},{4,5},{5,4},{6,7},{7,6},{8,9},{9,8},{10,11... | collective-permute-start | bytes 835592 | tf_op jit(solution)/shard_map/ppermute | solution.py:359
  12.8 0.0 collective-permute-done.1.refs_0_
  12.8 0.0 collective-permute-done.2.refs_1_
  12.8 0.7 pack.4
  13.5 0.1 collective-permute-start.3
  13.6 16.2 %collective-permute-done.refs_1_ = bf16[4,272,128]{2,1,0:T(8,128)(2,1)S(1)} collective-permute-done((bf16[4,272,128]{2,1,0:T(8,128)(2,1)S(1)}, bf16[4,272,128]{2,1,0:T(8,128)(2,1)S(1)}, u32[]{:S(2)}, u32[]{:S(2)}) %collective-permute-start) | collective-permute-done | bytes 278560 | tf_op jit(solution)/shard_map/ppermute | solution.py:359
  29.8 7.3 %collective-permute-done.3.refs_3_ = bf16[4,256,128]{2,1,0:T(8,128)(2,1)S(1)} collective-permute-done((bf16[4,256,128]{2,1,0:T(8,128)(2,1)S(1)}, bf16[4,256,128]{2,1,0:T(8,128)(2,1)S(1)}, u32[]{:S(2)}, u32[]{:S(2)}) %collective-permute-start.3) | collective-permute-done | bytes 262176 | tf_op jit(solution)/shard_map/ppermute | solution.py:359
  37.1 0.6 join.3
  37.7 1.7 collective-permute-start.4
  39.3 2.9 %collective-permute-start.5 = (bf16[2,528,128]{2,1,0:T(8,128)(2,1)S(1)}, bf16[2,528,128]{2,1,0:T(8,128)(2,1)S(1)}, u32[]{:S(2)}, u32[]{:S(2)}) collective-permute-start(bf16[2,528,128]{2,1,0:T(8,128)(2,1)S(1)} %get-tuple-element.56), channel_id=1, source_target_pairs={{0,4},{1,5},{2,6},{3,7},{4,0},{5,1},{6,2},{7,3},{8,12},{9,13},{10,... | collective-permute-start | bytes 811016 | tf_op jit(solution)/shard_map/ppermute | solution.py:365
  42.2 1.3 collective-permute-start.6
  43.6 0.8 pack.5
  44.4 5.6 %collective-permute-start.9 = (bf16[4,384,128]{2,1,0:T(8,128)(2,1)S(1)}, bf16[4,384,128]{2,1,0:T(8,128)(2,1)S(1)}, u32[]{:S(2)}, u32[]{:S(2)}) collective-permute-start(bf16[4,384,128]{2,1,0:T(8,128)(2,1)S(1)} %get-tuple-element.62), channel_id=1, source_target_pairs={{0,1},{1,0},{2,3},{3,2},{4,5},{5,4},{6,7},{7,6},{8,9},{9,8},{10,11... | collective-permute-start | bytes 1179656 | tf_op jit(solution)/shard_map/ppermute | solution.py:359
  50.0 0.0 collective-permute-done.4.refs_1_
  50.0 3.9 %collective-permute-done.5.refs_2_ = bf16[2,528,128]{2,1,0:T(8,128)(2,1)S(1)} collective-permute-done((bf16[2,528,128]{2,1,0:T(8,128)(2,1)S(1)}, bf16[2,528,128]{2,1,0:T(8,128)(2,1)S(1)}, u32[]{:S(2)}, u32[]{:S(2)}) %collective-permute-start.5) | collective-permute-done | bytes 270368 | tf_op jit(solution)/shard_map/ppermute | solution.py:365
  53.8 0.0 collective-permute-done.6.refs_3_
  53.8 0.7 halves.1
  54.5 3.4 %collective-permute-start.7 = (bf16[4,528,128]{2,1,0:T(8,128)(2,1)S(1)}, bf16[4,528,128]{2,1,0:T(8,128)(2,1)S(1)}, u32[]{:S(2)}, u32[]{:S(2)}) collective-permute-start(bf16[4,528,128]{2,1,0:T(8,128)(2,1)S(1)} %get-tuple-element.58.high), channel_id=1, source_target_pairs={{0,8},{8,16},{16,24},{24,32},{32,40},{40,48},{48,56},{56,64},{64,7... | collective-permute-start | bytes 1622024 | tf_op jit(solution)/shard_map/ppermute | solution.py:399
  57.9 4.6 %collective-permute-start.8 = (bf16[4,528,128]{2,1,0:T(8,128)(2,1)S(1)}, bf16[4,528,128]{2,1,0:T(8,128)(2,1)S(1)}, u32[]{:S(2)}, u32[]{:S(2)}) collective-permute-start(bf16[4,528,128]{2,1,0:T(8,128)(2,1)S(1)} %get-tuple-element.59.low), channel_id=1, source_target_pairs={{8,0},{16,8},{24,16},{32,24},{40,32},{48,40},{56,48},{64,56},{72,6... | collective-permute-start | bytes 1622024 | tf_op jit(solution)/shard_map/ppermute | solution.py:400
  62.5 1.0 collective-permute-done.9.refs_1_
  63.5 0.6 join.4
  64.1 0.7 collective-permute-start.10
  64.8 2.0 %collective-permute-start.11 = (bf16[2,384,128]{2,1,0:T(8,128)(2,1)S(1)}, bf16[2,384,128]{2,1,0:T(8,128)(2,1)S(1)}, u32[]{:S(2)}, u32[]{:S(2)}) collective-permute-start(bf16[2,384,128]{2,1,0:T(8,128)(2,1)S(1)} %get-tuple-element.65), channel_id=1, source_target_pairs={{0,4},{1,5},{2,6},{3,7},{4,0},{5,1},{6,2},{7,3},{8,12},{9,13},{10,... | collective-permute-start | bytes 589832 | tf_op jit(solution)/shard_map/ppermute | solution.py:365
  66.8 1.6 collective-permute-start.12
  68.4 7.9 %collective-permute-done.10.refs_1_ = bf16[2,384,128]{2,1,0:T(8,128)(2,1)S(1)} collective-permute-done((bf16[2,384,128]{2,1,0:T(8,128)(2,1)S(1)}, bf16[2,384,128]{2,1,0:T(8,128)(2,1)S(1)}, u32[]{:S(2)}, u32[]{:S(2)}) %collective-permute-start.10) | collective-permute-done | bytes 196640 | tf_op jit(solution)/shard_map/ppermute | solution.py:365
  76.3 0.0 collective-permute-done.11.refs_2_
  76.3 0.6 collective-permute-done.12.refs_3_
  76.9 0.6 whole.1.asks
  77.5 0.0 collective-permute-done.8.after
  77.5 11.6 %self_attention.1 = (f32[128,1024]{1,0:T(8,128)S(1)}, bf16[8,128,128]{2,1,0:T(8,128)(2,1)S(1)}, bf16[8,256,128]{2,1,0:T(8,128)(2,1)S(1)}, bf16[4,256,128]{2,1,0:T(8,128)(2,1)S(1)}, bf16[4,256,128]{2,1,0:T(8,128)(2,1)S(1)}) custom-call(bf16[4,528,128]{2,1,0:T(8,128)(2,1)S(1)} %collective-permute-done.7.before, ...), custom_call_target="tpu_custom_call" | custom-call | flops 8000000000 | bytes 3145728 | tf_op jit(solution)/shard_map/self_attention/pallas_call | solution.py:197
  89.1 11.4 %cross_attention.1 = (bf16[8,256,128]{2,1,0:T(8,128)(2,1)S(1)}, bf16[8,256,128]{2,1,0:T(8,128)(2,1)S(1)}, bf16[4,256,128]{2,1,0:T(8,128)(2,1)S(1)}, bf16[4,256,128]{2,1,0:T(8,128)(2,1)S(1)}) custom-call(s32[4]{0:T(128)S(1)} %pad_add_fusion.pos, bf16[4,528,128]{2,1,0:T(8,128)(2,1)S(1)} %collective-permute-done.7.before, ...), custom_call_target="tpu_custom_call" | custom-call | flops 8000000000 | bytes 3145728 | tf_op jit(solution)/shard_map/cross_attention/pallas_call | solution.py:197
  100.5 0.6 order.1
  101.2 5.5 %collective-permute-start.13 = (bf16[4,384,128]{2,1,0:T(8,128)(2,1)S(1)}, bf16[4,384,128]{2,1,0:T(8,128)(2,1)S(1)}, u32[]{:S(2)}, u32[]{:S(2)}) collective-permute-start(bf16[4,384,128]{2,1,0:T(8,128)(2,1)S(1)} %get-tuple-element.71), channel_id=1, source_target_pairs={{0,1},{1,0},{2,3},{3,2},{4,5},{5,4},{6,7},{7,6},{8,9},{9,8},{10,11... | collective-permute-start | bytes 1179656 | tf_op jit(solution)/shard_map/ppermute | solution.py:359
  106.7 0.0 collective-permute-start.19
  106.7 3.5 %collective-permute-start.20 = (bf16[4,256,128]{2,1,0:T(8,128)(2,1)S(1)}, bf16[4,256,128]{2,1,0:T(8,128)(2,1)S(1)}, u32[]{:S(2)}, u32[]{:S(2)}) collective-permute-start(bf16[4,256,128]{2,1,0:T(8,128)(2,1)S(1)} %get-tuple-element.84), channel_id=1, source_target_pairs={{0,136},{8,144},{16,152},{24,160},{32,168},{40,176},{48,184},{56,1... | collective-permute-start | bytes 786440 | tf_op jit(solution)/shard_map/ppermute | solution.py:410
  110.2 4.2 %collective-permute-start.21 = (bf16[4,256,128]{2,1,0:T(8,128)(2,1)S(1)}, bf16[4,256,128]{2,1,0:T(8,128)(2,1)S(1)}, u32[]{:S(2)}, u32[]{:S(2)}) collective-permute-start(bf16[4,256,128]{2,1,0:T(8,128)(2,1)S(1)} %get-tuple-element.85), channel_id=1, source_target_pairs={{8,128},{16,136},{24,144},{32,152},{40,160},{48,168},{56,176},{64,... | collective-permute-start | bytes 786440 | tf_op jit(solution)/shard_map/ppermute | solution.py:409
  114.4 1.9 %collective-permute-start.17 = (bf16[4,256,128]{2,1,0:T(8,128)(2,1)S(1)}, bf16[4,256,128]{2,1,0:T(8,128)(2,1)S(1)}, u32[]{:S(2)}, u32[]{:S(2)}) collective-permute-start(bf16[4,256,128]{2,1,0:T(8,128)(2,1)S(1)} %get-tuple-element.81), channel_id=1, source_target_pairs={{0,8},{8,16},{16,24},{24,32},{32,40},{40,48},{48,56},{56,64},{64,7... | collective-permute-start | bytes 786440 | tf_op jit(solution)/shard_map/ppermute | solution.py:405
  116.3 5.9 %collective-permute-done.13.refs_1_ = bf16[4,384,128]{2,1,0:T(8,128)(2,1)S(1)} collective-permute-done((bf16[4,384,128]{2,1,0:T(8,128)(2,1)S(1)}, bf16[4,384,128]{2,1,0:T(8,128)(2,1)S(1)}, u32[]{:S(2)}, u32[]{:S(2)}) %collective-permute-start.13) | collective-permute-done | bytes 393248 | tf_op jit(solution)/shard_map/ppermute | solution.py:359
  122.2 6.0 %collective-permute-start.18 = (bf16[4,256,128]{2,1,0:T(8,128)(2,1)S(1)}, bf16[4,256,128]{2,1,0:T(8,128)(2,1)S(1)}, u32[]{:S(2)}, u32[]{:S(2)}) collective-permute-start(bf16[4,256,128]{2,1,0:T(8,128)(2,1)S(1)} %get-tuple-element.82), channel_id=1, source_target_pairs={{8,0},{16,8},{24,16},{32,24},{40,32},{48,40},{56,48},{64,56},{72,6... | collective-permute-start | bytes 786440 | tf_op jit(solution)/shard_map/ppermute | solution.py:404
  128.2 0.0 collective-permute-done.21.refs_5_
  128.2 3.6 %collective-permute-done.17.refs_1_ = bf16[4,256,128]{2,1,0:T(8,128)(2,1)S(1)} collective-permute-done((bf16[4,256,128]{2,1,0:T(8,128)(2,1)S(1)}, bf16[4,256,128]{2,1,0:T(8,128)(2,1)S(1)}, u32[]{:S(2)}, u32[]{:S(2)}) %collective-permute-start.17) | collective-permute-done | bytes 262176 | tf_op jit(solution)/shard_map/ppermute | solution.py:405
  131.8 0.3 collective-permute-done.18.refs_2_
  132.1 0.0 collective-permute-done.19.refs_3_
  132.1 1.8 %merge.1 = bf16[8,512,128]{2,1,0:T(8,128)(2,1)} custom-call(s32[4]{0:T(128)S(1)} %pad_add_fusion.pos, bf16[8,256,128]{2,1,0:T(8,128)(2,1)S(1)} %get-tuple-element.80.refs_0_, bf16[4,256,128]{2,1,0:T(8,128)(2,1)S(1)} %collective-permute-done.17.refs_1_, bf16[4,256,128]{2,1,0:T(8,128)(2,1)S(1)} %collective-permute-done.18.refs_2_, ...), custom_call_target="tpu_custom_call" | custom-call | bytes 2097152 | tf_op jit(solution)/shard_map/merge/pallas_call | solution.py:221
  133.9 7.3 %all-to-all-start = ((bf16[8,512,128]{2,1,0:T(8,128)(2,1)}), bf16[8,512,128]{2,1,0:T(8,128)(2,1)S(1)}, u32[]{:S(2)}, u32[]{:S(2)}) async-start(bf16[8,512,128]{2,1,0:T(8,128)(2,1)} %merge.1), calls=%async_computation | async-start | bytes 2097152 | tf_op jit(solution)/shard_map/all_to_all | solution.py:370
  141.2 0.6 join.5
  141.8 2.1 %collective-permute-start.14 = (bf16[2,384,128]{2,1,0:T(8,128)(2,1)S(1)}, bf16[2,384,128]{2,1,0:T(8,128)(2,1)S(1)}, u32[]{:S(2)}, u32[]{:S(2)}) collective-permute-start(bf16[2,384,128]{2,1,0:T(8,128)(2,1)S(1)} %get-tuple-element.75), channel_id=1, source_target_pairs={{0,2},{1,3},{2,4},{3,5},{4,6},{5,7},{6,0},{7,1},{8,10},{9,11},{10,... | collective-permute-start | bytes 589832 | tf_op jit(solution)/shard_map/ppermute | solution.py:365
  143.9 2.7 %collective-permute-start.15 = (bf16[2,384,128]{2,1,0:T(8,128)(2,1)S(1)}, bf16[2,384,128]{2,1,0:T(8,128)(2,1)S(1)}, u32[]{:S(2)}, u32[]{:S(2)}) collective-permute-start(bf16[2,384,128]{2,1,0:T(8,128)(2,1)S(1)} %get-tuple-element.76), channel_id=1, source_target_pairs={{0,4},{1,5},{2,6},{3,7},{4,0},{5,1},{6,2},{7,3},{8,12},{9,13},{10,... | collective-permute-start | bytes 589832 | tf_op jit(solution)/shard_map/ppermute | solution.py:365
  146.6 1.5 collective-permute-start.16
  148.0 7.7 %collective-permute-done.14.refs_1_ = bf16[2,384,128]{2,1,0:T(8,128)(2,1)S(1)} collective-permute-done((bf16[2,384,128]{2,1,0:T(8,128)(2,1)S(1)}, bf16[2,384,128]{2,1,0:T(8,128)(2,1)S(1)}, u32[]{:S(2)}, u32[]{:S(2)}) %collective-permute-start.14) | collective-permute-done | bytes 196640 | tf_op jit(solution)/shard_map/ppermute | solution.py:365
  155.8 2.5 %collective-permute-done.15.refs_2_ = bf16[2,384,128]{2,1,0:T(8,128)(2,1)S(1)} collective-permute-done((bf16[2,384,128]{2,1,0:T(8,128)(2,1)S(1)}, bf16[2,384,128]{2,1,0:T(8,128)(2,1)S(1)}, u32[]{:S(2)}, u32[]{:S(2)}) %collective-permute-start.15) | collective-permute-done | bytes 196640 | tf_op jit(solution)/shard_map/ppermute | solution.py:365
  158.3 1.6 unpack_parts.1
  159.9 10.6 %all-to-all-done.got = bf16[8,512,128]{2,1,0:T(8,128)(2,1)S(1)} async-done(((bf16[8,512,128]{2,1,0:T(8,128)(2,1)}), bf16[8,512,128]{2,1,0:T(8,128)(2,1)S(1)}, u32[]{:S(2)}, u32[]{:S(2)}) %all-to-all-start) | async-done | bytes 1048608 | tf_op jit(solution)/shard_map/all_to_all | solution.py:370
  170.5 1.8 %unpack.1 = (bf16[1,128,1024]{2,1,0:T(8,128)(2,1)}, bf16[1,128,1024]{2,1,0:T(8,128)(2,1)}, bf16[1,128,1024]{2,1,0:T(8,128)(2,1)}, bf16[1,128,1024]{2,1,0:T(8,128)(2,1)}) custom-call(s32[4]{0:T(128)S(1)} %pad_add_fusion.pos, bf16[8,512,128]{2,1,0:T(8,128)(2,1)S(1)} %all-to-all-done.got), custom_call_target="tpu_custom_call" | custom-call | bytes 2097152 | tf_op jit(solution)/shard_map/unpack/pallas_call | solution.py:221
  (12 shorter events, 0.0 us)
Async XLA Ops:
  0.6 12.2 %collective-permute-start.1 = (bf16[1,128,1024]{2,1,0:T(8,128)(2,1)}, bf16[1,128,1024]{2,1,0:T(8,128)(2,1)S(1)}, u32[]{:S(2)}, u32[]{:S(2)}) collective-permute-start(bf16[1,128,1024]{2,1,0:T(8,128)(2,1)} %param.13), channel_id=1, source_target_pairs={{0,128},{128,0},{1,129},{129,1},{2,130},{130,2},{3,131},{131,3},{4... | collective-permute-start | bytes 786440 | tf_op jit(solution)/shard_map/ppermute | solution.py:389
  0.7 12.1 %collective-permute-start.2 = (bf16[1,128,1024]{2,1,0:T(8,128)(2,1)}, bf16[1,128,1024]{2,1,0:T(8,128)(2,1)S(1)}, u32[]{:S(2)}, u32[]{:S(2)}) collective-permute-start(bf16[1,128,1024]{2,1,0:T(8,128)(2,1)} %param.14), channel_id=1, source_target_pairs={{0,128},{128,0},{1,129},{129,1},{2,130},{130,2},{3,131},{131,3},{4... | collective-permute-start | bytes 786440 | tf_op jit(solution)/shard_map/ppermute | solution.py:390
  1.2 0.7 copy-start.6
  3.1 0.7 copy-start.5
  3.8 0.9 copy-start
  4.8 0.9 copy-start.1
  6.4 23.4 %collective-permute-start = (bf16[4,272,128]{2,1,0:T(8,128)(2,1)S(1)}, bf16[4,272,128]{2,1,0:T(8,128)(2,1)S(1)}, u32[]{:S(2)}, u32[]{:S(2)}) collective-permute-start(bf16[4,272,128]{2,1,0:T(8,128)(2,1)S(1)} %get-tuple-element.50), channel_id=1, source_target_pairs={{0,1},{1,0},{2,3},{3,2},{4,5},{5,4},{6,7},{7,6},{8,9},{9,8},{10,11... | collective-permute-start | bytes 835592 | tf_op jit(solution)/shard_map/ppermute | solution.py:359
  13.5 23.6 %collective-permute-start.3 = (bf16[4,256,128]{2,1,0:T(8,128)(2,1)S(1)}, bf16[4,256,128]{2,1,0:T(8,128)(2,1)S(1)}, u32[]{:S(2)}, u32[]{:S(2)}) collective-permute-start(bf16[4,256,128]{2,1,0:T(8,128)(2,1)S(1)} %get-tuple-element.53), channel_id=1, source_target_pairs={{0,1},{1,0},{2,3},{3,2},{4,5},{5,4},{6,7},{7,6},{8,9},{9,8},{10,11... | collective-permute-start | bytes 786440 | tf_op jit(solution)/shard_map/ppermute | solution.py:359
  37.1 6.5 %copy-start.2 = (bf16[1,128,1024]{2,1,0:T(8,128)(2,1)S(1)}, bf16[1,128,1024]{2,1,0:T(8,128)(2,1)}, u32[]{:S(2)}) copy-start(bf16[1,128,1024]{2,1,0:T(8,128)(2,1)} %refs_0_.2) | copy-start | bytes 786436
  37.1 6.5 %copy-start.3 = (bf16[1,128,1024]{2,1,0:T(8,128)(2,1)S(1)}, bf16[1,128,1024]{2,1,0:T(8,128)(2,1)}, u32[]{:S(2)}) copy-start(bf16[1,128,1024]{2,1,0:T(8,128)(2,1)} %refs_1_.3) | copy-start | bytes 786436
  37.1 6.5 %copy-start.4 = (bf16[1,128,1024]{2,1,0:T(8,128)(2,1)S(1)}, bf16[1,128,1024]{2,1,0:T(8,128)(2,1)}, u32[]{:S(2)}) copy-start(bf16[1,128,1024]{2,1,0:T(8,128)(2,1)} %refs_2_.3) | copy-start | bytes 786436
  37.7 12.3 %collective-permute-start.4 = (bf16[2,528,128]{2,1,0:T(8,128)(2,1)S(1)}, bf16[2,528,128]{2,1,0:T(8,128)(2,1)S(1)}, u32[]{:S(2)}, u32[]{:S(2)}) collective-permute-start(bf16[2,528,128]{2,1,0:T(8,128)(2,1)S(1)} %get-tuple-element.55), channel_id=1, source_target_pairs={{0,2},{1,3},{2,4},{3,5},{4,6},{5,7},{6,0},{7,1},{8,10},{9,11},{10,... | collective-permute-start | bytes 811016 | tf_op jit(solution)/shard_map/ppermute | solution.py:365
  39.3 14.5 %collective-permute-start.5 = (bf16[2,528,128]{2,1,0:T(8,128)(2,1)S(1)}, bf16[2,528,128]{2,1,0:T(8,128)(2,1)S(1)}, u32[]{:S(2)}, u32[]{:S(2)}) collective-permute-start(bf16[2,528,128]{2,1,0:T(8,128)(2,1)S(1)} %get-tuple-element.56), channel_id=1, source_target_pairs={{0,4},{1,5},{2,6},{3,7},{4,0},{5,1},{6,2},{7,3},{8,12},{9,13},{10,... | collective-permute-start | bytes 811016 | tf_op jit(solution)/shard_map/ppermute | solution.py:365
  42.2 11.6 %collective-permute-start.6 = (bf16[2,528,128]{2,1,0:T(8,128)(2,1)S(1)}, bf16[2,528,128]{2,1,0:T(8,128)(2,1)S(1)}, u32[]{:S(2)}, u32[]{:S(2)}) collective-permute-start(bf16[2,528,128]{2,1,0:T(8,128)(2,1)S(1)} %get-tuple-element.57), channel_id=1, source_target_pairs={{0,6},{1,7},{2,0},{3,1},{4,2},{5,3},{6,4},{7,5},{8,14},{9,15},{10,... | collective-permute-start | bytes 811016 | tf_op jit(solution)/shard_map/ppermute | solution.py:365
  44.4 19.2 %collective-permute-start.9 = (bf16[4,384,128]{2,1,0:T(8,128)(2,1)S(1)}, bf16[4,384,128]{2,1,0:T(8,128)(2,1)S(1)}, u32[]{:S(2)}, u32[]{:S(2)}) collective-permute-start(bf16[4,384,128]{2,1,0:T(8,128)(2,1)S(1)} %get-tuple-element.62), channel_id=1, source_target_pairs={{0,1},{1,0},{2,3},{3,2},{4,5},{5,4},{6,7},{7,6},{8,9},{9,8},{10,11... | collective-permute-start | bytes 1179656 | tf_op jit(solution)/shard_map/ppermute | solution.py:359
  54.5 23.0 %collective-permute-start.7 = (bf16[4,528,128]{2,1,0:T(8,128)(2,1)S(1)}, bf16[4,528,128]{2,1,0:T(8,128)(2,1)S(1)}, u32[]{:S(2)}, u32[]{:S(2)}) collective-permute-start(bf16[4,528,128]{2,1,0:T(8,128)(2,1)S(1)} %get-tuple-element.58.high), channel_id=1, source_target_pairs={{0,8},{8,16},{16,24},{24,32},{32,40},{40,48},{48,56},{56,64},{64,7... | collective-permute-start | bytes 1622024 | tf_op jit(solution)/shard_map/ppermute | solution.py:399
  57.9 19.6 %collective-permute-start.8 = (bf16[4,528,128]{2,1,0:T(8,128)(2,1)S(1)}, bf16[4,528,128]{2,1,0:T(8,128)(2,1)S(1)}, u32[]{:S(2)}, u32[]{:S(2)}) collective-permute-start(bf16[4,528,128]{2,1,0:T(8,128)(2,1)S(1)} %get-tuple-element.59.low), channel_id=1, source_target_pairs={{8,0},{16,8},{24,16},{32,24},{40,32},{48,40},{56,48},{64,56},{72,6... | collective-permute-start | bytes 1622024 | tf_op jit(solution)/shard_map/ppermute | solution.py:400
  64.1 12.1 %collective-permute-start.10 = (bf16[2,384,128]{2,1,0:T(8,128)(2,1)S(1)}, bf16[2,384,128]{2,1,0:T(8,128)(2,1)S(1)}, u32[]{:S(2)}, u32[]{:S(2)}) collective-permute-start(bf16[2,384,128]{2,1,0:T(8,128)(2,1)S(1)} %get-tuple-element.64), channel_id=1, source_target_pairs={{0,2},{1,3},{2,4},{3,5},{4,6},{5,7},{6,0},{7,1},{8,10},{9,11},{10,... | collective-permute-start | bytes 589832 | tf_op jit(solution)/shard_map/ppermute | solution.py:365
  64.8 11.5 %collective-permute-start.11 = (bf16[2,384,128]{2,1,0:T(8,128)(2,1)S(1)}, bf16[2,384,128]{2,1,0:T(8,128)(2,1)S(1)}, u32[]{:S(2)}, u32[]{:S(2)}) collective-permute-start(bf16[2,384,128]{2,1,0:T(8,128)(2,1)S(1)} %get-tuple-element.65), channel_id=1, source_target_pairs={{0,4},{1,5},{2,6},{3,7},{4,0},{5,1},{6,2},{7,3},{8,12},{9,13},{10,... | collective-permute-start | bytes 589832 | tf_op jit(solution)/shard_map/ppermute | solution.py:365
  66.8 10.1 %collective-permute-start.12 = (bf16[2,384,128]{2,1,0:T(8,128)(2,1)S(1)}, bf16[2,384,128]{2,1,0:T(8,128)(2,1)S(1)}, u32[]{:S(2)}, u32[]{:S(2)}) collective-permute-start(bf16[2,384,128]{2,1,0:T(8,128)(2,1)S(1)} %get-tuple-element.66), channel_id=1, source_target_pairs={{0,6},{1,7},{2,0},{3,1},{4,2},{5,3},{6,4},{7,5},{8,14},{9,15},{10,... | collective-permute-start | bytes 589832 | tf_op jit(solution)/shard_map/ppermute | solution.py:365
  101.2 21.0 %collective-permute-start.13 = (bf16[4,384,128]{2,1,0:T(8,128)(2,1)S(1)}, bf16[4,384,128]{2,1,0:T(8,128)(2,1)S(1)}, u32[]{:S(2)}, u32[]{:S(2)}) collective-permute-start(bf16[4,384,128]{2,1,0:T(8,128)(2,1)S(1)} %get-tuple-element.71), channel_id=1, source_target_pairs={{0,1},{1,0},{2,3},{3,2},{4,5},{5,4},{6,7},{7,6},{8,9},{9,8},{10,11... | collective-permute-start | bytes 1179656 | tf_op jit(solution)/shard_map/ppermute | solution.py:359
  106.7 25.4 %collective-permute-start.19 = (bf16[8,256,128]{2,1,0:T(8,128)(2,1)S(1)}, bf16[8,256,128]{2,1,0:T(8,128)(2,1)S(1)}, u32[]{:S(2)}, u32[]{:S(2)}) collective-permute-start(bf16[8,256,128]{2,1,0:T(8,128)(2,1)S(1)} %get-tuple-element.83), channel_id=1, source_target_pairs={{0,128},{128,0},{1,129},{129,1},{2,130},{130,2},{3,131},{131,3},{4... | collective-permute-start | bytes 1572872 | tf_op jit(solution)/shard_map/ppermute | solution.py:411
  106.7 21.5 %collective-permute-start.20 = (bf16[4,256,128]{2,1,0:T(8,128)(2,1)S(1)}, bf16[4,256,128]{2,1,0:T(8,128)(2,1)S(1)}, u32[]{:S(2)}, u32[]{:S(2)}) collective-permute-start(bf16[4,256,128]{2,1,0:T(8,128)(2,1)S(1)} %get-tuple-element.84), channel_id=1, source_target_pairs={{0,136},{8,144},{16,152},{24,160},{32,168},{40,176},{48,184},{56,1... | collective-permute-start | bytes 786440 | tf_op jit(solution)/shard_map/ppermute | solution.py:410
  110.2 18.0 %collective-permute-start.21 = (bf16[4,256,128]{2,1,0:T(8,128)(2,1)S(1)}, bf16[4,256,128]{2,1,0:T(8,128)(2,1)S(1)}, u32[]{:S(2)}, u32[]{:S(2)}) collective-permute-start(bf16[4,256,128]{2,1,0:T(8,128)(2,1)S(1)} %get-tuple-element.85), channel_id=1, source_target_pairs={{8,128},{16,136},{24,144},{32,152},{40,160},{48,168},{56,176},{64,... | collective-permute-start | bytes 786440 | tf_op jit(solution)/shard_map/ppermute | solution.py:409
  114.4 17.5 %collective-permute-start.17 = (bf16[4,256,128]{2,1,0:T(8,128)(2,1)S(1)}, bf16[4,256,128]{2,1,0:T(8,128)(2,1)S(1)}, u32[]{:S(2)}, u32[]{:S(2)}) collective-permute-start(bf16[4,256,128]{2,1,0:T(8,128)(2,1)S(1)} %get-tuple-element.81), channel_id=1, source_target_pairs={{0,8},{8,16},{16,24},{24,32},{32,40},{40,48},{48,56},{56,64},{64,7... | collective-permute-start | bytes 786440 | tf_op jit(solution)/shard_map/ppermute | solution.py:405
  122.2 9.9 %collective-permute-start.18 = (bf16[4,256,128]{2,1,0:T(8,128)(2,1)S(1)}, bf16[4,256,128]{2,1,0:T(8,128)(2,1)S(1)}, u32[]{:S(2)}, u32[]{:S(2)}) collective-permute-start(bf16[4,256,128]{2,1,0:T(8,128)(2,1)S(1)} %get-tuple-element.82), channel_id=1, source_target_pairs={{8,0},{16,8},{24,16},{32,24},{40,32},{48,40},{56,48},{64,56},{72,6... | collective-permute-start | bytes 786440 | tf_op jit(solution)/shard_map/ppermute | solution.py:404
  133.9 36.6 %all-to-all-start = ((bf16[8,512,128]{2,1,0:T(8,128)(2,1)}), bf16[8,512,128]{2,1,0:T(8,128)(2,1)S(1)}, u32[]{:S(2)}, u32[]{:S(2)}) async-start(bf16[8,512,128]{2,1,0:T(8,128)(2,1)} %merge.1), calls=%async_computation | async-start | bytes 2097152 | tf_op jit(solution)/shard_map/all_to_all | solution.py:370
  141.8 14.0 %collective-permute-start.14 = (bf16[2,384,128]{2,1,0:T(8,128)(2,1)S(1)}, bf16[2,384,128]{2,1,0:T(8,128)(2,1)S(1)}, u32[]{:S(2)}, u32[]{:S(2)}) collective-permute-start(bf16[2,384,128]{2,1,0:T(8,128)(2,1)S(1)} %get-tuple-element.75), channel_id=1, source_target_pairs={{0,2},{1,3},{2,4},{3,5},{4,6},{5,7},{6,0},{7,1},{8,10},{9,11},{10,... | collective-permute-start | bytes 589832 | tf_op jit(solution)/shard_map/ppermute | solution.py:365
  143.9 14.4 %collective-permute-start.15 = (bf16[2,384,128]{2,1,0:T(8,128)(2,1)S(1)}, bf16[2,384,128]{2,1,0:T(8,128)(2,1)S(1)}, u32[]{:S(2)}, u32[]{:S(2)}) collective-permute-start(bf16[2,384,128]{2,1,0:T(8,128)(2,1)S(1)} %get-tuple-element.76), channel_id=1, source_target_pairs={{0,4},{1,5},{2,6},{3,7},{4,0},{5,1},{6,2},{7,3},{8,12},{9,13},{10,... | collective-permute-start | bytes 589832 | tf_op jit(solution)/shard_map/ppermute | solution.py:365
  146.6 11.7 %collective-permute-start.16 = (bf16[2,384,128]{2,1,0:T(8,128)(2,1)S(1)}, bf16[2,384,128]{2,1,0:T(8,128)(2,1)S(1)}, u32[]{:S(2)}, u32[]{:S(2)}) collective-permute-start(bf16[2,384,128]{2,1,0:T(8,128)(2,1)S(1)} %get-tuple-element.77), channel_id=1, source_target_pairs={{0,6},{1,7},{2,0},{3,1},{4,2},{5,3},{6,4},{7,5},{8,14},{9,15},{10,... | collective-permute-start | bytes 589832 | tf_op jit(solution)/shard_map/ppermute | solution.py:365

commit v3 on v2

--- a/solution.py
+++ b/solution.py
@@ -124,7 +124,7 @@
         to_hi[:, rows, :] = acc[HALF + BLOCK : EXT, :].astype(BF16).reshape(4, CHUNK, CHUNK)
 
 
-def self_kernel(before, low, high, after, asks, out_t, pay, back, to_lo, to_hi, kx, kt, v, vt, gt, s, e, ds, dk, dv):
+def self_kernel(before, low, high, after, asks, out_t, gt, pay, back, to_lo, to_hi, kx, kt, v, vt, s, e, ds, dk, dv):
     refs = (before, low, high, after)
     bias = jnp.where(validity(refs, 0) > 0.5, 0.0, NEG)
     stage_keys(piece(refs, VROWS), piece(refs, VROWS + CHUNK), bias, kx, kt, v, vt)
@@ -146,15 +146,13 @@
     emit_sums(dk, dv, back, to_lo, to_hi)
 
 
-def cross_kernel(pos, before, low, high, after, asks, out_t, pay, back, to_lo, to_hi, kx, kt, v, vt, gt, s, e, ds, dk, dv):
-    first = pos[2]
+def cross_kernel(band, vb, vl, vh, va, before, low, high, after, asks, out_t, gt, pay, back, to_lo, to_hi, kx, kt, v, vt, s, e, ds, dk, dv):
+    first = band[0]
     place = lax.broadcasted_iota(jnp.int32, (16, CHUNK), 0) * CHUNK + lax.broadcasted_iota(jnp.int32, (16, CHUNK), 1)
     inside = (place >= first) & (place < first + BLOCK)
     refs = (before, low, high, after)
-    bias = jnp.where(inside & (validity(refs, 1) > 0.5), 0.0, NEG)
-    stage_keys(piece(refs, VROWS + 2 * CHUNK), piece(refs, VROWS + 3 * CHUNK), bias, kx, kt, v, vt)
-    for c in range(8):
-        gt[:, c * CHUNK : (c + 1) * CHUNK] = flipped(asks[c, CHUNK : 2 * CHUNK, :])
+    bias = jnp.where(inside & (validity((vb, vl, vh, va), 1) > 0.5), 0.0, NEG)
+    stage_keys(piece(refs, 0), piece(refs, CHUNK), bias, kx, kt, v, vt)
     dk[...] = jnp.zeros_like(dk)
     dv[...] = jnp.zeros_like(dv)
     start = pl.multiple_of(lax.shift_right_logical(first, 7) * CHUNK, CHUNK)
@@ -178,7 +176,6 @@
         pltpu.VMEM((CHUNK, EXT), BF16),
         pltpu.VMEM((EXT, CHUNK), BF16),
         pltpu.VMEM((CHUNK, EXT), BF16),
-        pltpu.VMEM((CHUNK, BLOCK), BF16),
         pltpu.VMEM((2, width, QROWS), F32),
         pltpu.VMEM((width, 2 * QROWS), BF16),
         pltpu.VMEM((width, 2 * QROWS), BF16),
@@ -207,7 +204,7 @@
 
 
 def run_self(*operands):
-    outs = (shaped((CHUNK, BLOCK), F32), shaped((8, CHUNK, CHUNK)))
+    outs = (shaped((CHUNK, BLOCK), F32), shaped((CHUNK, BLOCK)), shaped((8, CHUNK, CHUNK)))
     return run_attention(self_kernel, "self_attention", SELF_WIN, operands, outs)
 
 
@@ -229,30 +226,50 @@
     )(pos, *operands)
 
 
-def pack_kernel(marked, count, pos, *refs):
-    rows, outs = refs[:count], refs[count:]
-    at = 0
-    if marked:
-        valid = rows[0][...].astype(F32)
-        own = jnp.where(pos[3] == 0, valid[0:1], valid[1:2])
-        other = jnp.where(pos[3] == 0, valid[1:2], valid[0:1])
-        marks = jnp.concatenate([own, other, jnp.zeros((VROWS - 2, CHUNK), F32)], axis=0).astype(BF16)
-        for out in outs:
-            for d in range(4):
-                out[d, 0:VROWS, :] = marks
-        at, rows = VROWS, rows[1:]
-    for n, ref in enumerate(rows):
-        spot = slice(at + n * CHUNK, at + (n + 1) * CHUNK)
-        for out, z in zip(outs, (pos[1], 1 - pos[1])):
-            for d in range(4):
-                first = pl.multiple_of((2 * lax.rem(pos[0] + d, 4) + z) * CHUNK, CHUNK)
-                out[d, spot, :] = ref[0, :, pl.ds(first, CHUNK)]
-
-
-def pack(pos, *rows, marked=False):
-    height = (len(rows) - 1) * CHUNK + VROWS if marked else len(rows) * CHUNK
-    kernel = functools.partial(pack_kernel, marked, len(rows))
-    return small_call(kernel, "pack", pos, rows, (shaped((4, height, CHUNK)),) * 2)
+def column_pieces(pos, ref, keep, send, spot):
+    for out, z in ((keep, pos[1]), (send, 1 - pos[1])):
+        for d in range(4):
+            first = pl.multiple_of((2 * lax.rem(pos[0] + d, 4) + z) * CHUNK, CHUNK)
+            out[d, spot, :] = ref[0, :, pl.ds(first, CHUNK)]
+
+
+def pack_kernel(pos, *refs):
+    for n, ref in enumerate(refs[:-2]):
+        column_pieces(pos, ref, *refs[-2:], slice(n * CHUNK, (n + 1) * CHUNK))
+
+
+def pack(pos, *rows):
+    return small_call(pack_kernel, "pack", pos, rows, (shaped((4, len(rows) * CHUNK, CHUNK)),) * 2)
+
+
+def pack_marked_kernel(pos, key_valid, keys, values, keep, send, held_k, held_v, sems):
+    copies = [pltpu.make_async_copy(keys, held_k, sems.at[0]), pltpu.make_async_copy(values, held_v, sems.at[1])]
+    for copy in copies:
+        copy.start()
+    valid = key_valid[...].astype(F32)
+    own = jnp.where(pos[2] == 0, valid[0:1], valid[1:2])
+    other = jnp.where(pos[2] == 0, valid[1:2], valid[0:1])
+    marks = jnp.concatenate([own, other, jnp.zeros((VROWS - 2, CHUNK), F32)], axis=0).astype(BF16)
+    for out in (keep, send):
+        for d in range(4):
+            out[d, 0:VROWS, :] = marks
+    for n, (copy, held) in enumerate(zip(copies, (held_k, held_v))):
+        copy.wait()
+        column_pieces(pos, held, keep, send, slice(VROWS + n * CHUNK, VROWS + (n + 1) * CHUNK))
+
+
+def pack_marked(pos, key_valid, keys, values):
+    vmem = pl.BlockSpec(memory_space=pltpu.VMEM)
+    whole_hbm = pl.BlockSpec(memory_space=pl.ANY)
+    return pl.pallas_call(
+        pack_marked_kernel,
+        out_shape=(shaped((4, VROWS + 2 * CHUNK, CHUNK)),) * 2,
+        in_specs=[pl.BlockSpec(memory_space=pltpu.SMEM), vmem, whole_hbm, whole_hbm],
+        out_specs=[vmem] * 2,
+        scratch_shapes=[pltpu.VMEM(keys.shape, BF16), pltpu.VMEM(values.shape, BF16), pltpu.SemaphoreType.DMA((2,))],
+        cost_estimate=pl.CostEstimate(flops=0, bytes_accessed=2**21, transcendentals=0),
+        name="pack_marked",
+    )(pos, key_valid, keys, values)
 
 
 def join_kernel(pos, *refs):
@@ -289,13 +306,40 @@
     return small_call(halves_kernel, "halves", pos, parts, (shaped((4,) + parts[0].shape[1:]),) * 2)
 
 
-def whole_kernel(pos, *refs):
+def pack_y_kernel(pos, *refs):
+    rows, outs = refs[:-4], refs[-4:]
+    for n, ref in enumerate(rows):
+        for d in range(4):
+            first = pl.multiple_of(2 * lax.rem(pos[0] + d, 4) * CHUNK, 2 * CHUNK)
+            pair = ref[0, :, pl.ds(first, 2 * CHUNK)]
+            outs[d][0, n * CHUNK : (n + 1) * CHUNK, :] = pair[:, 0:CHUNK]
+            outs[d][1, n * CHUNK : (n + 1) * CHUNK, :] = pair[:, CHUNK:]
+
+
+def pack_y(pos, *rows):
+    return small_call(pack_y_kernel, "pack_y", pos, rows, (shaped((2, len(rows) * CHUNK, CHUNK)),) * 4)
+
+
+def split_kernel(pos, *refs):
+    keep, send = refs[4:]
     for d in range(4):
-        refs[-1][pl.ds(2 * lax.rem(pos[0] - d + 4, 4), 2)] = refs[d][...]
-
-
-def whole(pos, parts):
-    return small_call(whole_kernel, "whole", pos, parts, (shaped((8,) + parts[0].shape[1:]),))[0]
+        keep[d] = refs[d][pl.ds(pos[1], 1)][0]
+        send[d] = refs[d][pl.ds(1 - pos[1], 1)][0]
+
+
+def split(pos, parts):
+    return small_call(split_kernel, "split", pos, parts, (shaped((4,) + parts[0].shape[1:]),) * 2)
+
+
+def whole_kernel(pos, keep, got, out):
+    for d in range(4):
+        at = 2 * lax.rem(pos[0] - d + 4, 4)
+        out[pl.ds(at + pos[1], 1)] = keep[d][None]
+        out[pl.ds(at + 1 - pos[1], 1)] = got[d][None]
+
+
+def whole(pos, keep, got):
+    return small_call(whole_kernel, "whole", pos, (keep, got), (shaped((8,) + keep.shape[1:]),))[0]
 
 
 def unpack_kernel(pos, got, *outs):
@@ -382,28 +426,32 @@
     both = ("tower", "blk")
 
     seq_id = lax.axis_index("seq")
-    band = HALF + offsets[tower_id, block_id]
-    pos = jnp.stack([seq_id // 2, seq_id % 2, band, tower_id]).astype(jnp.int32)
-
+    pos = jnp.stack([seq_id // 2, seq_id % 2, tower_id]).astype(jnp.int32)
+    band = (HALF + offsets[tower_id, block_id]).reshape(1)
     hold = lax.optimization_barrier
     swapped_k = lax.ppermute(cross_keys, "tower", swap)
     swapped_v = lax.ppermute(cross_values, "tower", swap)
-    keep_a, send_a = pack(pos, key_valid, key_rows, value_rows, marked=True)
+    keep_a, send_a = pack_marked(pos, key_valid, key_rows, value_rows)
     got_a = across_z(send_a)
     keep_c, send_c = pack(pos, swapped_k, swapped_v)
-    queries, send_c = hold((queries, send_c))
     got_c = across_z(send_c)
-    keep_b, send_b = pack(pos, queries, grad_out, cross_queries)
+    keep_b, send_b = split(pos, along_y(pack_y(pos, queries, grad_out, cross_queries)))
     got_b = across_z(send_b)
-    low, high = halves(pos, along_y(join(pos, keep_a, got_a, keep_c, got_c)))
+    low, high = halves(pos, along_y(join(pos, keep_a, got_a)))
     before = lax.ppermute(high, "blk", up)
     after = lax.ppermute(low, "blk", down)
-    asks = whole(pos, along_y(join(pos, keep_b, got_b)))
-
-    out_t, pay_q, center, to_lo, to_hi = run_self(before, low, high, after, asks)
+    c_low, c_high = halves(pos, along_y(join(pos, keep_c, got_c)))
+    got_b, c_low, c_high = hold((got_b, c_low, c_high))
+    c_before = lax.ppermute(c_high, "blk", up)
+    c_after = lax.ppermute(c_low, "blk", down)
+    asks = whole(pos, keep_b, got_b)
+
+    out_t, turned, pay_q, center, to_lo, to_hi = run_self(before, low, high, after, asks)
     above = lax.ppermute(to_lo, "blk", down)
     below = lax.ppermute(to_hi, "blk", up)
-    pay_x, back, c_lo, c_hi = run_cross(pos, before, low, high, after, asks, out_t)
+    pay_x, back, c_lo, c_hi = run_cross(
+        band, before, low, high, after, c_before, c_low, c_high, c_after, asks, out_t, turned
+    )
     keep_p, send_p = order(pos, pay_q, pay_x)
     got_p = across_z(send_p)
     c_above = lax.ppermute(c_lo, both, over_down)

time: 173 us -> 162 us (0.936)
  waiting for transfers between devices: 67.6 us -> 50.4 us
  starting transfers between devices: 65.4 us -> 70.6 us
  Pallas kernels: 33.9 us -> 36.3 us
    ppermute x4, waiting for transfers between devices: 30.4 us -> 11.8 us  [across_z(): return lax.ppermute(send, 'seq', [(i, i ^ 1) for i in range(size)])]
    ppermute x0 -> x2, starting transfers between devices: none -> 8.13 us  [the longest x1 6.21 us: shards(): c_after = lax.ppermute(c_low, 'blk', down)]
    ppermute x9 -> x12, starting transfers between devices: 16.4 us -> 22 us  [along_y(): lax.ppermute(parts[d], 'seq', [(i, (i + 2 * d) % size) for i in range(siz...]
    ppermute x1, waiting for transfers between devices: 0.01 us -> 3.22 us  [shards(): c_above = lax.ppermute(c_lo, both, over_down)]
    ppermute x4, starting transfers between devices: 17.6 us -> 14.7 us  [across_z(): return lax.ppermute(send, 'seq', [(i, i ^ 1) for i in range(size)])]
    pallas_call x0 -> x1, Pallas kernels: none -> 2.72 us  [pack_marked(): pl.pallas_call(pack_marked_kernel, out_shape=(shaped((4, VROWS + 2 * CHUN...]
    ppermute x1, starting transfers between devices: 4.16 us -> 1.91 us  [shards(): c_above = lax.ppermute(c_lo, both, over_down)]
    all_to_all x1, starting transfers between devices: 7.31 us -> 5.41 us  [exchange(): lax.all_to_all(packed, 'seq', split_axis=0, concat_axis=0, tiled=True)]
  transfers between devices with their start and end apart: 23 -> 28, of which waited for: 12 -> 9; matrix products, arithmetic and copies ran while one was open for 0% -> 1% of each run, Pallas kernels for 4% -> 13%
where the time goes in v3:
time: 162 us
  starting transfers between devices  70.6 us (44%)
  waiting for transfers between devices  50.4 us (31%)
  Pallas kernels  36.3 us (22%)
  local copies, waits for them, and re-layouts  2.23 us (1%)
    pallas_call x2, Pallas kernels, run_attention(): pl.pallas_call(kernel, out_shape=outs, in_specs=[pl.BlockSpec(memory_spac...  22.2 us
    ppermute x12, starting transfers between devices, along_y(): lax.ppermute(parts[d], 'seq', [(i, (i + 2 * d) % size) for i in range(siz...  22 us
    ppermute x12, waiting for transfers between devices, along_y(): lax.ppermute(parts[d], 'seq', [(i, (i + 2 * d) % size) for i in range(siz...  20.8 us
    ppermute x4, starting transfers between devices, across_z(): return lax.ppermute(send, 'seq', [(i, i ^ 1) for i in range(size)])  14.7 us
    ppermute x4, waiting for transfers between devices, across_z(): return lax.ppermute(send, 'seq', [(i, i ^ 1) for i in range(size)])  11.8 us
    pallas_call x13, Pallas kernels, small_call(): pl.pallas_call(kernel, out_shape=outs, in_specs=[pl.BlockSpec(memory_spac...  11.3 us
    all_to_all x1, waiting for transfers between devices, exchange(): lax.all_to_all(packed, 'seq', split_axis=0, concat_axis=0, tiled=True)  11.3 us
    ppermute x1, starting transfers between devices, shards(): c_after = lax.ppermute(c_low, 'blk', down)  6.21 us
  transfers between devices with their start and end apart: 28, of which 9 were waited for; matrix products, arithmetic and copies ran while one was open for 1% of the time, Pallas kernels for 13%

profile of v3, /device:TPU:32, one launch (start us, length us, event | category | flops | bytes accessed | tf_op | source)
XLA Modules:
  0.0 161.7 jit_solution(17799662703716083813)
XLA Ops:
  0.6 0.1 collective-permute-start.10
  0.7 0.5 collective-permute-start.11
  1.2 0.6 pad_add_fusion.pos
  1.8 2.7 %pack_marked.1 = (bf16[4,272,128]{2,1,0:T(8,128)(2,1)}, bf16[4,272,128]{2,1,0:T(8,128)(2,1)}) custom-call(s32[3]{0:T(128)} %pad_add_fusion.pos, s32[2,128]{1,0:T(2,128)} %key_valid.1, bf16[1,128,1024]{2,1,0:T(8,128)(2,1)} %keys.1, bf16[1,128,1024]{2,1,0:T(8,128)(2,1)} %values.1), custom_call_target="tpu_custom_call" | custom-call | bytes 2097152 | tf_op jit(solution)/shard_map/pack_marked/pallas_call | solution.py:264
  4.6 0.0 copy-start.4
  4.6 6.4 %collective-permute-start = (bf16[4,272,128]{2,1,0:T(8,128)(2,1)}, bf16[4,272,128]{2,1,0:T(8,128)(2,1)S(1)}, u32[]{:S(2)}, u32[]{:S(2)}) collective-permute-start(bf16[4,272,128]{2,1,0:T(8,128)(2,1)} %get-tuple-element.58), channel_id=1, source_target_pairs={{0,1},{1,0},{2,3},{3,2},{4,5},{5,4},{6,7},{7,6},{8,9},{9,8},{10,11... | collective-permute-start | bytes 835592 | tf_op jit(solution)/shard_map/ppermute | solution.py:403
  11.0 0.9 copy-done.3
  11.9 0.7 pack_y.1
  12.6 1.7 %collective-permute-start.6 = (bf16[2,384,128]{2,1,0:T(8,128)(2,1)S(1)}, bf16[2,384,128]{2,1,0:T(8,128)(2,1)S(1)}, u32[]{:S(2)}, u32[]{:S(2)}) collective-permute-start(bf16[2,384,128]{2,1,0:T(8,128)(2,1)S(1)} %get-tuple-element.66), channel_id=1, source_target_pairs={{0,2},{1,3},{2,4},{3,5},{4,6},{5,7},{6,0},{7,1},{8,10},{9,11},{10,... | collective-permute-start | bytes 589832 | tf_op jit(solution)/shard_map/ppermute | solution.py:409
  14.2 2.9 %collective-permute-start.7 = (bf16[2,384,128]{2,1,0:T(8,128)(2,1)S(1)}, bf16[2,384,128]{2,1,0:T(8,128)(2,1)S(1)}, u32[]{:S(2)}, u32[]{:S(2)}) collective-permute-start(bf16[2,384,128]{2,1,0:T(8,128)(2,1)S(1)} %get-tuple-element.67), channel_id=1, source_target_pairs={{0,4},{1,5},{2,6},{3,7},{4,0},{5,1},{6,2},{7,3},{8,12},{9,13},{10,... | collective-permute-start | bytes 589832 | tf_op jit(solution)/shard_map/ppermute | solution.py:409
  17.1 0.0 collective-permute-done.10.refs_0_
  17.1 1.3 collective-permute-start.8
  18.5 0.7 pack.1
  19.2 0.6 collective-permute-start.12
  19.8 5.4 %collective-permute-done.refs_1_ = bf16[4,272,128]{2,1,0:T(8,128)(2,1)S(1)} collective-permute-done((bf16[4,272,128]{2,1,0:T(8,128)(2,1)}, bf16[4,272,128]{2,1,0:T(8,128)(2,1)S(1)}, u32[]{:S(2)}, u32[]{:S(2)}) %collective-permute-start) | collective-permute-done | bytes 278560 | tf_op jit(solution)/shard_map/ppermute | solution.py:403
  25.2 0.6 join.3
  25.8 0.8 collective-permute-start.1
  26.6 6.2 %collective-permute-start.2 = (bf16[2,272,128]{2,1,0:T(8,128)(2,1)S(1)}, bf16[2,272,128]{2,1,0:T(8,128)(2,1)S(1)}, u32[]{:S(2)}, u32[]{:S(2)}) collective-permute-start(bf16[2,272,128]{2,1,0:T(8,128)(2,1)S(1)} %get-tuple-element.61), channel_id=1, source_target_pairs={{0,4},{1,5},{2,6},{3,7},{4,0},{5,1},{6,2},{7,3},{8,12},{9,13},{10,... | collective-permute-start | bytes 417800 | tf_op jit(solution)/shard_map/ppermute | solution.py:409
  32.8 1.3 collective-permute-start.3
  34.1 0.0 collective-permute-done.8.refs_3_
  34.1 0.6 split.1
  34.7 6.0 %collective-permute-start.9 = (bf16[4,384,128]{2,1,0:T(8,128)(2,1)S(1)}, bf16[4,384,128]{2,1,0:T(8,128)(2,1)S(1)}, u32[]{:S(2)}, u32[]{:S(2)}) collective-permute-start(bf16[4,384,128]{2,1,0:T(8,128)(2,1)S(1)} %get-tuple-element.70), channel_id=1, source_target_pairs={{0,1},{1,0},{2,3},{3,2},{4,5},{5,4},{6,7},{7,6},{8,9},{9,8},{10,11... | collective-permute-start | bytes 1179656 | tf_op jit(solution)/shard_map/ppermute | solution.py:403
  40.8 0.0 collective-permute-done.2.refs_2_
  40.8 0.0 collective-permute-done.3.refs_3_
  40.8 0.6 halves.2
  41.5 3.4 %collective-permute-start.4 = (bf16[4,272,128]{2,1,0:T(8,128)(2,1)S(1)}, bf16[4,272,128]{2,1,0:T(8,128)(2,1)S(1)}, u32[]{:S(2)}, u32[]{:S(2)}) collective-permute-start(bf16[4,272,128]{2,1,0:T(8,128)(2,1)S(1)} %get-tuple-element.63.high.vh), channel_id=1, source_target_pairs={{0,8},{8,16},{16,24},{24,32},{32,40},{40,48},{48,56},{56,64},{64,7... | collective-permute-start | bytes 835592 | tf_op jit(solution)/shard_map/ppermute | solution.py:441
  44.9 4.6 %collective-permute-start.5 = (bf16[4,272,128]{2,1,0:T(8,128)(2,1)S(1)}, bf16[4,272,128]{2,1,0:T(8,128)(2,1)S(1)}, u32[]{:S(2)}, u32[]{:S(2)}) collective-permute-start(bf16[4,272,128]{2,1,0:T(8,128)(2,1)S(1)} %get-tuple-element.64.low.vl), channel_id=1, source_target_pairs={{8,0},{16,8},{24,16},{32,24},{40,32},{48,40},{56,48},{64,56},{72,6... | collective-permute-start | bytes 835592 | tf_op jit(solution)/shard_map/ppermute | solution.py:442
  49.4 0.6 join.4
  50.0 0.7 collective-permute-start.13
  50.7 0.8 collective-permute-start.14
  51.6 6.1 %collective-permute-done.13.refs_1_ = bf16[2,256,128]{2,1,0:T(8,128)(2,1)S(1)} collective-permute-done((bf16[2,256,128]{2,1,0:T(8,128)(2,1)S(1)}, bf16[2,256,128]{2,1,0:T(8,128)(2,1)S(1)}, u32[]{:S(2)}, u32[]{:S(2)}) %collective-permute-start.13) | collective-permute-done | bytes 131104 | tf_op jit(solution)/shard_map/ppermute | solution.py:409
  57.7 0.0 collective-permute-start.15
  57.7 0.7 copy-done.5
  58.4 0.6 dynamic_slice.3
  59.6 0.0 collective-permute-done.14.refs_2_
  59.6 3.0 %collective-permute-done.15.refs_3_ = bf16[2,256,128]{2,1,0:T(8,128)(2,1)S(1)} collective-permute-done((bf16[2,256,128]{2,1,0:T(8,128)(2,1)S(1)}, bf16[2,256,128]{2,1,0:T(8,128)(2,1)S(1)}, u32[]{:S(2)}, u32[]{:S(2)}) %collective-permute-start.15) | collective-permute-done | bytes 131104 | tf_op jit(solution)/shard_map/ppermute | solution.py:409
  62.7 0.6 halves.3
  63.3 1.9 %collective-permute-start.16 = (bf16[4,256,128]{2,1,0:T(8,128)(2,1)S(1)}, bf16[4,256,128]{2,1,0:T(8,128)(2,1)S(1)}, u32[]{:S(2)}, u32[]{:S(2)}) collective-permute-start(bf16[4,256,128]{2,1,0:T(8,128)(2,1)S(1)} %get-tuple-element.81.high), channel_id=1, source_target_pairs={{0,8},{8,16},{16,24},{24,32},{32,40},{40,48},{48,56},{56,64},{64,7... | collective-permute-start | bytes 786440 | tf_op jit(solution)/shard_map/ppermute | solution.py:445
  65.2 6.2 %collective-permute-start.17 = (bf16[4,256,128]{2,1,0:T(8,128)(2,1)S(1)}, bf16[4,256,128]{2,1,0:T(8,128)(2,1)S(1)}, u32[]{:S(2)}, u32[]{:S(2)}) collective-permute-start(bf16[4,256,128]{2,1,0:T(8,128)(2,1)S(1)} %get-tuple-element.82.low), channel_id=1, source_target_pairs={{8,0},{16,8},{24,16},{32,24},{40,32},{48,40},{56,48},{64,56},{72,6... | collective-permute-start | bytes 786440 | tf_op jit(solution)/shard_map/ppermute | solution.py:446
  71.4 0.6 whole.1.asks
  72.1 0.0 collective-permute-done.5.after.va
  72.1 11.6 %self_attention.1 = (f32[128,1024]{1,0:T(8,128)S(1)}, bf16[128,1024]{1,0:T(8,128)(2,1)S(1)}, bf16[8,128,128]{2,1,0:T(8,128)(2,1)S(1)}, bf16[8,256,128]{2,1,0:T(8...) custom-call(bf16[4,272,128]{2,1,0:T(8,128)(2,1)S(1)} %collective-permute-done.4.before.vb, ...), custom_call_target="tpu_custom_call" | custom-call | flops 8000000000 | bytes 3145728 | tf_op jit(solution)/shard_map/self_attention/pallas_call | solution.py:194
  83.7 0.0 collective-permute-done.16.before
  83.8 10.6 %cross_attention.1 = (bf16[8,256,128]{2,1,0:T(8,128)(2,1)S(1)}, bf16[8,256,128]{2,1,0:T(8,128)(2,1)S(1)}, bf16[4,256,128]{2,1,0:T(8,128)(2,1)S(1)}, bf16[4,256,128]{2,1,0:T(8,128)(2,1)S(1)}) custom-call(s32[1]{0:T(128)} %bitcast.3.band, bf16[4,272,128]{2,1,0:T(8,128)(2,1)S(1)} %collective-permute-done.4.before.vb, ...), custom_call_target="tpu_custom_call" | custom-call | flops 8000000000 | bytes 3145728 | tf_op jit(solution)/shard_map/cross_attention/pallas_call | solution.py:194
  94.4 0.6 order.1
  95.0 1.6 %collective-permute-start.18 = (bf16[4,384,128]{2,1,0:T(8,128)(2,1)S(1)}, bf16[4,384,128]{2,1,0:T(8,128)(2,1)S(1)}, u32[]{:S(2)}, u32[]{:S(2)}) collective-permute-start(bf16[4,384,128]{2,1,0:T(8,128)(2,1)S(1)} %get-tuple-element.87), channel_id=1, source_target_pairs={{0,1},{1,0},{2,3},{3,2},{4,5},{5,4},{6,7},{7,6},{8,9},{9,8},{10,11... | collective-permute-start | bytes 1179656 | tf_op jit(solution)/shard_map/ppermute | solution.py:403
  96.6 1.9 %collective-permute-start.22 = (bf16[4,256,128]{2,1,0:T(8,128)(2,1)S(1)}, bf16[4,256,128]{2,1,0:T(8,128)(2,1)S(1)}, u32[]{:S(2)}, u32[]{:S(2)}) collective-permute-start(bf16[4,256,128]{2,1,0:T(8,128)(2,1)S(1)} %get-tuple-element.97), channel_id=1, source_target_pairs={{0,8},{8,16},{16,24},{24,32},{32,40},{40,48},{48,56},{56,64},{64,7... | collective-permute-start | bytes 786440 | tf_op jit(solution)/shard_map/ppermute | solution.py:451
  98.5 6.0 %collective-permute-start.23 = (bf16[4,256,128]{2,1,0:T(8,128)(2,1)S(1)}, bf16[4,256,128]{2,1,0:T(8,128)(2,1)S(1)}, u32[]{:S(2)}, u32[]{:S(2)}) collective-permute-start(bf16[4,256,128]{2,1,0:T(8,128)(2,1)S(1)} %get-tuple-element.98), channel_id=1, source_target_pairs={{8,0},{16,8},{24,16},{32,24},{40,32},{48,40},{56,48},{64,56},{72,6... | collective-permute-start | bytes 786440 | tf_op jit(solution)/shard_map/ppermute | solution.py:450
  104.6 1.9 %collective-permute-start.25 = (bf16[4,256,128]{2,1,0:T(8,128)(2,1)S(1)}, bf16[4,256,128]{2,1,0:T(8,128)(2,1)S(1)}, u32[]{:S(2)}, u32[]{:S(2)}) collective-permute-start(bf16[4,256,128]{2,1,0:T(8,128)(2,1)S(1)} %get-tuple-element.100), channel_id=1, source_target_pairs={{0,136},{8,144},{16,152},{24,160},{32,168},{40,176},{48,184},{56,1... | collective-permute-start | bytes 786440 | tf_op jit(solution)/shard_map/ppermute | solution.py:458
  106.5 6.4 %collective-permute-done.18.refs_1_ = bf16[4,384,128]{2,1,0:T(8,128)(2,1)S(1)} collective-permute-done((bf16[4,384,128]{2,1,0:T(8,128)(2,1)S(1)}, bf16[4,384,128]{2,1,0:T(8,128)(2,1)S(1)}, u32[]{:S(2)}, u32[]{:S(2)}) %collective-permute-start.18) | collective-permute-done | bytes 393248 | tf_op jit(solution)/shard_map/ppermute | solution.py:403
  112.9 1.9 %collective-permute-start.26 = (bf16[4,256,128]{2,1,0:T(8,128)(2,1)S(1)}, bf16[4,256,128]{2,1,0:T(8,128)(2,1)S(1)}, u32[]{:S(2)}, u32[]{:S(2)}) collective-permute-start(bf16[4,256,128]{2,1,0:T(8,128)(2,1)S(1)} %get-tuple-element.101), channel_id=1, source_target_pairs={{8,128},{16,136},{24,144},{32,152},{40,160},{48,168},{56,176},{64,... | collective-permute-start | bytes 786440 | tf_op jit(solution)/shard_map/ppermute | solution.py:457
  114.8 3.2 %collective-permute-done.22.refs_1_ = bf16[4,256,128]{2,1,0:T(8,128)(2,1)S(1)} collective-permute-done((bf16[4,256,128]{2,1,0:T(8,128)(2,1)S(1)}, bf16[4,256,128]{2,1,0:T(8,128)(2,1)S(1)}, u32[]{:S(2)}, u32[]{:S(2)}) %collective-permute-start.22) | collective-permute-done | bytes 262176 | tf_op jit(solution)/shard_map/ppermute | solution.py:451
  118.1 3.2 %collective-permute-done.26.refs_5_ = bf16[4,256,128]{2,1,0:T(8,128)(2,1)S(1)} collective-permute-done((bf16[4,256,128]{2,1,0:T(8,128)(2,1)S(1)}, bf16[4,256,128]{2,1,0:T(8,128)(2,1)S(1)}, u32[]{:S(2)}, u32[]{:S(2)}) %collective-permute-start.26) | collective-permute-done | bytes 262176 | tf_op jit(solution)/shard_map/ppermute | solution.py:457
  121.3 1.8 %merge.1 = bf16[8,512,128]{2,1,0:T(8,128)(2,1)} custom-call(s32[3]{0:T(128)S(1)} %copy-done.4, bf16[8,256,128]{2,1,0:T(8,128)(2,1)S(1)} %get-tuple-element.96.refs_0_, bf16[4,256,128]{2,1,0:T(8,128)(2,1)S(1)} %collective-permute-done.22.refs_1_, bf16[4,256,128]{2,1,0:T(8,128)(2,1)S(1)} %collective-permute-done.23.refs_2_, ...), custom_call_target="tpu_custom_call" | custom-call | bytes 2097152 | tf_op jit(solution)/shard_map/merge/pallas_call | solution.py:218
  123.1 5.4 %all-to-all-start = ((bf16[8,512,128]{2,1,0:T(8,128)(2,1)}), bf16[8,512,128]{2,1,0:T(8,128)(2,1)S(1)}, u32[]{:S(2)}, u32[]{:S(2)}) async-start(bf16[8,512,128]{2,1,0:T(8,128)(2,1)} %merge.1), calls=%async_computation | async-start | bytes 2097152 | tf_op jit(solution)/shard_map/all_to_all | solution.py:414
  128.5 0.6 join.5
  129.1 2.1 %collective-permute-start.19 = (bf16[2,384,128]{2,1,0:T(8,128)(2,1)S(1)}, bf16[2,384,128]{2,1,0:T(8,128)(2,1)S(1)}, u32[]{:S(2)}, u32[]{:S(2)}) collective-permute-start(bf16[2,384,128]{2,1,0:T(8,128)(2,1)S(1)} %get-tuple-element.91), channel_id=1, source_target_pairs={{0,2},{1,3},{2,4},{3,5},{4,6},{5,7},{6,0},{7,1},{8,10},{9,11},{10,... | collective-permute-start | bytes 589832 | tf_op jit(solution)/shard_map/ppermute | solution.py:409
  131.2 2.7 %collective-permute-start.20 = (bf16[2,384,128]{2,1,0:T(8,128)(2,1)S(1)}, bf16[2,384,128]{2,1,0:T(8,128)(2,1)S(1)}, u32[]{:S(2)}, u32[]{:S(2)}) collective-permute-start(bf16[2,384,128]{2,1,0:T(8,128)(2,1)S(1)} %get-tuple-element.92), channel_id=1, source_target_pairs={{0,4},{1,5},{2,6},{3,7},{4,0},{5,1},{6,2},{7,3},{8,12},{9,13},{10,... | collective-permute-start | bytes 589832 | tf_op jit(solution)/shard_map/ppermute | solution.py:409
  133.9 1.5 collective-permute-start.21
  135.4 7.6 %collective-permute-done.19.refs_1_ = bf16[2,384,128]{2,1,0:T(8,128)(2,1)S(1)} collective-permute-done((bf16[2,384,128]{2,1,0:T(8,128)(2,1)S(1)}, bf16[2,384,128]{2,1,0:T(8,128)(2,1)S(1)}, u32[]{:S(2)}, u32[]{:S(2)}) %collective-permute-start.19) | collective-permute-done | bytes 196640 | tf_op jit(solution)/shard_map/ppermute | solution.py:409
  143.0 4.0 %collective-permute-done.20.refs_2_ = bf16[2,384,128]{2,1,0:T(8,128)(2,1)S(1)} collective-permute-done((bf16[2,384,128]{2,1,0:T(8,128)(2,1)S(1)}, bf16[2,384,128]{2,1,0:T(8,128)(2,1)S(1)}, u32[]{:S(2)}, u32[]{:S(2)}) %collective-permute-start.20) | collective-permute-done | bytes 196640 | tf_op jit(solution)/shard_map/ppermute | solution.py:409
  147.0 1.6 unpack_parts.1
  148.6 11.3 %all-to-all-done.got = bf16[8,512,128]{2,1,0:T(8,128)(2,1)S(1)} async-done(((bf16[8,512,128]{2,1,0:T(8,128)(2,1)}), bf16[8,512,128]{2,1,0:T(8,128)(2,1)S(1)}, u32[]{:S(2)}, u32[]{:S(2)}) %all-to-all-start) | async-done | bytes 1048608 | tf_op jit(solution)/shard_map/all_to_all | solution.py:414
  159.9 1.8 %unpack.1 = (bf16[1,128,1024]{2,1,0:T(8,128)(2,1)}, bf16[1,128,1024]{2,1,0:T(8,128)(2,1)}, bf16[1,128,1024]{2,1,0:T(8,128)(2,1)}, bf16[1,128,1024]{2,1,0:T(8,128)(2,1)}) custom-call(s32[3]{0:T(128)S(1)} %copy-done.4, bf16[8,512,128]{2,1,0:T(8,128)(2,1)S(1)} %all-to-all-done.got), custom_call_target="tpu_custom_call" | custom-call | bytes 2097152 | tf_op jit(solution)/shard_map/unpack/pallas_call | solution.py:218
  (22 shorter events, 0.1 us)
Async XLA Ops:
  0.6 16.5 %collective-permute-start.10 = (bf16[1,128,1024]{2,1,0:T(8,128)(2,1)}, bf16[1,128,1024]{2,1,0:T(8,128)(2,1)S(1)}, u32[]{:S(2)}, u32[]{:S(2)}) collective-permute-start(bf16[1,128,1024]{2,1,0:T(8,128)(2,1)} %param.13), channel_id=1, source_target_pairs={{0,128},{128,0},{1,129},{129,1},{2,130},{130,2},{3,131},{131,3},{4... | collective-permute-start | bytes 786440 | tf_op jit(solution)/shard_map/ppermute | solution.py:432
  0.7 17.8 %collective-permute-start.11 = (bf16[1,128,1024]{2,1,0:T(8,128)(2,1)}, bf16[1,128,1024]{2,1,0:T(8,128)(2,1)S(1)}, u32[]{:S(2)}, u32[]{:S(2)}) collective-permute-start(bf16[1,128,1024]{2,1,0:T(8,128)(2,1)} %param.14), channel_id=1, source_target_pairs={{0,128},{128,0},{1,129},{129,1},{2,130},{130,2},{3,131},{131,3},{4... | collective-permute-start | bytes 786440 | tf_op jit(solution)/shard_map/ppermute | solution.py:433
  1.8 9.1 %copy-start.1 = (bf16[1,128,1024]{2,1,0:T(8,128)(2,1)S(1)}, bf16[1,128,1024]{2,1,0:T(8,128)(2,1)}, u32[]{:S(2)}) copy-start(bf16[1,128,1024]{2,1,0:T(8,128)(2,1)} %refs_0_.1) | copy-start | bytes 786436
  1.8 9.1 %copy-start.2 = (bf16[1,128,1024]{2,1,0:T(8,128)(2,1)S(1)}, bf16[1,128,1024]{2,1,0:T(8,128)(2,1)}, u32[]{:S(2)}) copy-start(bf16[1,128,1024]{2,1,0:T(8,128)(2,1)} %refs_1_.1) | copy-start | bytes 786436
  4.6 6.4 %copy-start.4 = (s32[3]{0:T(128)S(1)}, s32[3]{0:T(128)}, u32[]{:S(2)}) copy-start(s32[3]{0:T(128)} %pad_add_fusion.pos) | copy-start | bytes 40
  4.6 20.6 %collective-permute-start = (bf16[4,272,128]{2,1,0:T(8,128)(2,1)}, bf16[4,272,128]{2,1,0:T(8,128)(2,1)S(1)}, u32[]{:S(2)}, u32[]{:S(2)}) collective-permute-start(bf16[4,272,128]{2,1,0:T(8,128)(2,1)} %get-tuple-element.58), channel_id=1, source_target_pairs={{0,1},{1,0},{2,3},{3,2},{4,5},{5,4},{6,7},{7,6},{8,9},{9,8},{10,11... | collective-permute-start | bytes 835592 | tf_op jit(solution)/shard_map/ppermute | solution.py:403
  10.9 1.0 copy-start.3
  12.6 12.6 %copy-start = (bf16[4,272,128]{2,1,0:T(8,128)(2,1)S(1)}, bf16[4,272,128]{2,1,0:T(8,128)(2,1)}, u32[]{:S(2)}) copy-start(bf16[4,272,128]{2,1,0:T(8,128)(2,1)} %get-tuple-element.57.refs_0_) | copy-start | bytes 835588
  12.6 14.0 %collective-permute-start.6 = (bf16[2,384,128]{2,1,0:T(8,128)(2,1)S(1)}, bf16[2,384,128]{2,1,0:T(8,128)(2,1)S(1)}, u32[]{:S(2)}, u32[]{:S(2)}) collective-permute-start(bf16[2,384,128]{2,1,0:T(8,128)(2,1)S(1)} %get-tuple-element.66), channel_id=1, source_target_pairs={{0,2},{1,3},{2,4},{3,5},{4,6},{5,7},{6,0},{7,1},{8,10},{9,11},{10,... | collective-permute-start | bytes 589832 | tf_op jit(solution)/shard_map/ppermute | solution.py:409
  14.2 18.6 %collective-permute-start.7 = (bf16[2,384,128]{2,1,0:T(8,128)(2,1)S(1)}, bf16[2,384,128]{2,1,0:T(8,128)(2,1)S(1)}, u32[]{:S(2)}, u32[]{:S(2)}) collective-permute-start(bf16[2,384,128]{2,1,0:T(8,128)(2,1)S(1)} %get-tuple-element.67), channel_id=1, source_target_pairs={{0,4},{1,5},{2,6},{3,7},{4,0},{5,1},{6,2},{7,3},{8,12},{9,13},{10,... | collective-permute-start | bytes 589832 | tf_op jit(solution)/shard_map/ppermute | solution.py:409
  17.1 17.0 %collective-permute-start.8 = (bf16[2,384,128]{2,1,0:T(8,128)(2,1)S(1)}, bf16[2,384,128]{2,1,0:T(8,128)(2,1)S(1)}, u32[]{:S(2)}, u32[]{:S(2)}) collective-permute-start(bf16[2,384,128]{2,1,0:T(8,128)(2,1)S(1)} %get-tuple-element.68), channel_id=1, source_target_pairs={{0,6},{1,7},{2,0},{3,1},{4,2},{5,3},{6,4},{7,5},{8,14},{9,15},{10,... | collective-permute-start | bytes 589832 | tf_op jit(solution)/shard_map/ppermute | solution.py:409
  19.2 30.2 %collective-permute-start.12 = (bf16[4,256,128]{2,1,0:T(8,128)(2,1)S(1)}, bf16[4,256,128]{2,1,0:T(8,128)(2,1)S(1)}, u32[]{:S(2)}, u32[]{:S(2)}) collective-permute-start(bf16[4,256,128]{2,1,0:T(8,128)(2,1)S(1)} %get-tuple-element.72), channel_id=1, source_target_pairs={{0,1},{1,0},{2,3},{3,2},{4,5},{5,4},{6,7},{7,6},{8,9},{9,8},{10,11... | collective-permute-start | bytes 786440 | tf_op jit(solution)/shard_map/ppermute | solution.py:403
  25.8 15.0 %collective-permute-start.1 = (bf16[2,272,128]{2,1,0:T(8,128)(2,1)S(1)}, bf16[2,272,128]{2,1,0:T(8,128)(2,1)S(1)}, u32[]{:S(2)}, u32[]{:S(2)}) collective-permute-start(bf16[2,272,128]{2,1,0:T(8,128)(2,1)S(1)} %get-tuple-element.60), channel_id=1, source_target_pairs={{0,2},{1,3},{2,4},{3,5},{4,6},{5,7},{6,0},{7,1},{8,10},{9,11},{10,... | collective-permute-start | bytes 417800 | tf_op jit(solution)/shard_map/ppermute | solution.py:409
  26.6 14.2 %collective-permute-start.2 = (bf16[2,272,128]{2,1,0:T(8,128)(2,1)S(1)}, bf16[2,272,128]{2,1,0:T(8,128)(2,1)S(1)}, u32[]{:S(2)}, u32[]{:S(2)}) collective-permute-start(bf16[2,272,128]{2,1,0:T(8,128)(2,1)S(1)} %get-tuple-element.61), channel_id=1, source_target_pairs={{0,4},{1,5},{2,6},{3,7},{4,0},{5,1},{6,2},{7,3},{8,12},{9,13},{10,... | collective-permute-start | bytes 417800 | tf_op jit(solution)/shard_map/ppermute | solution.py:409
  32.8 8.0 %collective-permute-start.3 = (bf16[2,272,128]{2,1,0:T(8,128)(2,1)S(1)}, bf16[2,272,128]{2,1,0:T(8,128)(2,1)S(1)}, u32[]{:S(2)}, u32[]{:S(2)}) collective-permute-start(bf16[2,272,128]{2,1,0:T(8,128)(2,1)S(1)} %get-tuple-element.62), channel_id=1, source_target_pairs={{0,6},{1,7},{2,0},{3,1},{4,2},{5,3},{6,4},{7,5},{8,14},{9,15},{10,... | collective-permute-start | bytes 417800 | tf_op jit(solution)/shard_map/ppermute | solution.py:409
  34.7 28.5 %collective-permute-start.9 = (bf16[4,384,128]{2,1,0:T(8,128)(2,1)S(1)}, bf16[4,384,128]{2,1,0:T(8,128)(2,1)S(1)}, u32[]{:S(2)}, u32[]{:S(2)}) collective-permute-start(bf16[4,384,128]{2,1,0:T(8,128)(2,1)S(1)} %get-tuple-element.70), channel_id=1, source_target_pairs={{0,1},{1,0},{2,3},{3,2},{4,5},{5,4},{6,7},{7,6},{8,9},{9,8},{10,11... | collective-permute-start | bytes 1179656 | tf_op jit(solution)/shard_map/ppermute | solution.py:403
  41.5 30.6 %collective-permute-start.4 = (bf16[4,272,128]{2,1,0:T(8,128)(2,1)S(1)}, bf16[4,272,128]{2,1,0:T(8,128)(2,1)S(1)}, u32[]{:S(2)}, u32[]{:S(2)}) collective-permute-start(bf16[4,272,128]{2,1,0:T(8,128)(2,1)S(1)} %get-tuple-element.63.high.vh), channel_id=1, source_target_pairs={{0,8},{8,16},{16,24},{24,32},{32,40},{40,48},{48,56},{56,64},{64,7... | collective-permute-start | bytes 835592 | tf_op jit(solution)/shard_map/ppermute | solution.py:441
  44.9 27.2 %collective-permute-start.5 = (bf16[4,272,128]{2,1,0:T(8,128)(2,1)S(1)}, bf16[4,272,128]{2,1,0:T(8,128)(2,1)S(1)}, u32[]{:S(2)}, u32[]{:S(2)}) collective-permute-start(bf16[4,272,128]{2,1,0:T(8,128)(2,1)S(1)} %get-tuple-element.64.low.vl), channel_id=1, source_target_pairs={{8,0},{16,8},{24,16},{32,24},{40,32},{48,40},{56,48},{64,56},{72,6... | collective-permute-start | bytes 835592 | tf_op jit(solution)/shard_map/ppermute | solution.py:442
  50.0 7.7 %collective-permute-start.13 = (bf16[2,256,128]{2,1,0:T(8,128)(2,1)S(1)}, bf16[2,256,128]{2,1,0:T(8,128)(2,1)S(1)}, u32[]{:S(2)}, u32[]{:S(2)}) collective-permute-start(bf16[2,256,128]{2,1,0:T(8,128)(2,1)S(1)} %get-tuple-element.74), channel_id=1, source_target_pairs={{0,2},{1,3},{2,4},{3,5},{4,6},{5,7},{6,0},{7,1},{8,10},{9,11},{10,... | collective-permute-start | bytes 393224 | tf_op jit(solution)/shard_map/ppermute | solution.py:409
  50.7 8.9 %collective-permute-start.14 = (bf16[2,256,128]{2,1,0:T(8,128)(2,1)S(1)}, bf16[2,256,128]{2,1,0:T(8,128)(2,1)S(1)}, u32[]{:S(2)}, u32[]{:S(2)}) collective-permute-start(bf16[2,256,128]{2,1,0:T(8,128)(2,1)S(1)} %get-tuple-element.75), channel_id=1, source_target_pairs={{0,4},{1,5},{2,6},{3,7},{4,0},{5,1},{6,2},{7,3},{8,12},{9,13},{10,... | collective-permute-start | bytes 393224 | tf_op jit(solution)/shard_map/ppermute | solution.py:409
  57.7 5.0 %collective-permute-start.15 = (bf16[2,256,128]{2,1,0:T(8,128)(2,1)S(1)}, bf16[2,256,128]{2,1,0:T(8,128)(2,1)S(1)}, u32[]{:S(2)}, u32[]{:S(2)}) collective-permute-start(bf16[2,256,128]{2,1,0:T(8,128)(2,1)S(1)} %get-tuple-element.76), channel_id=1, source_target_pairs={{0,6},{1,7},{2,0},{3,1},{4,2},{5,3},{6,4},{7,5},{8,14},{9,15},{10,... | collective-permute-start | bytes 393224 | tf_op jit(solution)/shard_map/ppermute | solution.py:409
  57.7 0.7 copy-start.5
  63.3 20.4 %collective-permute-start.16 = (bf16[4,256,128]{2,1,0:T(8,128)(2,1)S(1)}, bf16[4,256,128]{2,1,0:T(8,128)(2,1)S(1)}, u32[]{:S(2)}, u32[]{:S(2)}) collective-permute-start(bf16[4,256,128]{2,1,0:T(8,128)(2,1)S(1)} %get-tuple-element.81.high), channel_id=1, source_target_pairs={{0,8},{8,16},{16,24},{24,32},{32,40},{40,48},{48,56},{56,64},{64,7... | collective-permute-start | bytes 786440 | tf_op jit(solution)/shard_map/ppermute | solution.py:445
  65.2 18.5 %collective-permute-start.17 = (bf16[4,256,128]{2,1,0:T(8,128)(2,1)S(1)}, bf16[4,256,128]{2,1,0:T(8,128)(2,1)S(1)}, u32[]{:S(2)}, u32[]{:S(2)}) collective-permute-start(bf16[4,256,128]{2,1,0:T(8,128)(2,1)S(1)} %get-tuple-element.82.low), channel_id=1, source_target_pairs={{8,0},{16,8},{24,16},{32,24},{40,32},{48,40},{56,48},{64,56},{72,6... | collective-permute-start | bytes 786440 | tf_op jit(solution)/shard_map/ppermute | solution.py:446
  95.0 18.0 %collective-permute-start.18 = (bf16[4,384,128]{2,1,0:T(8,128)(2,1)S(1)}, bf16[4,384,128]{2,1,0:T(8,128)(2,1)S(1)}, u32[]{:S(2)}, u32[]{:S(2)}) collective-permute-start(bf16[4,384,128]{2,1,0:T(8,128)(2,1)S(1)} %get-tuple-element.87), channel_id=1, source_target_pairs={{0,1},{1,0},{2,3},{3,2},{4,5},{5,4},{6,7},{7,6},{8,9},{9,8},{10,11... | collective-permute-start | bytes 1179656 | tf_op jit(solution)/shard_map/ppermute | solution.py:403
  96.6 24.7 %collective-permute-start.24 = (bf16[8,256,128]{2,1,0:T(8,128)(2,1)S(1)}, bf16[8,256,128]{2,1,0:T(8,128)(2,1)S(1)}, u32[]{:S(2)}, u32[]{:S(2)}) collective-permute-start(bf16[8,256,128]{2,1,0:T(8,128)(2,1)S(1)} %get-tuple-element.99), channel_id=1, source_target_pairs={{0,128},{128,0},{1,129},{129,1},{2,130},{130,2},{3,131},{131,3},{4... | collective-permute-start | bytes 1572872 | tf_op jit(solution)/shard_map/ppermute | solution.py:459
  96.6 21.5 %collective-permute-start.22 = (bf16[4,256,128]{2,1,0:T(8,128)(2,1)S(1)}, bf16[4,256,128]{2,1,0:T(8,128)(2,1)S(1)}, u32[]{:S(2)}, u32[]{:S(2)}) collective-permute-start(bf16[4,256,128]{2,1,0:T(8,128)(2,1)S(1)} %get-tuple-element.97), channel_id=1, source_target_pairs={{0,8},{8,16},{16,24},{24,32},{32,40},{40,48},{48,56},{56,64},{64,7... | collective-permute-start | bytes 786440 | tf_op jit(solution)/shard_map/ppermute | solution.py:451
  98.5 19.6 %collective-permute-start.23 = (bf16[4,256,128]{2,1,0:T(8,128)(2,1)S(1)}, bf16[4,256,128]{2,1,0:T(8,128)(2,1)S(1)}, u32[]{:S(2)}, u32[]{:S(2)}) collective-permute-start(bf16[4,256,128]{2,1,0:T(8,128)(2,1)S(1)} %get-tuple-element.98), channel_id=1, source_target_pairs={{8,0},{16,8},{24,16},{32,24},{40,32},{48,40},{56,48},{64,56},{72,6... | collective-permute-start | bytes 786440 | tf_op jit(solution)/shard_map/ppermute | solution.py:450
  104.6 13.5 %collective-permute-start.25 = (bf16[4,256,128]{2,1,0:T(8,128)(2,1)S(1)}, bf16[4,256,128]{2,1,0:T(8,128)(2,1)S(1)}, u32[]{:S(2)}, u32[]{:S(2)}) collective-permute-start(bf16[4,256,128]{2,1,0:T(8,128)(2,1)S(1)} %get-tuple-element.100), channel_id=1, source_target_pairs={{0,136},{8,144},{16,152},{24,160},{32,168},{40,176},{48,184},{56,1... | collective-permute-start | bytes 786440 | tf_op jit(solution)/shard_map/ppermute | solution.py:458
  112.9 8.4 %collective-permute-start.26 = (bf16[4,256,128]{2,1,0:T(8,128)(2,1)S(1)}, bf16[4,256,128]{2,1,0:T(8,128)(2,1)S(1)}, u32[]{:S(2)}, u32[]{:S(2)}) collective-permute-start(bf16[4,256,128]{2,1,0:T(8,128)(2,1)S(1)} %get-tuple-element.101), channel_id=1, source_target_pairs={{8,128},{16,136},{24,144},{32,152},{40,160},{48,168},{56,176},{64,... | collective-permute-start | bytes 786440 | tf_op jit(solution)/shard_map/ppermute | solution.py:457
  123.1 36.8 %all-to-all-start = ((bf16[8,512,128]{2,1,0:T(8,128)(2,1)}), bf16[8,512,128]{2,1,0:T(8,128)(2,1)S(1)}, u32[]{:S(2)}, u32[]{:S(2)}) async-start(bf16[8,512,128]{2,1,0:T(8,128)(2,1)} %merge.1), calls=%async_computation | async-start | bytes 2097152 | tf_op jit(solution)/shard_map/all_to_all | solution.py:414
  129.1 13.9 %collective-permute-start.19 = (bf16[2,384,128]{2,1,0:T(8,128)(2,1)S(1)}, bf16[2,384,128]{2,1,0:T(8,128)(2,1)S(1)}, u32[]{:S(2)}, u32[]{:S(2)}) collective-permute-start(bf16[2,384,128]{2,1,0:T(8,128)(2,1)S(1)} %get-tuple-element.91), channel_id=1, source_target_pairs={{0,2},{1,3},{2,4},{3,5},{4,6},{5,7},{6,0},{7,1},{8,10},{9,11},{10,... | collective-permute-start | bytes 589832 | tf_op jit(solution)/shard_map/ppermute | solution.py:409
  131.2 15.8 %collective-permute-start.20 = (bf16[2,384,128]{2,1,0:T(8,128)(2,1)S(1)}, bf16[2,384,128]{2,1,0:T(8,128)(2,1)S(1)}, u32[]{:S(2)}, u32[]{:S(2)}) collective-permute-start(bf16[2,384,128]{2,1,0:T(8,128)(2,1)S(1)} %get-tuple-element.92), channel_id=1, source_target_pairs={{0,4},{1,5},{2,6},{3,7},{4,0},{5,1},{6,2},{7,3},{8,12},{9,13},{10,... | collective-permute-start | bytes 589832 | tf_op jit(solution)/shard_map/ppermute | solution.py:409
  133.9 13.1 %collective-permute-start.21 = (bf16[2,384,128]{2,1,0:T(8,128)(2,1)S(1)}, bf16[2,384,128]{2,1,0:T(8,128)(2,1)S(1)}, u32[]{:S(2)}, u32[]{:S(2)}) collective-permute-start(bf16[2,384,128]{2,1,0:T(8,128)(2,1)S(1)} %get-tuple-element.93), channel_id=1, source_target_pairs={{0,6},{1,7},{2,0},{3,1},{4,2},{5,3},{6,4},{7,5},{8,14},{9,15},{10,... | collective-permute-start | bytes 589832 | tf_op jit(solution)/shard_map/ppermute | solution.py:409

commit v4 on v3

--- a/solution.py
+++ b/solution.py
@@ -42,15 +42,16 @@
     padded = jnp.concatenate([bias, jnp.zeros((CHUNK - 16, CHUNK), F32)], axis=0).astype(BF16)
     turned = dot(eye(CHUNK), padded, NT)
     lane = lax.broadcasted_iota(jnp.int32, (CHUNK, CHUNK), 1)
-    for c in range(EXT // CHUNK):
-        at = pl.ds(c * CHUNK, CHUNK)
-        k = chunks(c)
-        val = values(c)
-        kx[at, 0:CHUNK] = k
-        kx[at, CHUNK : 2 * CHUNK] = jnp.where(lane == c, turned, 0.0).astype(BF16)
-        kt[:, at] = flipped(k)
-        v[at, :] = val
-        vt[:, at] = flipped(val)
+    for c in range(0, EXT // CHUNK, 2):
+        pair = pl.ds(c * CHUNK, 2 * CHUNK)
+        k = jnp.concatenate([chunks(c), chunks(c + 1)], axis=0)
+        val = jnp.concatenate([values(c), values(c + 1)], axis=0)
+        kx[pair, 0:CHUNK] = k
+        for n in range(2):
+            kx[pl.ds((c + n) * CHUNK, CHUNK), CHUNK : 2 * CHUNK] = jnp.where(lane == c + n, turned, 0.0).astype(BF16)
+        kt[:, pair] = flipped(k)
+        v[pair, :] = val
+        vt[:, pair] = flipped(val)
 
 
 def tile_step(q, gt, start, width, step, windowed, scratch):
@@ -128,8 +129,9 @@
     refs = (before, low, high, after)
     bias = jnp.where(validity(refs, 0) > 0.5, 0.0, NEG)
     stage_keys(piece(refs, VROWS), piece(refs, VROWS + CHUNK), bias, kx, kt, v, vt)
-    for c in range(8):
-        gt[:, c * CHUNK : (c + 1) * CHUNK] = flipped(asks[c, CHUNK : 2 * CHUNK, :])
+    for c in range(0, 8, 2):
+        pair = jnp.concatenate([asks[c, CHUNK : 2 * CHUNK, :], asks[c + 1, CHUNK : 2 * CHUNK, :]], axis=0)
+        gt[:, c * CHUNK : (c + 2) * CHUNK] = flipped(pair)
     dk[...] = jnp.zeros_like(dk)
     dv[...] = jnp.zeros_like(dv)
 
@@ -142,7 +144,7 @@
         pay[pl.ds(2 * i, 2), 0:CHUNK, :] = flipped(gq.astype(BF16)).reshape(2, CHUNK, CHUNK)
         return carry
 
-    lax.fori_loop(0, BLOCK // QROWS, step, 0)
+    lax.fori_loop(0, BLOCK // QROWS, step, 0, unroll=4)
     emit_sums(dk, dv, back, to_lo, to_hi)
 
 
@@ -166,7 +168,7 @@
         pay[pl.ds(2 * i, 2), CHUNK : 2 * CHUNK, :] = flipped(gq.astype(BF16)).reshape(2, CHUNK, CHUNK)
         return carry
 
-    lax.fori_loop(0, BLOCK // QROWS, step, 0)
+    lax.fori_loop(0, BLOCK // QROWS, step, 0, unroll=4)
     emit_sums(dk, dv, back, to_lo, to_hi)
 
 

time: 162 us -> 159 us (0.981)
  Pallas kernels: 36.3 us -> 33.1 us
    pallas_call x2, Pallas kernels: 22.2 us -> 19.1 us  [run_attention(): pl.pallas_call(kernel, out_shape=outs, in_specs=[pl.BlockSpec(memory_spac...]
  transfers between devices with their start and end apart: 28 -> 28, of which waited for: 9 -> 9; matrix products, arithmetic and copies ran while one was open for 1% -> 1% of each run, Pallas kernels for 13% -> 12%
where the time goes in v4:
time: 159 us; the launch traced here: 158 us
  starting transfers between devices  70.4 us (44%)
  waiting for transfers between devices  50.5 us (32%)
  Pallas kernels  33.1 us (21%)
  local copies, waits for them, and re-layouts  2.23 us (1%)
    ppermute x12, starting transfers between devices, along_y(): lax.ppermute(parts[d], 'seq', [(i, (i + 2 * d) % size) for i in range(siz...  22 us
    ppermute x12, waiting for transfers between devices, along_y(): lax.ppermute(parts[d], 'seq', [(i, (i + 2 * d) % size) for i in range(siz...  21 us
    pallas_call x2, Pallas kernels, run_attention(): pl.pallas_call(kernel, out_shape=outs, in_specs=[pl.BlockSpec(memory_spac...  19.1 us
    ppermute x4, starting transfers between devices, across_z(): return lax.ppermute(send, 'seq', [(i, i ^ 1) for i in range(size)])  14.7 us
    ppermute x4, waiting for transfers between devices, across_z(): return lax.ppermute(send, 'seq', [(i, i ^ 1) for i in range(size)])  11.8 us
    pallas_call x13, Pallas kernels, small_call(): pl.pallas_call(kernel, out_shape=outs, in_specs=[pl.BlockSpec(memory_spac...  11.3 us
    all_to_all x1, waiting for transfers between devices, exchange(): lax.all_to_all(packed, 'seq', split_axis=0, concat_axis=0, tiled=True)  11.3 us
    ppermute x1, starting transfers between devices, shards(): c_after = lax.ppermute(c_low, 'blk', down)  6.21 us
  transfers between devices with their start and end apart: 28, of which 9 were waited for; matrix products, arithmetic and copies ran while one was open for 1% of the time, Pallas kernels for 12%

profile of v4, /device:TPU:32, one launch (start us, length us, event | category | flops | bytes accessed | tf_op | source)
XLA Modules:
  0.0 158.4 jit_solution(17210110280043376821)
XLA Ops:
  0.6 0.1 collective-permute-start.10
  0.7 0.5 collective-permute-start.11
  1.2 0.6 pad_add_fusion.pos
  1.8 2.7 %pack_marked.1 = (bf16[4,272,128]{2,1,0:T(8,128)(2,1)}, bf16[4,272,128]{2,1,0:T(8,128)(2,1)}) custom-call(s32[3]{0:T(128)} %pad_add_fusion.pos, s32[2,128]{1,0:T(2,128)} %key_valid.1, bf16[1,128,1024]{2,1,0:T(8,128)(2,1)} %keys.1, bf16[1,128,1024]{2,1,0:T(8,128)(2,1)} %values.1), custom_call_target="tpu_custom_call" | custom-call | bytes 2097152 | tf_op jit(solution)/shard_map/pack_marked/pallas_call | solution.py:266
  4.6 0.0 copy-start.4
  4.6 6.4 %collective-permute-start = (bf16[4,272,128]{2,1,0:T(8,128)(2,1)}, bf16[4,272,128]{2,1,0:T(8,128)(2,1)S(1)}, u32[]{:S(2)}, u32[]{:S(2)}) collective-permute-start(bf16[4,272,128]{2,1,0:T(8,128)(2,1)} %get-tuple-element.58), channel_id=1, source_target_pairs={{0,1},{1,0},{2,3},{3,2},{4,5},{5,4},{6,7},{7,6},{8,9},{9,8},{10,11... | collective-permute-start | bytes 835592 | tf_op jit(solution)/shard_map/ppermute | solution.py:405
  11.0 0.9 copy-done.3
  11.9 0.7 pack_y.1
  12.6 1.7 %collective-permute-start.6 = (bf16[2,384,128]{2,1,0:T(8,128)(2,1)S(1)}, bf16[2,384,128]{2,1,0:T(8,128)(2,1)S(1)}, u32[]{:S(2)}, u32[]{:S(2)}) collective-permute-start(bf16[2,384,128]{2,1,0:T(8,128)(2,1)S(1)} %get-tuple-element.66), channel_id=1, source_target_pairs={{0,2},{1,3},{2,4},{3,5},{4,6},{5,7},{6,0},{7,1},{8,10},{9,11},{10,... | collective-permute-start | bytes 589832 | tf_op jit(solution)/shard_map/ppermute | solution.py:411
  14.2 2.9 %collective-permute-start.7 = (bf16[2,384,128]{2,1,0:T(8,128)(2,1)S(1)}, bf16[2,384,128]{2,1,0:T(8,128)(2,1)S(1)}, u32[]{:S(2)}, u32[]{:S(2)}) collective-permute-start(bf16[2,384,128]{2,1,0:T(8,128)(2,1)S(1)} %get-tuple-element.67), channel_id=1, source_target_pairs={{0,4},{1,5},{2,6},{3,7},{4,0},{5,1},{6,2},{7,3},{8,12},{9,13},{10,... | collective-permute-start | bytes 589832 | tf_op jit(solution)/shard_map/ppermute | solution.py:411
  17.1 0.0 collective-permute-done.10.refs_0_
  17.1 1.3 collective-permute-start.8
  18.5 0.7 pack.1
  19.2 0.6 collective-permute-start.12
  19.8 5.4 %collective-permute-done.refs_1_ = bf16[4,272,128]{2,1,0:T(8,128)(2,1)S(1)} collective-permute-done((bf16[4,272,128]{2,1,0:T(8,128)(2,1)}, bf16[4,272,128]{2,1,0:T(8,128)(2,1)S(1)}, u32[]{:S(2)}, u32[]{:S(2)}) %collective-permute-start) | collective-permute-done | bytes 278560 | tf_op jit(solution)/shard_map/ppermute | solution.py:405
  25.2 0.6 join.3
  25.8 0.8 collective-permute-start.1
  26.6 0.0 collective-permute-done.6.refs_1_
  26.6 6.2 %collective-permute-start.2 = (bf16[2,272,128]{2,1,0:T(8,128)(2,1)S(1)}, bf16[2,272,128]{2,1,0:T(8,128)(2,1)S(1)}, u32[]{:S(2)}, u32[]{:S(2)}) collective-permute-start(bf16[2,272,128]{2,1,0:T(8,128)(2,1)S(1)} %get-tuple-element.61), channel_id=1, source_target_pairs={{0,4},{1,5},{2,6},{3,7},{4,0},{5,1},{6,2},{7,3},{8,12},{9,13},{10,... | collective-permute-start | bytes 417800 | tf_op jit(solution)/shard_map/ppermute | solution.py:411
  32.8 1.3 collective-permute-start.3
  34.1 0.0 collective-permute-done.8.refs_3_
  34.1 0.6 split.1
  34.7 6.0 %collective-permute-start.9 = (bf16[4,384,128]{2,1,0:T(8,128)(2,1)S(1)}, bf16[4,384,128]{2,1,0:T(8,128)(2,1)S(1)}, u32[]{:S(2)}, u32[]{:S(2)}) collective-permute-start(bf16[4,384,128]{2,1,0:T(8,128)(2,1)S(1)} %get-tuple-element.70), channel_id=1, source_target_pairs={{0,1},{1,0},{2,3},{3,2},{4,5},{5,4},{6,7},{7,6},{8,9},{9,8},{10,11... | collective-permute-start | bytes 1179656 | tf_op jit(solution)/shard_map/ppermute | solution.py:405
  40.8 0.6 halves.2
  41.5 3.4 %collective-permute-start.4 = (bf16[4,272,128]{2,1,0:T(8,128)(2,1)S(1)}, bf16[4,272,128]{2,1,0:T(8,128)(2,1)S(1)}, u32[]{:S(2)}, u32[]{:S(2)}) collective-permute-start(bf16[4,272,128]{2,1,0:T(8,128)(2,1)S(1)} %get-tuple-element.63.high.vh), channel_id=1, source_target_pairs={{0,8},{8,16},{16,24},{24,32},{32,40},{40,48},{48,56},{56,64},{64,7... | collective-permute-start | bytes 835592 | tf_op jit(solution)/shard_map/ppermute | solution.py:443
  44.9 4.6 %collective-permute-start.5 = (bf16[4,272,128]{2,1,0:T(8,128)(2,1)S(1)}, bf16[4,272,128]{2,1,0:T(8,128)(2,1)S(1)}, u32[]{:S(2)}, u32[]{:S(2)}) collective-permute-start(bf16[4,272,128]{2,1,0:T(8,128)(2,1)S(1)} %get-tuple-element.64.low.vl), channel_id=1, source_target_pairs={{8,0},{16,8},{24,16},{32,24},{40,32},{48,40},{56,48},{64,56},{72,6... | collective-permute-start | bytes 835592 | tf_op jit(solution)/shard_map/ppermute | solution.py:444
  49.4 0.6 join.4
  50.0 0.7 collective-permute-start.13
  50.7 0.8 collective-permute-start.14
  51.6 6.1 %collective-permute-done.13.refs_1_ = bf16[2,256,128]{2,1,0:T(8,128)(2,1)S(1)} collective-permute-done((bf16[2,256,128]{2,1,0:T(8,128)(2,1)S(1)}, bf16[2,256,128]{2,1,0:T(8,128)(2,1)S(1)}, u32[]{:S(2)}, u32[]{:S(2)}) %collective-permute-start.13) | collective-permute-done | bytes 131104 | tf_op jit(solution)/shard_map/ppermute | solution.py:411
  57.7 0.7 copy-done.5
  58.4 0.6 dynamic_slice.3
  59.6 0.0 collective-permute-done.14.refs_2_
  59.6 3.0 %collective-permute-done.15.refs_3_ = bf16[2,256,128]{2,1,0:T(8,128)(2,1)S(1)} collective-permute-done((bf16[2,256,128]{2,1,0:T(8,128)(2,1)S(1)}, bf16[2,256,128]{2,1,0:T(8,128)(2,1)S(1)}, u32[]{:S(2)}, u32[]{:S(2)}) %collective-permute-start.15) | collective-permute-done | bytes 131104 | tf_op jit(solution)/shard_map/ppermute | solution.py:411
  62.7 0.6 halves.3
  63.3 1.9 %collective-permute-start.16 = (bf16[4,256,128]{2,1,0:T(8,128)(2,1)S(1)}, bf16[4,256,128]{2,1,0:T(8,128)(2,1)S(1)}, u32[]{:S(2)}, u32[]{:S(2)}) collective-permute-start(bf16[4,256,128]{2,1,0:T(8,128)(2,1)S(1)} %get-tuple-element.81.high), channel_id=1, source_target_pairs={{0,8},{8,16},{16,24},{24,32},{32,40},{40,48},{48,56},{56,64},{64,7... | collective-permute-start | bytes 786440 | tf_op jit(solution)/shard_map/ppermute | solution.py:447
  65.2 6.2 %collective-permute-start.17 = (bf16[4,256,128]{2,1,0:T(8,128)(2,1)S(1)}, bf16[4,256,128]{2,1,0:T(8,128)(2,1)S(1)}, u32[]{:S(2)}, u32[]{:S(2)}) collective-permute-start(bf16[4,256,128]{2,1,0:T(8,128)(2,1)S(1)} %get-tuple-element.82.low), channel_id=1, source_target_pairs={{8,0},{16,8},{24,16},{32,24},{40,32},{48,40},{56,48},{64,56},{72,6... | collective-permute-start | bytes 786440 | tf_op jit(solution)/shard_map/ppermute | solution.py:448
  71.4 0.6 whole.1.asks
  72.1 0.0 collective-permute-done.4.before.vb
  72.1 0.0 collective-permute-done.5.after.va
  72.1 9.8 %self_attention.1 = (f32[128,1024]{1,0:T(8,128)S(1)}, bf16[128,1024]{1,0:T(8,128)(2,1)S(1)}, bf16[8,128,128]{2,1,0:T(8,128)(2,1)S(1)}, bf16[8,256,128]{2,1,0:T(8...) custom-call(bf16[4,272,128]{2,1,0:T(8,128)(2,1)S(1)} %collective-permute-done.4.before.vb, ...), custom_call_target="tpu_custom_call" | custom-call | flops 8000000000 | bytes 3145728 | tf_op jit(solution)/shard_map/self_attention/pallas_call | solution.py:196
  81.9 0.0 collective-permute-done.17.after
  81.9 9.3 %cross_attention.1 = (bf16[8,256,128]{2,1,0:T(8,128)(2,1)S(1)}, bf16[8,256,128]{2,1,0:T(8,128)(2,1)S(1)}, bf16[4,256,128]{2,1,0:T(8,128)(2,1)S(1)}, bf16[4,256,128]{2,1,0:T(8,128)(2,1)S(1)}) custom-call(s32[1]{0:T(128)} %bitcast.3.band, bf16[4,272,128]{2,1,0:T(8,128)(2,1)S(1)} %collective-permute-done.4.before.vb, ...), custom_call_target="tpu_custom_call" | custom-call | flops 8000000000 | bytes 3145728 | tf_op jit(solution)/shard_map/cross_attention/pallas_call | solution.py:196
  91.2 0.6 order.1
  91.8 1.6 %collective-permute-start.18 = (bf16[4,384,128]{2,1,0:T(8,128)(2,1)S(1)}, bf16[4,384,128]{2,1,0:T(8,128)(2,1)S(1)}, u32[]{:S(2)}, u32[]{:S(2)}) collective-permute-start(bf16[4,384,128]{2,1,0:T(8,128)(2,1)S(1)} %get-tuple-element.87), channel_id=1, source_target_pairs={{0,1},{1,0},{2,3},{3,2},{4,5},{5,4},{6,7},{7,6},{8,9},{9,8},{10,11... | collective-permute-start | bytes 1179656 | tf_op jit(solution)/shard_map/ppermute | solution.py:405
  93.5 1.9 %collective-permute-start.22 = (bf16[4,256,128]{2,1,0:T(8,128)(2,1)S(1)}, bf16[4,256,128]{2,1,0:T(8,128)(2,1)S(1)}, u32[]{:S(2)}, u32[]{:S(2)}) collective-permute-start(bf16[4,256,128]{2,1,0:T(8,128)(2,1)S(1)} %get-tuple-element.97), channel_id=1, source_target_pairs={{0,8},{8,16},{16,24},{24,32},{32,40},{40,48},{48,56},{56,64},{64,7... | collective-permute-start | bytes 786440 | tf_op jit(solution)/shard_map/ppermute | solution.py:453
  95.4 6.0 %collective-permute-start.23 = (bf16[4,256,128]{2,1,0:T(8,128)(2,1)S(1)}, bf16[4,256,128]{2,1,0:T(8,128)(2,1)S(1)}, u32[]{:S(2)}, u32[]{:S(2)}) collective-permute-start(bf16[4,256,128]{2,1,0:T(8,128)(2,1)S(1)} %get-tuple-element.98), channel_id=1, source_target_pairs={{8,0},{16,8},{24,16},{32,24},{40,32},{48,40},{56,48},{64,56},{72,6... | collective-permute-start | bytes 786440 | tf_op jit(solution)/shard_map/ppermute | solution.py:452
  101.4 1.9 %collective-permute-start.25 = (bf16[4,256,128]{2,1,0:T(8,128)(2,1)S(1)}, bf16[4,256,128]{2,1,0:T(8,128)(2,1)S(1)}, u32[]{:S(2)}, u32[]{:S(2)}) collective-permute-start(bf16[4,256,128]{2,1,0:T(8,128)(2,1)S(1)} %get-tuple-element.100), channel_id=1, source_target_pairs={{0,136},{8,144},{16,152},{24,160},{32,168},{40,176},{48,184},{56,1... | collective-permute-start | bytes 786440 | tf_op jit(solution)/shard_map/ppermute | solution.py:460
  103.3 6.4 %collective-permute-done.18.refs_1_ = bf16[4,384,128]{2,1,0:T(8,128)(2,1)S(1)} collective-permute-done((bf16[4,384,128]{2,1,0:T(8,128)(2,1)S(1)}, bf16[4,384,128]{2,1,0:T(8,128)(2,1)S(1)}, u32[]{:S(2)}, u32[]{:S(2)}) %collective-permute-start.18) | collective-permute-done | bytes 393248 | tf_op jit(solution)/shard_map/ppermute | solution.py:405
  109.7 1.9 %collective-permute-start.26 = (bf16[4,256,128]{2,1,0:T(8,128)(2,1)S(1)}, bf16[4,256,128]{2,1,0:T(8,128)(2,1)S(1)}, u32[]{:S(2)}, u32[]{:S(2)}) collective-permute-start(bf16[4,256,128]{2,1,0:T(8,128)(2,1)S(1)} %get-tuple-element.101), channel_id=1, source_target_pairs={{8,128},{16,136},{24,144},{32,152},{40,160},{48,168},{56,176},{64,... | collective-permute-start | bytes 786440 | tf_op jit(solution)/shard_map/ppermute | solution.py:459
  111.6 3.3 %collective-permute-done.22.refs_1_ = bf16[4,256,128]{2,1,0:T(8,128)(2,1)S(1)} collective-permute-done((bf16[4,256,128]{2,1,0:T(8,128)(2,1)S(1)}, bf16[4,256,128]{2,1,0:T(8,128)(2,1)S(1)}, u32[]{:S(2)}, u32[]{:S(2)}) %collective-permute-start.22) | collective-permute-done | bytes 262176 | tf_op jit(solution)/shard_map/ppermute | solution.py:453
  114.9 3.1 %collective-permute-done.26.refs_5_ = bf16[4,256,128]{2,1,0:T(8,128)(2,1)S(1)} collective-permute-done((bf16[4,256,128]{2,1,0:T(8,128)(2,1)S(1)}, bf16[4,256,128]{2,1,0:T(8,128)(2,1)S(1)}, u32[]{:S(2)}, u32[]{:S(2)}) %collective-permute-start.26) | collective-permute-done | bytes 262176 | tf_op jit(solution)/shard_map/ppermute | solution.py:459
  118.0 1.8 %merge.1 = bf16[8,512,128]{2,1,0:T(8,128)(2,1)} custom-call(s32[3]{0:T(128)S(1)} %copy-done.4, bf16[8,256,128]{2,1,0:T(8,128)(2,1)S(1)} %get-tuple-element.96.refs_0_, bf16[4,256,128]{2,1,0:T(8,128)(2,1)S(1)} %collective-permute-done.22.refs_1_, bf16[4,256,128]{2,1,0:T(8,128)(2,1)S(1)} %collective-permute-done.23.refs_2_, ...), custom_call_target="tpu_custom_call" | custom-call | bytes 2097152 | tf_op jit(solution)/shard_map/merge/pallas_call | solution.py:220
  119.8 5.3 %all-to-all-start = ((bf16[8,512,128]{2,1,0:T(8,128)(2,1)}), bf16[8,512,128]{2,1,0:T(8,128)(2,1)S(1)}, u32[]{:S(2)}, u32[]{:S(2)}) async-start(bf16[8,512,128]{2,1,0:T(8,128)(2,1)} %merge.1), calls=%async_computation | async-start | bytes 2097152 | tf_op jit(solution)/shard_map/all_to_all | solution.py:416
  125.1 0.6 join.5
  125.7 2.1 %collective-permute-start.19 = (bf16[2,384,128]{2,1,0:T(8,128)(2,1)S(1)}, bf16[2,384,128]{2,1,0:T(8,128)(2,1)S(1)}, u32[]{:S(2)}, u32[]{:S(2)}) collective-permute-start(bf16[2,384,128]{2,1,0:T(8,128)(2,1)S(1)} %get-tuple-element.91), channel_id=1, source_target_pairs={{0,2},{1,3},{2,4},{3,5},{4,6},{5,7},{6,0},{7,1},{8,10},{9,11},{10,... | collective-permute-start | bytes 589832 | tf_op jit(solution)/shard_map/ppermute | solution.py:411
  127.8 2.7 %collective-permute-start.20 = (bf16[2,384,128]{2,1,0:T(8,128)(2,1)S(1)}, bf16[2,384,128]{2,1,0:T(8,128)(2,1)S(1)}, u32[]{:S(2)}, u32[]{:S(2)}) collective-permute-start(bf16[2,384,128]{2,1,0:T(8,128)(2,1)S(1)} %get-tuple-element.92), channel_id=1, source_target_pairs={{0,4},{1,5},{2,6},{3,7},{4,0},{5,1},{6,2},{7,3},{8,12},{9,13},{10,... | collective-permute-start | bytes 589832 | tf_op jit(solution)/shard_map/ppermute | solution.py:411
  130.5 1.5 collective-permute-start.21
  131.9 7.6 %collective-permute-done.19.refs_1_ = bf16[2,384,128]{2,1,0:T(8,128)(2,1)S(1)} collective-permute-done((bf16[2,384,128]{2,1,0:T(8,128)(2,1)S(1)}, bf16[2,384,128]{2,1,0:T(8,128)(2,1)S(1)}, u32[]{:S(2)}, u32[]{:S(2)}) %collective-permute-start.19) | collective-permute-done | bytes 196640 | tf_op jit(solution)/shard_map/ppermute | solution.py:411
  139.5 4.2 %collective-permute-done.20.refs_2_ = bf16[2,384,128]{2,1,0:T(8,128)(2,1)S(1)} collective-permute-done((bf16[2,384,128]{2,1,0:T(8,128)(2,1)S(1)}, bf16[2,384,128]{2,1,0:T(8,128)(2,1)S(1)}, u32[]{:S(2)}, u32[]{:S(2)}) %collective-permute-start.20) | collective-permute-done | bytes 196640 | tf_op jit(solution)/shard_map/ppermute | solution.py:411
  143.7 0.0 collective-permute-done.21.refs_3_
  143.7 1.6 unpack_parts.1
  145.3 11.3 %all-to-all-done.got = bf16[8,512,128]{2,1,0:T(8,128)(2,1)S(1)} async-done(((bf16[8,512,128]{2,1,0:T(8,128)(2,1)}), bf16[8,512,128]{2,1,0:T(8,128)(2,1)S(1)}, u32[]{:S(2)}, u32[]{:S(2)}) %all-to-all-start) | async-done | bytes 1048608 | tf_op jit(solution)/shard_map/all_to_all | solution.py:416
  156.6 1.8 %unpack.1 = (bf16[1,128,1024]{2,1,0:T(8,128)(2,1)}, bf16[1,128,1024]{2,1,0:T(8,128)(2,1)}, bf16[1,128,1024]{2,1,0:T(8,128)(2,1)}, bf16[1,128,1024]{2,1,0:T(8,128)(2,1)}) custom-call(s32[3]{0:T(128)S(1)} %copy-done.4, bf16[8,512,128]{2,1,0:T(8,128)(2,1)S(1)} %all-to-all-done.got), custom_call_target="tpu_custom_call" | custom-call | bytes 2097152 | tf_op jit(solution)/shard_map/unpack/pallas_call | solution.py:220
  (22 shorter events, 0.1 us)
Async XLA Ops:
  0.6 16.5 %collective-permute-start.10 = (bf16[1,128,1024]{2,1,0:T(8,128)(2,1)}, bf16[1,128,1024]{2,1,0:T(8,128)(2,1)S(1)}, u32[]{:S(2)}, u32[]{:S(2)}) collective-permute-start(bf16[1,128,1024]{2,1,0:T(8,128)(2,1)} %param.13), channel_id=1, source_target_pairs={{0,128},{128,0},{1,129},{129,1},{2,130},{130,2},{3,131},{131,3},{4... | collective-permute-start | bytes 786440 | tf_op jit(solution)/shard_map/ppermute | solution.py:434
  0.7 17.8 %collective-permute-start.11 = (bf16[1,128,1024]{2,1,0:T(8,128)(2,1)}, bf16[1,128,1024]{2,1,0:T(8,128)(2,1)S(1)}, u32[]{:S(2)}, u32[]{:S(2)}) collective-permute-start(bf16[1,128,1024]{2,1,0:T(8,128)(2,1)} %param.14), channel_id=1, source_target_pairs={{0,128},{128,0},{1,129},{129,1},{2,130},{130,2},{3,131},{131,3},{4... | collective-permute-start | bytes 786440 | tf_op jit(solution)/shard_map/ppermute | solution.py:435
  1.8 9.1 %copy-start.1 = (bf16[1,128,1024]{2,1,0:T(8,128)(2,1)S(1)}, bf16[1,128,1024]{2,1,0:T(8,128)(2,1)}, u32[]{:S(2)}) copy-start(bf16[1,128,1024]{2,1,0:T(8,128)(2,1)} %refs_0_.1) | copy-start | bytes 786436
  1.8 9.1 %copy-start.2 = (bf16[1,128,1024]{2,1,0:T(8,128)(2,1)S(1)}, bf16[1,128,1024]{2,1,0:T(8,128)(2,1)}, u32[]{:S(2)}) copy-start(bf16[1,128,1024]{2,1,0:T(8,128)(2,1)} %refs_1_.1) | copy-start | bytes 786436
  4.6 6.4 %copy-start.4 = (s32[3]{0:T(128)S(1)}, s32[3]{0:T(128)}, u32[]{:S(2)}) copy-start(s32[3]{0:T(128)} %pad_add_fusion.pos) | copy-start | bytes 40
  4.6 20.6 %collective-permute-start = (bf16[4,272,128]{2,1,0:T(8,128)(2,1)}, bf16[4,272,128]{2,1,0:T(8,128)(2,1)S(1)}, u32[]{:S(2)}, u32[]{:S(2)}) collective-permute-start(bf16[4,272,128]{2,1,0:T(8,128)(2,1)} %get-tuple-element.58), channel_id=1, source_target_pairs={{0,1},{1,0},{2,3},{3,2},{4,5},{5,4},{6,7},{7,6},{8,9},{9,8},{10,11... | collective-permute-start | bytes 835592 | tf_op jit(solution)/shard_map/ppermute | solution.py:405
  10.9 1.0 copy-start.3
  12.6 12.6 %copy-start = (bf16[4,272,128]{2,1,0:T(8,128)(2,1)S(1)}, bf16[4,272,128]{2,1,0:T(8,128)(2,1)}, u32[]{:S(2)}) copy-start(bf16[4,272,128]{2,1,0:T(8,128)(2,1)} %get-tuple-element.57.refs_0_) | copy-start | bytes 835588
  12.6 14.0 %collective-permute-start.6 = (bf16[2,384,128]{2,1,0:T(8,128)(2,1)S(1)}, bf16[2,384,128]{2,1,0:T(8,128)(2,1)S(1)}, u32[]{:S(2)}, u32[]{:S(2)}) collective-permute-start(bf16[2,384,128]{2,1,0:T(8,128)(2,1)S(1)} %get-tuple-element.66), channel_id=1, source_target_pairs={{0,2},{1,3},{2,4},{3,5},{4,6},{5,7},{6,0},{7,1},{8,10},{9,11},{10,... | collective-permute-start | bytes 589832 | tf_op jit(solution)/shard_map/ppermute | solution.py:411
  14.2 18.6 %collective-permute-start.7 = (bf16[2,384,128]{2,1,0:T(8,128)(2,1)S(1)}, bf16[2,384,128]{2,1,0:T(8,128)(2,1)S(1)}, u32[]{:S(2)}, u32[]{:S(2)}) collective-permute-start(bf16[2,384,128]{2,1,0:T(8,128)(2,1)S(1)} %get-tuple-element.67), channel_id=1, source_target_pairs={{0,4},{1,5},{2,6},{3,7},{4,0},{5,1},{6,2},{7,3},{8,12},{9,13},{10,... | collective-permute-start | bytes 589832 | tf_op jit(solution)/shard_map/ppermute | solution.py:411
  17.1 17.0 %collective-permute-start.8 = (bf16[2,384,128]{2,1,0:T(8,128)(2,1)S(1)}, bf16[2,384,128]{2,1,0:T(8,128)(2,1)S(1)}, u32[]{:S(2)}, u32[]{:S(2)}) collective-permute-start(bf16[2,384,128]{2,1,0:T(8,128)(2,1)S(1)} %get-tuple-element.68), channel_id=1, source_target_pairs={{0,6},{1,7},{2,0},{3,1},{4,2},{5,3},{6,4},{7,5},{8,14},{9,15},{10,... | collective-permute-start | bytes 589832 | tf_op jit(solution)/shard_map/ppermute | solution.py:411
  19.2 30.2 %collective-permute-start.12 = (bf16[4,256,128]{2,1,0:T(8,128)(2,1)S(1)}, bf16[4,256,128]{2,1,0:T(8,128)(2,1)S(1)}, u32[]{:S(2)}, u32[]{:S(2)}) collective-permute-start(bf16[4,256,128]{2,1,0:T(8,128)(2,1)S(1)} %get-tuple-element.72), channel_id=1, source_target_pairs={{0,1},{1,0},{2,3},{3,2},{4,5},{5,4},{6,7},{7,6},{8,9},{9,8},{10,11... | collective-permute-start | bytes 786440 | tf_op jit(solution)/shard_map/ppermute | solution.py:405
  25.8 15.0 %collective-permute-start.1 = (bf16[2,272,128]{2,1,0:T(8,128)(2,1)S(1)}, bf16[2,272,128]{2,1,0:T(8,128)(2,1)S(1)}, u32[]{:S(2)}, u32[]{:S(2)}) collective-permute-start(bf16[2,272,128]{2,1,0:T(8,128)(2,1)S(1)} %get-tuple-element.60), channel_id=1, source_target_pairs={{0,2},{1,3},{2,4},{3,5},{4,6},{5,7},{6,0},{7,1},{8,10},{9,11},{10,... | collective-permute-start | bytes 417800 | tf_op jit(solution)/shard_map/ppermute | solution.py:411
  26.6 14.2 %collective-permute-start.2 = (bf16[2,272,128]{2,1,0:T(8,128)(2,1)S(1)}, bf16[2,272,128]{2,1,0:T(8,128)(2,1)S(1)}, u32[]{:S(2)}, u32[]{:S(2)}) collective-permute-start(bf16[2,272,128]{2,1,0:T(8,128)(2,1)S(1)} %get-tuple-element.61), channel_id=1, source_target_pairs={{0,4},{1,5},{2,6},{3,7},{4,0},{5,1},{6,2},{7,3},{8,12},{9,13},{10,... | collective-permute-start | bytes 417800 | tf_op jit(solution)/shard_map/ppermute | solution.py:411
  32.8 8.0 %collective-permute-start.3 = (bf16[2,272,128]{2,1,0:T(8,128)(2,1)S(1)}, bf16[2,272,128]{2,1,0:T(8,128)(2,1)S(1)}, u32[]{:S(2)}, u32[]{:S(2)}) collective-permute-start(bf16[2,272,128]{2,1,0:T(8,128)(2,1)S(1)} %get-tuple-element.62), channel_id=1, source_target_pairs={{0,6},{1,7},{2,0},{3,1},{4,2},{5,3},{6,4},{7,5},{8,14},{9,15},{10,... | collective-permute-start | bytes 417800 | tf_op jit(solution)/shard_map/ppermute | solution.py:411
  34.7 28.5 %collective-permute-start.9 = (bf16[4,384,128]{2,1,0:T(8,128)(2,1)S(1)}, bf16[4,384,128]{2,1,0:T(8,128)(2,1)S(1)}, u32[]{:S(2)}, u32[]{:S(2)}) collective-permute-start(bf16[4,384,128]{2,1,0:T(8,128)(2,1)S(1)} %get-tuple-element.70), channel_id=1, source_target_pairs={{0,1},{1,0},{2,3},{3,2},{4,5},{5,4},{6,7},{7,6},{8,9},{9,8},{10,11... | collective-permute-start | bytes 1179656 | tf_op jit(solution)/shard_map/ppermute | solution.py:405
  41.5 30.6 %collective-permute-start.4 = (bf16[4,272,128]{2,1,0:T(8,128)(2,1)S(1)}, bf16[4,272,128]{2,1,0:T(8,128)(2,1)S(1)}, u32[]{:S(2)}, u32[]{:S(2)}) collective-permute-start(bf16[4,272,128]{2,1,0:T(8,128)(2,1)S(1)} %get-tuple-element.63.high.vh), channel_id=1, source_target_pairs={{0,8},{8,16},{16,24},{24,32},{32,40},{40,48},{48,56},{56,64},{64,7... | collective-permute-start | bytes 835592 | tf_op jit(solution)/shard_map/ppermute | solution.py:443
  44.9 27.2 %collective-permute-start.5 = (bf16[4,272,128]{2,1,0:T(8,128)(2,1)S(1)}, bf16[4,272,128]{2,1,0:T(8,128)(2,1)S(1)}, u32[]{:S(2)}, u32[]{:S(2)}) collective-permute-start(bf16[4,272,128]{2,1,0:T(8,128)(2,1)S(1)} %get-tuple-element.64.low.vl), channel_id=1, source_target_pairs={{8,0},{16,8},{24,16},{32,24},{40,32},{48,40},{56,48},{64,56},{72,6... | collective-permute-start | bytes 835592 | tf_op jit(solution)/shard_map/ppermute | solution.py:444
  50.0 7.7 %collective-permute-start.13 = (bf16[2,256,128]{2,1,0:T(8,128)(2,1)S(1)}, bf16[2,256,128]{2,1,0:T(8,128)(2,1)S(1)}, u32[]{:S(2)}, u32[]{:S(2)}) collective-permute-start(bf16[2,256,128]{2,1,0:T(8,128)(2,1)S(1)} %get-tuple-element.74), channel_id=1, source_target_pairs={{0,2},{1,3},{2,4},{3,5},{4,6},{5,7},{6,0},{7,1},{8,10},{9,11},{10,... | collective-permute-start | bytes 393224 | tf_op jit(solution)/shard_map/ppermute | solution.py:411
  50.7 8.9 %collective-permute-start.14 = (bf16[2,256,128]{2,1,0:T(8,128)(2,1)S(1)}, bf16[2,256,128]{2,1,0:T(8,128)(2,1)S(1)}, u32[]{:S(2)}, u32[]{:S(2)}) collective-permute-start(bf16[2,256,128]{2,1,0:T(8,128)(2,1)S(1)} %get-tuple-element.75), channel_id=1, source_target_pairs={{0,4},{1,5},{2,6},{3,7},{4,0},{5,1},{6,2},{7,3},{8,12},{9,13},{10,... | collective-permute-start | bytes 393224 | tf_op jit(solution)/shard_map/ppermute | solution.py:411
  57.7 5.0 %collective-permute-start.15 = (bf16[2,256,128]{2,1,0:T(8,128)(2,1)S(1)}, bf16[2,256,128]{2,1,0:T(8,128)(2,1)S(1)}, u32[]{:S(2)}, u32[]{:S(2)}) collective-permute-start(bf16[2,256,128]{2,1,0:T(8,128)(2,1)S(1)} %get-tuple-element.76), channel_id=1, source_target_pairs={{0,6},{1,7},{2,0},{3,1},{4,2},{5,3},{6,4},{7,5},{8,14},{9,15},{10,... | collective-permute-start | bytes 393224 | tf_op jit(solution)/shard_map/ppermute | solution.py:411
  57.7 0.7 copy-start.5
  63.3 18.6 %collective-permute-start.16 = (bf16[4,256,128]{2,1,0:T(8,128)(2,1)S(1)}, bf16[4,256,128]{2,1,0:T(8,128)(2,1)S(1)}, u32[]{:S(2)}, u32[]{:S(2)}) collective-permute-start(bf16[4,256,128]{2,1,0:T(8,128)(2,1)S(1)} %get-tuple-element.81.high), channel_id=1, source_target_pairs={{0,8},{8,16},{16,24},{24,32},{32,40},{40,48},{48,56},{56,64},{64,7... | collective-permute-start | bytes 786440 | tf_op jit(solution)/shard_map/ppermute | solution.py:447
  65.2 16.7 %collective-permute-start.17 = (bf16[4,256,128]{2,1,0:T(8,128)(2,1)S(1)}, bf16[4,256,128]{2,1,0:T(8,128)(2,1)S(1)}, u32[]{:S(2)}, u32[]{:S(2)}) collective-permute-start(bf16[4,256,128]{2,1,0:T(8,128)(2,1)S(1)} %get-tuple-element.82.low), channel_id=1, source_target_pairs={{8,0},{16,8},{24,16},{32,24},{40,32},{48,40},{56,48},{64,56},{72,6... | collective-permute-start | bytes 786440 | tf_op jit(solution)/shard_map/ppermute | solution.py:448
  91.8 17.9 %collective-permute-start.18 = (bf16[4,384,128]{2,1,0:T(8,128)(2,1)S(1)}, bf16[4,384,128]{2,1,0:T(8,128)(2,1)S(1)}, u32[]{:S(2)}, u32[]{:S(2)}) collective-permute-start(bf16[4,384,128]{2,1,0:T(8,128)(2,1)S(1)} %get-tuple-element.87), channel_id=1, source_target_pairs={{0,1},{1,0},{2,3},{3,2},{4,5},{5,4},{6,7},{7,6},{8,9},{9,8},{10,11... | collective-permute-start | bytes 1179656 | tf_op jit(solution)/shard_map/ppermute | solution.py:405
  93.4 24.6 %collective-permute-start.24 = (bf16[8,256,128]{2,1,0:T(8,128)(2,1)S(1)}, bf16[8,256,128]{2,1,0:T(8,128)(2,1)S(1)}, u32[]{:S(2)}, u32[]{:S(2)}) collective-permute-start(bf16[8,256,128]{2,1,0:T(8,128)(2,1)S(1)} %get-tuple-element.99), channel_id=1, source_target_pairs={{0,128},{128,0},{1,129},{129,1},{2,130},{130,2},{3,131},{131,3},{4... | collective-permute-start | bytes 1572872 | tf_op jit(solution)/shard_map/ppermute | solution.py:461
  93.5 21.5 %collective-permute-start.22 = (bf16[4,256,128]{2,1,0:T(8,128)(2,1)S(1)}, bf16[4,256,128]{2,1,0:T(8,128)(2,1)S(1)}, u32[]{:S(2)}, u32[]{:S(2)}) collective-permute-start(bf16[4,256,128]{2,1,0:T(8,128)(2,1)S(1)} %get-tuple-element.97), channel_id=1, source_target_pairs={{0,8},{8,16},{16,24},{24,32},{32,40},{40,48},{48,56},{56,64},{64,7... | collective-permute-start | bytes 786440 | tf_op jit(solution)/shard_map/ppermute | solution.py:453
  95.4 19.6 %collective-permute-start.23 = (bf16[4,256,128]{2,1,0:T(8,128)(2,1)S(1)}, bf16[4,256,128]{2,1,0:T(8,128)(2,1)S(1)}, u32[]{:S(2)}, u32[]{:S(2)}) collective-permute-start(bf16[4,256,128]{2,1,0:T(8,128)(2,1)S(1)} %get-tuple-element.98), channel_id=1, source_target_pairs={{8,0},{16,8},{24,16},{32,24},{40,32},{48,40},{56,48},{64,56},{72,6... | collective-permute-start | bytes 786440 | tf_op jit(solution)/shard_map/ppermute | solution.py:452
  101.4 13.5 %collective-permute-start.25 = (bf16[4,256,128]{2,1,0:T(8,128)(2,1)S(1)}, bf16[4,256,128]{2,1,0:T(8,128)(2,1)S(1)}, u32[]{:S(2)}, u32[]{:S(2)}) collective-permute-start(bf16[4,256,128]{2,1,0:T(8,128)(2,1)S(1)} %get-tuple-element.100), channel_id=1, source_target_pairs={{0,136},{8,144},{16,152},{24,160},{32,168},{40,176},{48,184},{56,1... | collective-permute-start | bytes 786440 | tf_op jit(solution)/shard_map/ppermute | solution.py:460
  109.7 8.3 %collective-permute-start.26 = (bf16[4,256,128]{2,1,0:T(8,128)(2,1)S(1)}, bf16[4,256,128]{2,1,0:T(8,128)(2,1)S(1)}, u32[]{:S(2)}, u32[]{:S(2)}) collective-permute-start(bf16[4,256,128]{2,1,0:T(8,128)(2,1)S(1)} %get-tuple-element.101), channel_id=1, source_target_pairs={{8,128},{16,136},{24,144},{32,152},{40,160},{48,168},{56,176},{64,... | collective-permute-start | bytes 786440 | tf_op jit(solution)/shard_map/ppermute | solution.py:459
  119.8 36.8 %all-to-all-start = ((bf16[8,512,128]{2,1,0:T(8,128)(2,1)}), bf16[8,512,128]{2,1,0:T(8,128)(2,1)S(1)}, u32[]{:S(2)}, u32[]{:S(2)}) async-start(bf16[8,512,128]{2,1,0:T(8,128)(2,1)} %merge.1), calls=%async_computation | async-start | bytes 2097152 | tf_op jit(solution)/shard_map/all_to_all | solution.py:416
  125.7 13.8 %collective-permute-start.19 = (bf16[2,384,128]{2,1,0:T(8,128)(2,1)S(1)}, bf16[2,384,128]{2,1,0:T(8,128)(2,1)S(1)}, u32[]{:S(2)}, u32[]{:S(2)}) collective-permute-start(bf16[2,384,128]{2,1,0:T(8,128)(2,1)S(1)} %get-tuple-element.91), channel_id=1, source_target_pairs={{0,2},{1,3},{2,4},{3,5},{4,6},{5,7},{6,0},{7,1},{8,10},{9,11},{10,... | collective-permute-start | bytes 589832 | tf_op jit(solution)/shard_map/ppermute | solution.py:411
  127.8 15.9 %collective-permute-start.20 = (bf16[2,384,128]{2,1,0:T(8,128)(2,1)S(1)}, bf16[2,384,128]{2,1,0:T(8,128)(2,1)S(1)}, u32[]{:S(2)}, u32[]{:S(2)}) collective-permute-start(bf16[2,384,128]{2,1,0:T(8,128)(2,1)S(1)} %get-tuple-element.92), channel_id=1, source_target_pairs={{0,4},{1,5},{2,6},{3,7},{4,0},{5,1},{6,2},{7,3},{8,12},{9,13},{10,... | collective-permute-start | bytes 589832 | tf_op jit(solution)/shard_map/ppermute | solution.py:411
  130.5 13.2 %collective-permute-start.21 = (bf16[2,384,128]{2,1,0:T(8,128)(2,1)S(1)}, bf16[2,384,128]{2,1,0:T(8,128)(2,1)S(1)}, u32[]{:S(2)}, u32[]{:S(2)}) collective-permute-start(bf16[2,384,128]{2,1,0:T(8,128)(2,1)S(1)} %get-tuple-element.93), channel_id=1, source_target_pairs={{0,6},{1,7},{2,0},{3,1},{4,2},{5,3},{6,4},{7,5},{8,14},{9,15},{10,... | collective-permute-start | bytes 589832 | tf_op jit(solution)/shard_map/ppermute | solution.py:411

commit v5 on v4

--- a/solution.py
+++ b/solution.py
@@ -117,12 +117,13 @@
     return lambda c: refs[c // 4][c % 4, first : first + CHUNK, :]
 
 
-def emit_sums(dk, dv, back, to_lo, to_hi):
+def emit_sums(dk, dv, back, to_lo, to_hi, first):
     for n, acc in enumerate((dk, dv)):
         rows = slice(n * CHUNK, (n + 1) * CHUNK)
-        to_lo[:, rows, :] = acc[0:HALF, :].astype(BF16).reshape(4, CHUNK, CHUNK)
+        share = slice(first + n * CHUNK, first + (n + 1) * CHUNK)
+        to_lo[:, share, :] = acc[0:HALF, :].astype(BF16).reshape(4, CHUNK, CHUNK)
         back[:, rows, :] = acc[HALF : HALF + BLOCK, :].astype(BF16).reshape(8, CHUNK, CHUNK)
-        to_hi[:, rows, :] = acc[HALF + BLOCK : EXT, :].astype(BF16).reshape(4, CHUNK, CHUNK)
+        to_hi[:, share, :] = acc[HALF + BLOCK : EXT, :].astype(BF16).reshape(4, CHUNK, CHUNK)
 
 
 def self_kernel(before, low, high, after, asks, out_t, gt, pay, back, to_lo, to_hi, kx, kt, v, vt, s, e, ds, dk, dv):
@@ -145,10 +146,12 @@
         return carry
 
     lax.fori_loop(0, BLOCK // QROWS, step, 0, unroll=4)
-    emit_sums(dk, dv, back, to_lo, to_hi)
-
-
-def cross_kernel(band, vb, vl, vh, va, before, low, high, after, asks, out_t, gt, pay, back, to_lo, to_hi, kx, kt, v, vt, s, e, ds, dk, dv):
+    emit_sums(dk, dv, back, to_lo, to_hi, 0)
+
+
+def cross_kernel(band, vb, vl, vh, va, before, low, high, after, asks, out_t, gt, self_lo, self_hi, pay, back, to_lo, to_hi, kx, kt, v, vt, s, e, ds, dk, dv):
+    to_lo[:, 0 : 2 * CHUNK, :] = self_lo[...]
+    to_hi[:, 0 : 2 * CHUNK, :] = self_hi[...]
     first = band[0]
     place = lax.broadcasted_iota(jnp.int32, (16, CHUNK), 0) * CHUNK + lax.broadcasted_iota(jnp.int32, (16, CHUNK), 1)
     inside = (place >= first) & (place < first + BLOCK)
@@ -169,7 +172,7 @@
         return carry
 
     lax.fori_loop(0, BLOCK // QROWS, step, 0, unroll=4)
-    emit_sums(dk, dv, back, to_lo, to_hi)
+    emit_sums(dk, dv, back, to_lo, to_hi, 2 * CHUNK)
 
 
 def scratch(width):
@@ -190,9 +193,9 @@
     return jax.ShapeDtypeStruct(shape, dtype)
 
 
-def run_attention(kernel, name, width, operands, outs):
+def run_attention(kernel, name, width, operands, outs, share):
     vmem = pl.BlockSpec(memory_space=pltpu.VMEM)
-    outs = outs + (shaped((8, 2 * CHUNK, CHUNK)), shaped((4, 2 * CHUNK, CHUNK)), shaped((4, 2 * CHUNK, CHUNK)))
+    outs = outs + (shaped((8, 2 * CHUNK, CHUNK)), shaped((4, share, CHUNK)), shaped((4, share, CHUNK)))
     return pl.pallas_call(
         kernel,
         out_shape=outs,
@@ -207,12 +210,12 @@
 
 def run_self(*operands):
     outs = (shaped((CHUNK, BLOCK), F32), shaped((CHUNK, BLOCK)), shaped((8, CHUNK, CHUNK)))
-    return run_attention(self_kernel, "self_attention", SELF_WIN, operands, outs)
+    return run_attention(self_kernel, "self_attention", SELF_WIN, operands, outs, 2 * CHUNK)
 
 
 def run_cross(*operands):
     outs = (shaped((8, 2 * CHUNK, CHUNK)),)
-    return run_attention(cross_kernel, "cross_attention", CROSS_WIN, operands, outs)
+    return run_attention(cross_kernel, "cross_attention", CROSS_WIN, operands, outs, 4 * CHUNK)
 
 
 def small_call(kernel, name, pos, operands, outs):
@@ -361,7 +364,7 @@
         rows = slice(2 * n * CHUNK, 2 * (n + 1) * CHUNK)
         center, below, above = refs[3 * n : 3 * n + 3]
         for first, halo in ((0, below), (4, above)):
-            total = center[first : first + 4].astype(F32) + halo[...].astype(F32)
+            total = center[first : first + 4].astype(F32) + halo[:, 0 : 2 * CHUNK, :].astype(F32)
             out[first : first + 4, rows, :] = total.astype(BF16)
 
 
@@ -449,15 +452,15 @@
     asks = whole(pos, keep_b, got_b)
 
     out_t, turned, pay_q, center, to_lo, to_hi = run_self(before, low, high, after, asks)
-    above = lax.ppermute(to_lo, "blk", down)
-    below = lax.ppermute(to_hi, "blk", up)
     pay_x, back, c_lo, c_hi = run_cross(
-        band, before, low, high, after, c_before, c_low, c_high, c_after, asks, out_t, turned
+        band, before, low, high, after, c_before, c_low, c_high, c_after, asks, out_t, turned, to_lo, to_hi
     )
     keep_p, send_p = order(pos, pay_q, pay_x)
     got_p = across_z(send_p)
-    c_above = lax.ppermute(c_lo, both, over_down)
-    c_below = lax.ppermute(c_hi, both, over_up)
+    above = lax.ppermute(c_lo, "blk", down)
+    below = lax.ppermute(c_hi, "blk", up)
+    c_above = lax.ppermute(above[:, 2 * CHUNK :], "tower", swap)
+    c_below = lax.ppermute(below[:, 2 * CHUNK :], "tower", swap)
     c_mid = lax.ppermute(back, "tower", swap)
     got_p, center = hold((got_p, center))
     got_s = exchange(merge(pos, center, below, above, c_mid, c_below, c_above))

time: 159 us -> 157 us (0.987)
  starting transfers between devices: 70.4 us -> 67.8 us
    all_to_all x1, waiting for transfers between devices: 11.3 us -> 0.02 us  [exchange(): lax.all_to_all(packed, 'seq', split_axis=0, concat_axis=0, tiled=True)]
    ppermute x4, waiting for transfers between devices: 6.41 us -> 16.8 us  [the longest x1 13 us: shards(): below = lax.ppermute(c_hi, 'blk', up)]
    ppermute x4, starting transfers between devices: 11.8 us -> 8.14 us  [the longest x1 6.03 us: shards(): above = lax.ppermute(c_lo, 'blk', down)]
  transfers between devices with their start and end apart: 28 -> 28, of which waited for: 9 -> 9; matrix products, arithmetic and copies ran while one was open for 1% -> 1% of each run, Pallas kernels for 12% -> 13%
where the time goes in v5:
time: 157 us; the launch traced here: 156 us
  starting transfers between devices  67.8 us (43%)
  waiting for transfers between devices  50.3 us (32%)
  Pallas kernels  33.1 us (21%)
  local copies, waits for them, and re-layouts  2.26 us (1%)
  between operations  1.58 us (1%)
    ppermute x12, starting transfers between devices, along_y(): lax.ppermute(parts[d], 'seq', [(i, (i + 2 * d) % size) for i in range(siz...  22 us
    ppermute x12, waiting for transfers between devices, along_y(): lax.ppermute(parts[d], 'seq', [(i, (i + 2 * d) % size) for i in range(siz...  21.8 us
    pallas_call x2, Pallas kernels, run_attention(): pl.pallas_call(kernel, out_shape=outs, in_specs=[pl.BlockSpec(memory_spac...  19.1 us
    ppermute x4, starting transfers between devices, across_z(): return lax.ppermute(send, 'seq', [(i, i ^ 1) for i in range(size)])  14.7 us
    ppermute x1, waiting for transfers between devices, shards(): below = lax.ppermute(c_hi, 'blk', up)  13 us
    ppermute x4, waiting for transfers between devices, across_z(): return lax.ppermute(send, 'seq', [(i, i ^ 1) for i in range(size)])  11.6 us
    pallas_call x13, Pallas kernels, small_call(): pl.pallas_call(kernel, out_shape=outs, in_specs=[pl.BlockSpec(memory_spac...  11.3 us
    all_to_all x1, starting transfers between devices, exchange(): lax.all_to_all(packed, 'seq', split_axis=0, concat_axis=0, tiled=True)  6.23 us
  transfers between devices with their start and end apart: 28, of which 9 were waited for; matrix products, arithmetic and copies ran while one was open for 1% of the time, Pallas kernels for 13%

profile of v5, /device:TPU:32, one launch (start us, length us, event | category | flops | bytes accessed | tf_op | source)
XLA Modules:
  0.0 155.7 jit_solution(17044439293918867950)
XLA Ops:
  0.6 0.1 collective-permute-start.10
  0.7 0.5 collective-permute-start.11
  1.2 0.6 pad_add_fusion.pos
  1.8 2.7 %pack_marked.1 = (bf16[4,272,128]{2,1,0:T(8,128)(2,1)}, bf16[4,272,128]{2,1,0:T(8,128)(2,1)}) custom-call(s32[3]{0:T(128)} %pad_add_fusion.pos, s32[2,128]{1,0:T(2,128)} %key_valid.1, bf16[1,128,1024]{2,1,0:T(8,128)(2,1)} %keys.1, bf16[1,128,1024]{2,1,0:T(8,128)(2,1)} %values.1), custom_call_target="tpu_custom_call" | custom-call | bytes 2097152 | tf_op jit(solution)/shard_map/pack_marked/pallas_call | solution.py:269
  4.6 0.0 copy-start.4
  4.6 6.4 %collective-permute-start = (bf16[4,272,128]{2,1,0:T(8,128)(2,1)}, bf16[4,272,128]{2,1,0:T(8,128)(2,1)S(1)}, u32[]{:S(2)}, u32[]{:S(2)}) collective-permute-start(bf16[4,272,128]{2,1,0:T(8,128)(2,1)} %get-tuple-element.58), channel_id=1, source_target_pairs={{0,1},{1,0},{2,3},{3,2},{4,5},{5,4},{6,7},{7,6},{8,9},{9,8},{10,11... | collective-permute-start | bytes 835592 | tf_op jit(solution)/shard_map/ppermute | solution.py:408
  11.0 0.9 copy-done.3
  11.9 0.7 pack_y.1
  12.6 1.7 %collective-permute-start.6 = (bf16[2,384,128]{2,1,0:T(8,128)(2,1)S(1)}, bf16[2,384,128]{2,1,0:T(8,128)(2,1)S(1)}, u32[]{:S(2)}, u32[]{:S(2)}) collective-permute-start(bf16[2,384,128]{2,1,0:T(8,128)(2,1)S(1)} %get-tuple-element.66), channel_id=1, source_target_pairs={{0,2},{1,3},{2,4},{3,5},{4,6},{5,7},{6,0},{7,1},{8,10},{9,11},{10,... | collective-permute-start | bytes 589832 | tf_op jit(solution)/shard_map/ppermute | solution.py:414
  14.2 2.9 %collective-permute-start.7 = (bf16[2,384,128]{2,1,0:T(8,128)(2,1)S(1)}, bf16[2,384,128]{2,1,0:T(8,128)(2,1)S(1)}, u32[]{:S(2)}, u32[]{:S(2)}) collective-permute-start(bf16[2,384,128]{2,1,0:T(8,128)(2,1)S(1)} %get-tuple-element.67), channel_id=1, source_target_pairs={{0,4},{1,5},{2,6},{3,7},{4,0},{5,1},{6,2},{7,3},{8,12},{9,13},{10,... | collective-permute-start | bytes 589832 | tf_op jit(solution)/shard_map/ppermute | solution.py:414
  17.1 1.3 collective-permute-start.8
  18.5 0.0 collective-permute-done.11.refs_1_
  18.5 0.7 pack.1
  19.2 0.6 collective-permute-start.12
  19.8 5.4 %collective-permute-done.refs_1_ = bf16[4,272,128]{2,1,0:T(8,128)(2,1)S(1)} collective-permute-done((bf16[4,272,128]{2,1,0:T(8,128)(2,1)}, bf16[4,272,128]{2,1,0:T(8,128)(2,1)S(1)}, u32[]{:S(2)}, u32[]{:S(2)}) %collective-permute-start) | collective-permute-done | bytes 278560 | tf_op jit(solution)/shard_map/ppermute | solution.py:408
  25.2 0.6 join.3
  25.8 0.8 collective-permute-start.1
  26.6 0.0 collective-permute-done.6.refs_1_
  26.6 6.2 %collective-permute-start.2 = (bf16[2,272,128]{2,1,0:T(8,128)(2,1)S(1)}, bf16[2,272,128]{2,1,0:T(8,128)(2,1)S(1)}, u32[]{:S(2)}, u32[]{:S(2)}) collective-permute-start(bf16[2,272,128]{2,1,0:T(8,128)(2,1)S(1)} %get-tuple-element.61), channel_id=1, source_target_pairs={{0,4},{1,5},{2,6},{3,7},{4,0},{5,1},{6,2},{7,3},{8,12},{9,13},{10,... | collective-permute-start | bytes 417800 | tf_op jit(solution)/shard_map/ppermute | solution.py:414
  32.8 0.0 collective-permute-done.7.refs_2_
  32.8 1.3 collective-permute-start.3
  34.1 0.6 split.1
  34.7 6.0 %collective-permute-start.9 = (bf16[4,384,128]{2,1,0:T(8,128)(2,1)S(1)}, bf16[4,384,128]{2,1,0:T(8,128)(2,1)S(1)}, u32[]{:S(2)}, u32[]{:S(2)}) collective-permute-start(bf16[4,384,128]{2,1,0:T(8,128)(2,1)S(1)} %get-tuple-element.70), channel_id=1, source_target_pairs={{0,1},{1,0},{2,3},{3,2},{4,5},{5,4},{6,7},{7,6},{8,9},{9,8},{10,11... | collective-permute-start | bytes 1179656 | tf_op jit(solution)/shard_map/ppermute | solution.py:408
  40.8 0.0 collective-permute-done.1.refs_1_
  40.8 0.0 collective-permute-done.2.refs_2_
  40.8 0.0 collective-permute-done.3.refs_3_
  40.8 0.6 halves.2
  41.5 3.4 %collective-permute-start.4 = (bf16[4,272,128]{2,1,0:T(8,128)(2,1)S(1)}, bf16[4,272,128]{2,1,0:T(8,128)(2,1)S(1)}, u32[]{:S(2)}, u32[]{:S(2)}) collective-permute-start(bf16[4,272,128]{2,1,0:T(8,128)(2,1)S(1)} %get-tuple-element.63.high.vh), channel_id=1, source_target_pairs={{0,8},{8,16},{16,24},{24,32},{32,40},{40,48},{48,56},{56,64},{64,7... | collective-permute-start | bytes 835592 | tf_op jit(solution)/shard_map/ppermute | solution.py:446
  44.9 4.6 %collective-permute-start.5 = (bf16[4,272,128]{2,1,0:T(8,128)(2,1)S(1)}, bf16[4,272,128]{2,1,0:T(8,128)(2,1)S(1)}, u32[]{:S(2)}, u32[]{:S(2)}) collective-permute-start(bf16[4,272,128]{2,1,0:T(8,128)(2,1)S(1)} %get-tuple-element.64.low.vl), channel_id=1, source_target_pairs={{8,0},{16,8},{24,16},{32,24},{40,32},{48,40},{56,48},{64,56},{72,6... | collective-permute-start | bytes 835592 | tf_op jit(solution)/shard_map/ppermute | solution.py:447
  49.4 0.6 join.4
  50.0 0.7 collective-permute-start.13
  50.7 0.8 collective-permute-start.14
  51.6 6.1 %collective-permute-done.13.refs_1_ = bf16[2,256,128]{2,1,0:T(8,128)(2,1)S(1)} collective-permute-done((bf16[2,256,128]{2,1,0:T(8,128)(2,1)S(1)}, bf16[2,256,128]{2,1,0:T(8,128)(2,1)S(1)}, u32[]{:S(2)}, u32[]{:S(2)}) %collective-permute-start.13) | collective-permute-done | bytes 131104 | tf_op jit(solution)/shard_map/ppermute | solution.py:414
  57.7 0.7 copy-done.5
  58.4 0.6 dynamic_slice.3
  59.6 3.0 %collective-permute-done.15.refs_3_ = bf16[2,256,128]{2,1,0:T(8,128)(2,1)S(1)} collective-permute-done((bf16[2,256,128]{2,1,0:T(8,128)(2,1)S(1)}, bf16[2,256,128]{2,1,0:T(8,128)(2,1)S(1)}, u32[]{:S(2)}, u32[]{:S(2)}) %collective-permute-start.15) | collective-permute-done | bytes 131104 | tf_op jit(solution)/shard_map/ppermute | solution.py:414
  62.7 0.6 halves.3
  63.3 1.9 %collective-permute-start.16 = (bf16[4,256,128]{2,1,0:T(8,128)(2,1)S(1)}, bf16[4,256,128]{2,1,0:T(8,128)(2,1)S(1)}, u32[]{:S(2)}, u32[]{:S(2)}) collective-permute-start(bf16[4,256,128]{2,1,0:T(8,128)(2,1)S(1)} %get-tuple-element.81.high), channel_id=1, source_target_pairs={{0,8},{8,16},{16,24},{24,32},{32,40},{40,48},{48,56},{56,64},{64,7... | collective-permute-start | bytes 786440 | tf_op jit(solution)/shard_map/ppermute | solution.py:450
  65.2 6.2 %collective-permute-start.17 = (bf16[4,256,128]{2,1,0:T(8,128)(2,1)S(1)}, bf16[4,256,128]{2,1,0:T(8,128)(2,1)S(1)}, u32[]{:S(2)}, u32[]{:S(2)}) collective-permute-start(bf16[4,256,128]{2,1,0:T(8,128)(2,1)S(1)} %get-tuple-element.82.low), channel_id=1, source_target_pairs={{8,0},{16,8},{24,16},{32,24},{40,32},{48,40},{56,48},{64,56},{72,6... | collective-permute-start | bytes 786440 | tf_op jit(solution)/shard_map/ppermute | solution.py:451
  71.4 0.6 whole.1.asks
  72.1 9.8 %self_attention.1 = (f32[128,1024]{1,0:T(8,128)S(1)}, bf16[128,1024]{1,0:T(8,128)(2,1)S(1)}, bf16[8,128,128]{2,1,0:T(8,128)(2,1)S(1)}, bf16[8,256,128]{2,1,0:T(8...) custom-call(bf16[4,272,128]{2,1,0:T(8,128)(2,1)S(1)} %collective-permute-done.4.before.vb, ...), custom_call_target="tpu_custom_call" | custom-call | flops 8000000000 | bytes 3145728 | tf_op jit(solution)/shard_map/self_attention/pallas_call | solution.py:199
  81.9 9.2 %cross_attention.1 = (bf16[8,256,128]{2,1,0:T(8,128)(2,1)S(1)}, bf16[8,256,128]{2,1,0:T(8,128)(2,1)S(1)}, bf16[4,512,128]{2,1,0:T(8,128)(2,1)S(1)}, bf16[4,512,128]{2,1,0:T(8,128)(2,1)S(1)}) custom-call(s32[1]{0:T(128)} %bitcast.3.band, bf16[4,272,128]{2,1,0:T(8,128)(2,1)S(1)} %collective-permute-done.4.before.vb, ...), custom_call_target="tpu_custom_call" | custom-call | flops 8000000000 | bytes 3145728 | tf_op jit(solution)/shard_map/cross_attention/pallas_call | solution.py:199
  91.2 1.9 %collective-permute-start.22 = (bf16[4,512,128]{2,1,0:T(8,128)(2,1)S(1)}, bf16[4,512,128]{2,1,0:T(8,128)(2,1)S(1)}, u32[]{:S(2)}, u32[]{:S(2)}) collective-permute-start(bf16[4,512,128]{2,1,0:T(8,128)(2,1)S(1)} %get-tuple-element.99), channel_id=1, source_target_pairs={{0,8},{8,16},{16,24},{24,32},{32,40},{40,48},{48,56},{56,64},{64,7... | collective-permute-start | bytes 1572872 | tf_op jit(solution)/shard_map/ppermute | solution.py:461
  93.1 6.0 %collective-permute-start.23 = (bf16[4,512,128]{2,1,0:T(8,128)(2,1)S(1)}, bf16[4,512,128]{2,1,0:T(8,128)(2,1)S(1)}, u32[]{:S(2)}, u32[]{:S(2)}) collective-permute-start(bf16[4,512,128]{2,1,0:T(8,128)(2,1)S(1)} %get-tuple-element.100), channel_id=1, source_target_pairs={{8,0},{16,8},{24,16},{32,24},{40,32},{48,40},{56,48},{64,56},{72,6... | collective-permute-start | bytes 1572872 | tf_op jit(solution)/shard_map/ppermute | solution.py:460
  99.1 0.1 collective-permute-start.24
  99.2 0.6 order.1
  99.9 1.6 %collective-permute-start.18 = (bf16[4,384,128]{2,1,0:T(8,128)(2,1)S(1)}, bf16[4,384,128]{2,1,0:T(8,128)(2,1)S(1)}, u32[]{:S(2)}, u32[]{:S(2)}) collective-permute-start(bf16[4,384,128]{2,1,0:T(8,128)(2,1)S(1)} %get-tuple-element.89), channel_id=1, source_target_pairs={{0,1},{1,0},{2,3},{3,2},{4,5},{5,4},{6,7},{7,6},{8,9},{9,8},{10,11... | collective-permute-start | bytes 1179656 | tf_op jit(solution)/shard_map/ppermute | solution.py:408
  101.5 13.0 %collective-permute-done.22.refs_1_ = bf16[4,512,128]{2,1,0:T(8,128)(2,1)S(1)} collective-permute-done((bf16[4,512,128]{2,1,0:T(8,128)(2,1)S(1)}, bf16[4,512,128]{2,1,0:T(8,128)(2,1)S(1)}, u32[]{:S(2)}, u32[]{:S(2)}) %collective-permute-start.22) | collective-permute-done | bytes 524320 | tf_op jit(solution)/shard_map/ppermute | solution.py:461
  114.5 0.1 collective-permute-start.25
  114.6 3.8 %collective-permute-done.23.refs_2_ = bf16[4,512,128]{2,1,0:T(8,128)(2,1)S(1)} collective-permute-done((bf16[4,512,128]{2,1,0:T(8,128)(2,1)S(1)}, bf16[4,512,128]{2,1,0:T(8,128)(2,1)S(1)}, u32[]{:S(2)}, u32[]{:S(2)}) %collective-permute-start.23) | collective-permute-done | bytes 524320 | tf_op jit(solution)/shard_map/ppermute | solution.py:460
  118.4 0.1 collective-permute-start.26
  118.5 6.2 %collective-permute-done.18.refs_1_ = bf16[4,384,128]{2,1,0:T(8,128)(2,1)S(1)} collective-permute-done((bf16[4,384,128]{2,1,0:T(8,128)(2,1)S(1)}, bf16[4,384,128]{2,1,0:T(8,128)(2,1)S(1)}, u32[]{:S(2)}, u32[]{:S(2)}) %collective-permute-start.18) | collective-permute-done | bytes 393248 | tf_op jit(solution)/shard_map/ppermute | solution.py:408
  124.8 1.8 %merge.1 = bf16[8,512,128]{2,1,0:T(8,128)(2,1)} custom-call(s32[3]{0:T(128)S(1)} %copy-done.4, bf16[8,256,128]{2,1,0:T(8,128)(2,1)S(1)} %get-tuple-element.98.refs_0_, bf16[4,512,128]{2,1,0:T(8,128)(2,1)S(1)} %collective-permute-done.22.refs_1_, bf16[4,512,128]{2,1,0:T(8,128)(2,1)S(1)} %collective-permute-done.23.refs_2_, ...), custom_call_target="tpu_custom_call" | custom-call | bytes 2097152 | tf_op jit(solution)/shard_map/merge/pallas_call | solution.py:223
  126.6 6.2 %all-to-all-start = ((bf16[8,512,128]{2,1,0:T(8,128)(2,1)}), bf16[8,512,128]{2,1,0:T(8,128)(2,1)S(1)}, u32[]{:S(2)}, u32[]{:S(2)}) async-start(bf16[8,512,128]{2,1,0:T(8,128)(2,1)} %merge.1), calls=%async_computation | async-start | bytes 2097152 | tf_op jit(solution)/shard_map/all_to_all | solution.py:419
  132.8 0.6 join.5
  133.4 2.1 %collective-permute-start.19 = (bf16[2,384,128]{2,1,0:T(8,128)(2,1)S(1)}, bf16[2,384,128]{2,1,0:T(8,128)(2,1)S(1)}, u32[]{:S(2)}, u32[]{:S(2)}) collective-permute-start(bf16[2,384,128]{2,1,0:T(8,128)(2,1)S(1)} %get-tuple-element.93), channel_id=1, source_target_pairs={{0,2},{1,3},{2,4},{3,5},{4,6},{5,7},{6,0},{7,1},{8,10},{9,11},{10,... | collective-permute-start | bytes 589832 | tf_op jit(solution)/shard_map/ppermute | solution.py:414
  135.5 2.7 %collective-permute-start.20 = (bf16[2,384,128]{2,1,0:T(8,128)(2,1)S(1)}, bf16[2,384,128]{2,1,0:T(8,128)(2,1)S(1)}, u32[]{:S(2)}, u32[]{:S(2)}) collective-permute-start(bf16[2,384,128]{2,1,0:T(8,128)(2,1)S(1)} %get-tuple-element.94), channel_id=1, source_target_pairs={{0,4},{1,5},{2,6},{3,7},{4,0},{5,1},{6,2},{7,3},{8,12},{9,13},{10,... | collective-permute-start | bytes 589832 | tf_op jit(solution)/shard_map/ppermute | solution.py:414
  138.2 1.5 collective-permute-start.21
  139.6 8.9 %collective-permute-done.19.refs_1_ = bf16[2,384,128]{2,1,0:T(8,128)(2,1)S(1)} collective-permute-done((bf16[2,384,128]{2,1,0:T(8,128)(2,1)S(1)}, bf16[2,384,128]{2,1,0:T(8,128)(2,1)S(1)}, u32[]{:S(2)}, u32[]{:S(2)}) %collective-permute-start.19) | collective-permute-done | bytes 196640 | tf_op jit(solution)/shard_map/ppermute | solution.py:414
  148.6 3.0 %collective-permute-done.20.refs_2_ = bf16[2,384,128]{2,1,0:T(8,128)(2,1)S(1)} collective-permute-done((bf16[2,384,128]{2,1,0:T(8,128)(2,1)S(1)}, bf16[2,384,128]{2,1,0:T(8,128)(2,1)S(1)}, u32[]{:S(2)}, u32[]{:S(2)}) %collective-permute-start.20) | collective-permute-done | bytes 196640 | tf_op jit(solution)/shard_map/ppermute | solution.py:414
  151.6 0.7 collective-permute-done.21.refs_3_
  152.3 1.6 %unpack_parts.1 = (bf16[1,128,1024]{2,1,0:T(8,128)(2,1)}, bf16[1,128,1024]{2,1,0:T(8,128)(2,1)}, bf16[1,128,1024]{2,1,0:T(8,128)(2,1)}) custom-call(s32[3]{0:T(128)S(1)} %copy-done.4, bf16[2,384,128]{2,1,0:T(8,128)(2,1)S(1)} %get-tuple-element.92.refs_0_, bf16[2,384,128]{2,1,0:T(8,128)(2,1)S(1)} %collective-permute-done.19.refs_1_, ...), custom_call_target="tpu_custom_call" | custom-call | bytes 2097152 | tf_op jit(solution)/shard_map/unpack_parts/pallas_call | solution.py:223
  153.9 0.0 all-to-all-done.got
  153.9 1.8 %unpack.1 = (bf16[1,128,1024]{2,1,0:T(8,128)(2,1)}, bf16[1,128,1024]{2,1,0:T(8,128)(2,1)}, bf16[1,128,1024]{2,1,0:T(8,128)(2,1)}, bf16[1,128,1024]{2,1,0:T(8,128)(2,1)}) custom-call(s32[3]{0:T(128)S(1)} %copy-done.4, bf16[8,512,128]{2,1,0:T(8,128)(2,1)S(1)} %all-to-all-done.got), custom_call_target="tpu_custom_call" | custom-call | bytes 2097152 | tf_op jit(solution)/shard_map/unpack/pallas_call | solution.py:223
  (24 shorter events, 0.1 us)
Async XLA Ops:
  0.6 16.5 %collective-permute-start.10 = (bf16[1,128,1024]{2,1,0:T(8,128)(2,1)}, bf16[1,128,1024]{2,1,0:T(8,128)(2,1)S(1)}, u32[]{:S(2)}, u32[]{:S(2)}) collective-permute-start(bf16[1,128,1024]{2,1,0:T(8,128)(2,1)} %param.13), channel_id=1, source_target_pairs={{0,128},{128,0},{1,129},{129,1},{2,130},{130,2},{3,131},{131,3},{4... | collective-permute-start | bytes 786440 | tf_op jit(solution)/shard_map/ppermute | solution.py:437
  0.7 17.8 %collective-permute-start.11 = (bf16[1,128,1024]{2,1,0:T(8,128)(2,1)}, bf16[1,128,1024]{2,1,0:T(8,128)(2,1)S(1)}, u32[]{:S(2)}, u32[]{:S(2)}) collective-permute-start(bf16[1,128,1024]{2,1,0:T(8,128)(2,1)} %param.14), channel_id=1, source_target_pairs={{0,128},{128,0},{1,129},{129,1},{2,130},{130,2},{3,131},{131,3},{4... | collective-permute-start | bytes 786440 | tf_op jit(solution)/shard_map/ppermute | solution.py:438
  1.8 9.1 %copy-start.1 = (bf16[1,128,1024]{2,1,0:T(8,128)(2,1)S(1)}, bf16[1,128,1024]{2,1,0:T(8,128)(2,1)}, u32[]{:S(2)}) copy-start(bf16[1,128,1024]{2,1,0:T(8,128)(2,1)} %refs_0_.1) | copy-start | bytes 786436
  1.8 9.1 %copy-start.2 = (bf16[1,128,1024]{2,1,0:T(8,128)(2,1)S(1)}, bf16[1,128,1024]{2,1,0:T(8,128)(2,1)}, u32[]{:S(2)}) copy-start(bf16[1,128,1024]{2,1,0:T(8,128)(2,1)} %refs_1_.1) | copy-start | bytes 786436
  4.6 6.4 %copy-start.4 = (s32[3]{0:T(128)S(1)}, s32[3]{0:T(128)}, u32[]{:S(2)}) copy-start(s32[3]{0:T(128)} %pad_add_fusion.pos) | copy-start | bytes 40
  4.6 20.6 %collective-permute-start = (bf16[4,272,128]{2,1,0:T(8,128)(2,1)}, bf16[4,272,128]{2,1,0:T(8,128)(2,1)S(1)}, u32[]{:S(2)}, u32[]{:S(2)}) collective-permute-start(bf16[4,272,128]{2,1,0:T(8,128)(2,1)} %get-tuple-element.58), channel_id=1, source_target_pairs={{0,1},{1,0},{2,3},{3,2},{4,5},{5,4},{6,7},{7,6},{8,9},{9,8},{10,11... | collective-permute-start | bytes 835592 | tf_op jit(solution)/shard_map/ppermute | solution.py:408
  10.9 1.0 copy-start.3
  12.6 12.6 %copy-start = (bf16[4,272,128]{2,1,0:T(8,128)(2,1)S(1)}, bf16[4,272,128]{2,1,0:T(8,128)(2,1)}, u32[]{:S(2)}) copy-start(bf16[4,272,128]{2,1,0:T(8,128)(2,1)} %get-tuple-element.57.refs_0_) | copy-start | bytes 835588
  12.6 14.0 %collective-permute-start.6 = (bf16[2,384,128]{2,1,0:T(8,128)(2,1)S(1)}, bf16[2,384,128]{2,1,0:T(8,128)(2,1)S(1)}, u32[]{:S(2)}, u32[]{:S(2)}) collective-permute-start(bf16[2,384,128]{2,1,0:T(8,128)(2,1)S(1)} %get-tuple-element.66), channel_id=1, source_target_pairs={{0,2},{1,3},{2,4},{3,5},{4,6},{5,7},{6,0},{7,1},{8,10},{9,11},{10,... | collective-permute-start | bytes 589832 | tf_op jit(solution)/shard_map/ppermute | solution.py:414
  14.2 18.6 %collective-permute-start.7 = (bf16[2,384,128]{2,1,0:T(8,128)(2,1)S(1)}, bf16[2,384,128]{2,1,0:T(8,128)(2,1)S(1)}, u32[]{:S(2)}, u32[]{:S(2)}) collective-permute-start(bf16[2,384,128]{2,1,0:T(8,128)(2,1)S(1)} %get-tuple-element.67), channel_id=1, source_target_pairs={{0,4},{1,5},{2,6},{3,7},{4,0},{5,1},{6,2},{7,3},{8,12},{9,13},{10,... | collective-permute-start | bytes 589832 | tf_op jit(solution)/shard_map/ppermute | solution.py:414
  17.1 17.0 %collective-permute-start.8 = (bf16[2,384,128]{2,1,0:T(8,128)(2,1)S(1)}, bf16[2,384,128]{2,1,0:T(8,128)(2,1)S(1)}, u32[]{:S(2)}, u32[]{:S(2)}) collective-permute-start(bf16[2,384,128]{2,1,0:T(8,128)(2,1)S(1)} %get-tuple-element.68), channel_id=1, source_target_pairs={{0,6},{1,7},{2,0},{3,1},{4,2},{5,3},{6,4},{7,5},{8,14},{9,15},{10,... | collective-permute-start | bytes 589832 | tf_op jit(solution)/shard_map/ppermute | solution.py:414
  19.2 30.2 %collective-permute-start.12 = (bf16[4,256,128]{2,1,0:T(8,128)(2,1)S(1)}, bf16[4,256,128]{2,1,0:T(8,128)(2,1)S(1)}, u32[]{:S(2)}, u32[]{:S(2)}) collective-permute-start(bf16[4,256,128]{2,1,0:T(8,128)(2,1)S(1)} %get-tuple-element.72), channel_id=1, source_target_pairs={{0,1},{1,0},{2,3},{3,2},{4,5},{5,4},{6,7},{7,6},{8,9},{9,8},{10,11... | collective-permute-start | bytes 786440 | tf_op jit(solution)/shard_map/ppermute | solution.py:408
  25.8 15.0 %collective-permute-start.1 = (bf16[2,272,128]{2,1,0:T(8,128)(2,1)S(1)}, bf16[2,272,128]{2,1,0:T(8,128)(2,1)S(1)}, u32[]{:S(2)}, u32[]{:S(2)}) collective-permute-start(bf16[2,272,128]{2,1,0:T(8,128)(2,1)S(1)} %get-tuple-element.60), channel_id=1, source_target_pairs={{0,2},{1,3},{2,4},{3,5},{4,6},{5,7},{6,0},{7,1},{8,10},{9,11},{10,... | collective-permute-start | bytes 417800 | tf_op jit(solution)/shard_map/ppermute | solution.py:414
  26.6 14.2 %collective-permute-start.2 = (bf16[2,272,128]{2,1,0:T(8,128)(2,1)S(1)}, bf16[2,272,128]{2,1,0:T(8,128)(2,1)S(1)}, u32[]{:S(2)}, u32[]{:S(2)}) collective-permute-start(bf16[2,272,128]{2,1,0:T(8,128)(2,1)S(1)} %get-tuple-element.61), channel_id=1, source_target_pairs={{0,4},{1,5},{2,6},{3,7},{4,0},{5,1},{6,2},{7,3},{8,12},{9,13},{10,... | collective-permute-start | bytes 417800 | tf_op jit(solution)/shard_map/ppermute | solution.py:414
  32.8 8.0 %collective-permute-start.3 = (bf16[2,272,128]{2,1,0:T(8,128)(2,1)S(1)}, bf16[2,272,128]{2,1,0:T(8,128)(2,1)S(1)}, u32[]{:S(2)}, u32[]{:S(2)}) collective-permute-start(bf16[2,272,128]{2,1,0:T(8,128)(2,1)S(1)} %get-tuple-element.62), channel_id=1, source_target_pairs={{0,6},{1,7},{2,0},{3,1},{4,2},{5,3},{6,4},{7,5},{8,14},{9,15},{10,... | collective-permute-start | bytes 417800 | tf_op jit(solution)/shard_map/ppermute | solution.py:414
  34.7 28.5 %collective-permute-start.9 = (bf16[4,384,128]{2,1,0:T(8,128)(2,1)S(1)}, bf16[4,384,128]{2,1,0:T(8,128)(2,1)S(1)}, u32[]{:S(2)}, u32[]{:S(2)}) collective-permute-start(bf16[4,384,128]{2,1,0:T(8,128)(2,1)S(1)} %get-tuple-element.70), channel_id=1, source_target_pairs={{0,1},{1,0},{2,3},{3,2},{4,5},{5,4},{6,7},{7,6},{8,9},{9,8},{10,11... | collective-permute-start | bytes 1179656 | tf_op jit(solution)/shard_map/ppermute | solution.py:408
  41.5 30.6 %collective-permute-start.4 = (bf16[4,272,128]{2,1,0:T(8,128)(2,1)S(1)}, bf16[4,272,128]{2,1,0:T(8,128)(2,1)S(1)}, u32[]{:S(2)}, u32[]{:S(2)}) collective-permute-start(bf16[4,272,128]{2,1,0:T(8,128)(2,1)S(1)} %get-tuple-element.63.high.vh), channel_id=1, source_target_pairs={{0,8},{8,16},{16,24},{24,32},{32,40},{40,48},{48,56},{56,64},{64,7... | collective-permute-start | bytes 835592 | tf_op jit(solution)/shard_map/ppermute | solution.py:446
  44.9 27.2 %collective-permute-start.5 = (bf16[4,272,128]{2,1,0:T(8,128)(2,1)S(1)}, bf16[4,272,128]{2,1,0:T(8,128)(2,1)S(1)}, u32[]{:S(2)}, u32[]{:S(2)}) collective-permute-start(bf16[4,272,128]{2,1,0:T(8,128)(2,1)S(1)} %get-tuple-element.64.low.vl), channel_id=1, source_target_pairs={{8,0},{16,8},{24,16},{32,24},{40,32},{48,40},{56,48},{64,56},{72,6... | collective-permute-start | bytes 835592 | tf_op jit(solution)/shard_map/ppermute | solution.py:447
  50.0 7.7 %collective-permute-start.13 = (bf16[2,256,128]{2,1,0:T(8,128)(2,1)S(1)}, bf16[2,256,128]{2,1,0:T(8,128)(2,1)S(1)}, u32[]{:S(2)}, u32[]{:S(2)}) collective-permute-start(bf16[2,256,128]{2,1,0:T(8,128)(2,1)S(1)} %get-tuple-element.74), channel_id=1, source_target_pairs={{0,2},{1,3},{2,4},{3,5},{4,6},{5,7},{6,0},{7,1},{8,10},{9,11},{10,... | collective-permute-start | bytes 393224 | tf_op jit(solution)/shard_map/ppermute | solution.py:414
  50.7 8.9 %collective-permute-start.14 = (bf16[2,256,128]{2,1,0:T(8,128)(2,1)S(1)}, bf16[2,256,128]{2,1,0:T(8,128)(2,1)S(1)}, u32[]{:S(2)}, u32[]{:S(2)}) collective-permute-start(bf16[2,256,128]{2,1,0:T(8,128)(2,1)S(1)} %get-tuple-element.75), channel_id=1, source_target_pairs={{0,4},{1,5},{2,6},{3,7},{4,0},{5,1},{6,2},{7,3},{8,12},{9,13},{10,... | collective-permute-start | bytes 393224 | tf_op jit(solution)/shard_map/ppermute | solution.py:414
  57.7 5.0 %collective-permute-start.15 = (bf16[2,256,128]{2,1,0:T(8,128)(2,1)S(1)}, bf16[2,256,128]{2,1,0:T(8,128)(2,1)S(1)}, u32[]{:S(2)}, u32[]{:S(2)}) collective-permute-start(bf16[2,256,128]{2,1,0:T(8,128)(2,1)S(1)} %get-tuple-element.76), channel_id=1, source_target_pairs={{0,6},{1,7},{2,0},{3,1},{4,2},{5,3},{6,4},{7,5},{8,14},{9,15},{10,... | collective-permute-start | bytes 393224 | tf_op jit(solution)/shard_map/ppermute | solution.py:414
  57.7 0.7 copy-start.5
  63.3 18.6 %collective-permute-start.16 = (bf16[4,256,128]{2,1,0:T(8,128)(2,1)S(1)}, bf16[4,256,128]{2,1,0:T(8,128)(2,1)S(1)}, u32[]{:S(2)}, u32[]{:S(2)}) collective-permute-start(bf16[4,256,128]{2,1,0:T(8,128)(2,1)S(1)} %get-tuple-element.81.high), channel_id=1, source_target_pairs={{0,8},{8,16},{16,24},{24,32},{32,40},{40,48},{48,56},{56,64},{64,7... | collective-permute-start | bytes 786440 | tf_op jit(solution)/shard_map/ppermute | solution.py:450
  65.2 16.7 %collective-permute-start.17 = (bf16[4,256,128]{2,1,0:T(8,128)(2,1)S(1)}, bf16[4,256,128]{2,1,0:T(8,128)(2,1)S(1)}, u32[]{:S(2)}, u32[]{:S(2)}) collective-permute-start(bf16[4,256,128]{2,1,0:T(8,128)(2,1)S(1)} %get-tuple-element.82.low), channel_id=1, source_target_pairs={{8,0},{16,8},{24,16},{32,24},{40,32},{48,40},{56,48},{64,56},{72,6... | collective-permute-start | bytes 786440 | tf_op jit(solution)/shard_map/ppermute | solution.py:451
  91.2 23.4 %collective-permute-start.22 = (bf16[4,512,128]{2,1,0:T(8,128)(2,1)S(1)}, bf16[4,512,128]{2,1,0:T(8,128)(2,1)S(1)}, u32[]{:S(2)}, u32[]{:S(2)}) collective-permute-start(bf16[4,512,128]{2,1,0:T(8,128)(2,1)S(1)} %get-tuple-element.99), channel_id=1, source_target_pairs={{0,8},{8,16},{16,24},{24,32},{32,40},{40,48},{48,56},{56,64},{64,7... | collective-permute-start | bytes 1572872 | tf_op jit(solution)/shard_map/ppermute | solution.py:461
  93.1 25.3 %collective-permute-start.23 = (bf16[4,512,128]{2,1,0:T(8,128)(2,1)S(1)}, bf16[4,512,128]{2,1,0:T(8,128)(2,1)S(1)}, u32[]{:S(2)}, u32[]{:S(2)}) collective-permute-start(bf16[4,512,128]{2,1,0:T(8,128)(2,1)S(1)} %get-tuple-element.100), channel_id=1, source_target_pairs={{8,0},{16,8},{24,16},{32,24},{40,32},{48,40},{56,48},{64,56},{72,6... | collective-permute-start | bytes 1572872 | tf_op jit(solution)/shard_map/ppermute | solution.py:460
  99.1 25.6 %collective-permute-start.24 = (bf16[8,256,128]{2,1,0:T(8,128)(2,1)S(1)}, bf16[8,256,128]{2,1,0:T(8,128)(2,1)S(1)}, u32[]{:S(2)}, u32[]{:S(2)}) collective-permute-start(bf16[8,256,128]{2,1,0:T(8,128)(2,1)S(1)} %get-tuple-element.101), channel_id=1, source_target_pairs={{0,128},{128,0},{1,129},{129,1},{2,130},{130,2},{3,131},{131,3},{4... | collective-permute-start | bytes 1572872 | tf_op jit(solution)/shard_map/ppermute | solution.py:464
  99.9 24.9 %collective-permute-start.18 = (bf16[4,384,128]{2,1,0:T(8,128)(2,1)S(1)}, bf16[4,384,128]{2,1,0:T(8,128)(2,1)S(1)}, u32[]{:S(2)}, u32[]{:S(2)}) collective-permute-start(bf16[4,384,128]{2,1,0:T(8,128)(2,1)S(1)} %get-tuple-element.89), channel_id=1, source_target_pairs={{0,1},{1,0},{2,3},{3,2},{4,5},{5,4},{6,7},{7,6},{8,9},{9,8},{10,11... | collective-permute-start | bytes 1179656 | tf_op jit(solution)/shard_map/ppermute | solution.py:408
  114.5 10.2 %collective-permute-start.25 = (bf16[4,256,128]{2,1,0:T(8,128)(2,1)S(1)}, bf16[4,256,128]{2,1,0:T(8,128)(2,1)S(1)}, u32[]{:S(2)}, u32[]{:S(2)}) collective-permute-start(bf16[4,256,128]{2,1,0:T(8,128)(2,1)S(1)} %slice.8), channel_id=1, source_target_pairs={{0,128},{128,0},{1,129},{129,1},{2,130},{130,2},{3,131},{131,3},{4... | collective-permute-start | bytes 786440 | tf_op jit(solution)/shard_map/ppermute | solution.py:463
  118.4 6.3 %collective-permute-start.26 = (bf16[4,256,128]{2,1,0:T(8,128)(2,1)S(1)}, bf16[4,256,128]{2,1,0:T(8,128)(2,1)S(1)}, u32[]{:S(2)}, u32[]{:S(2)}) collective-permute-start(bf16[4,256,128]{2,1,0:T(8,128)(2,1)S(1)} %slice.9), channel_id=1, source_target_pairs={{0,128},{128,0},{1,129},{129,1},{2,130},{130,2},{3,131},{131,3},{4... | collective-permute-start | bytes 786440 | tf_op jit(solution)/shard_map/ppermute | solution.py:462
  126.6 27.3 %all-to-all-start = ((bf16[8,512,128]{2,1,0:T(8,128)(2,1)}), bf16[8,512,128]{2,1,0:T(8,128)(2,1)S(1)}, u32[]{:S(2)}, u32[]{:S(2)}) async-start(bf16[8,512,128]{2,1,0:T(8,128)(2,1)} %merge.1), calls=%async_computation | async-start | bytes 2097152 | tf_op jit(solution)/shard_map/all_to_all | solution.py:419
  133.4 15.2 %collective-permute-start.19 = (bf16[2,384,128]{2,1,0:T(8,128)(2,1)S(1)}, bf16[2,384,128]{2,1,0:T(8,128)(2,1)S(1)}, u32[]{:S(2)}, u32[]{:S(2)}) collective-permute-start(bf16[2,384,128]{2,1,0:T(8,128)(2,1)S(1)} %get-tuple-element.93), channel_id=1, source_target_pairs={{0,2},{1,3},{2,4},{3,5},{4,6},{5,7},{6,0},{7,1},{8,10},{9,11},{10,... | collective-permute-start | bytes 589832 | tf_op jit(solution)/shard_map/ppermute | solution.py:414
  135.5 16.1 %collective-permute-start.20 = (bf16[2,384,128]{2,1,0:T(8,128)(2,1)S(1)}, bf16[2,384,128]{2,1,0:T(8,128)(2,1)S(1)}, u32[]{:S(2)}, u32[]{:S(2)}) collective-permute-start(bf16[2,384,128]{2,1,0:T(8,128)(2,1)S(1)} %get-tuple-element.94), channel_id=1, source_target_pairs={{0,4},{1,5},{2,6},{3,7},{4,0},{5,1},{6,2},{7,3},{8,12},{9,13},{10,... | collective-permute-start | bytes 589832 | tf_op jit(solution)/shard_map/ppermute | solution.py:414
  138.2 14.1 %collective-permute-start.21 = (bf16[2,384,128]{2,1,0:T(8,128)(2,1)S(1)}, bf16[2,384,128]{2,1,0:T(8,128)(2,1)S(1)}, u32[]{:S(2)}, u32[]{:S(2)}) collective-permute-start(bf16[2,384,128]{2,1,0:T(8,128)(2,1)S(1)} %get-tuple-element.95), channel_id=1, source_target_pairs={{0,6},{1,7},{2,0},{3,1},{4,2},{5,3},{6,4},{7,5},{8,14},{9,15},{10,... | collective-permute-start | bytes 589832 | tf_op jit(solution)/shard_map/ppermute | solution.py:414
